TPU v7x, 256 devices: a whole 4x4x8 slice. The times are simulated.
256 devices in a mesh: row: 64 (over y, z_lo, x), head: 4 (over z_hi, core).
Axes of the slice: x: 4, y: 4, z: 8 (z_hi: 2, z_lo: 4; z = z_hi * 4 + z_lo), core: 2. Of those that a mesh axis runs over, the one named last changes fastest.
Arguments:
- queries: bfloat16 [256, 1024, 4, 128], P('row', None, 'head'), may hold values from -40 to 40
- keys_proj: bfloat16 [256, 1024, 4, 128], P('row', None, 'head'), may hold values from -40 to 40
- values_proj: bfloat16 [256, 1024, 4, 128], P('row', None, 'head'), may hold values from -6 to 6
- grad_output: bfloat16 [256, 1024, 4, 128], P('row', None, 'head'), may hold values from -6 to 6
Outputs:
- attended: bfloat16 [256, 1024, 4, 128], P('row', 'head')
- grad_queries: bfloat16 [256, 1024, 4, 128], P('row', 'head')
- grad_keys: bfloat16 [256, 1024, 4, 128], P('row', 'head')
- grad_values: bfloat16 [256, 1024, 4, 128], P('row', 'head')
All inputs are finite; a program needn't handle non-finite values.
Results may differ from a plain program's by a relative error of at most 0.024.
Values may be sent and summed in bfloat16 or wider, within the bound.
No kernel may reach another device: no remote copies, remote signals or barrier semaphores. Data moves between devices by JAX's collectives and lax.ppermute only.
A program may use at most 64 MiB of HBM per device.

v0:
```python
import jax
import jax.numpy as jnp
from jax import lax
from jax.sharding import PartitionSpec as P


def attend(queries, keys_proj, values_proj, grad_output):
    count_rows = queries.shape[0]
    scale_factor = queries.shape[-1] ** (-0.5)
    scores = (
        jnp.einsum("rbd,sbd->brs", queries, keys_proj, preferred_element_type=jnp.float32)
        * scale_factor
    )
    causal = lax.broadcasted_iota(jnp.int32, (count_rows, count_rows), 1) <= lax.broadcasted_iota(
        jnp.int32, (count_rows, count_rows), 0
    )
    scores = jnp.where(causal[None], scores, -jnp.inf)
    largest = jnp.max(scores, axis=-1, keepdims=True)
    raw_weights = jnp.exp(scores - largest)
    weights = raw_weights / jnp.sum(raw_weights, axis=-1, keepdims=True)
    low_weights = weights.astype(jnp.bfloat16)
    attended = jnp.einsum(
        "brs,sbd->rbd", low_weights, values_proj, preferred_element_type=jnp.float32
    ).astype(jnp.bfloat16)
    row_dots = jnp.sum(grad_output.astype(jnp.float32) * attended.astype(jnp.float32), axis=-1)
    grad_weights = jnp.einsum(
        "rbd,sbd->brs", grad_output, values_proj, preferred_element_type=jnp.float32
    )
    grad_scores = (weights * (grad_weights - row_dots.T[:, :, None]) * scale_factor).astype(
        jnp.bfloat16
    )
    grad_values = jnp.einsum(
        "brs,rbd->sbd", low_weights, grad_output, preferred_element_type=jnp.float32
    ).astype(jnp.bfloat16)
    grad_queries = jnp.einsum(
        "brs,sbd->rbd", grad_scores, keys_proj, preferred_element_type=jnp.float32
    ).astype(jnp.bfloat16)
    grad_keys = jnp.einsum(
        "brs,rbd->sbd", grad_scores, queries, preferred_element_type=jnp.float32
    ).astype(jnp.bfloat16)
    return (attended, grad_queries, grad_keys, grad_values)


def attend_block(pieces):
    shape_full = pieces[0].shape
    flat = [piece.reshape(shape_full[0], -1, shape_full[-1]) for piece in pieces]
    results = attend(flat[0], flat[1], flat[2], flat[3])
    return tuple((result.reshape(shape_full) for result in results))


def shards(queries, keys_proj, values_proj, grad_output):
    row_devs = lax.axis_size("row")
    head_devs = lax.axis_size("head")
    local_rows, columns, local_heads, head_dim = queries.shape
    inner_cols = columns // (row_devs * head_devs)

    def split_columns(array):
        return array.reshape(local_rows, head_devs, row_devs, inner_cols, local_heads, head_dim)

    results = attend_block(
        (
            lax.all_to_all(split_columns(queries), "row", split_axis=2, concat_axis=0, tiled=True),
            lax.all_to_all(
                split_columns(keys_proj), "row", split_axis=2, concat_axis=0, tiled=True
            ),
            lax.all_to_all(
                split_columns(values_proj), "row", split_axis=2, concat_axis=0, tiled=True
            ),
            lax.all_to_all(
                split_columns(grad_output), "row", split_axis=2, concat_axis=0, tiled=True
            ),
        )
    )
    regrouped = (
        lax.all_to_all(
            lax.all_to_all(results[0], "row", split_axis=0, concat_axis=2, tiled=True),
            "head",
            split_axis=1,
            concat_axis=4,
            tiled=True,
        ),
        lax.all_to_all(
            lax.all_to_all(results[1], "row", split_axis=0, concat_axis=2, tiled=True),
            "head",
            split_axis=1,
            concat_axis=4,
            tiled=True,
        ),
        lax.all_to_all(
            lax.all_to_all(results[2], "row", split_axis=0, concat_axis=2, tiled=True),
            "head",
            split_axis=1,
            concat_axis=4,
            tiled=True,
        ),
        lax.all_to_all(
            lax.all_to_all(results[3], "row", split_axis=0, concat_axis=2, tiled=True),
            "head",
            split_axis=1,
            concat_axis=4,
            tiled=True,
        ),
    )
    out_shape = (local_rows, columns // head_devs, local_heads * head_devs, head_dim)
    return (
        regrouped[0].reshape(out_shape),
        regrouped[1].reshape(out_shape),
        regrouped[2].reshape(out_shape),
        regrouped[3].reshape(out_shape),
    )


def solution(mesh):
    in_specs = (
        P("row", None, "head", None),
        P("row", None, "head", None),
        P("row", None, "head", None),
        P("row", None, "head", None),
    )
    out_specs = (
        P("row", "head", None, None),
        P("row", "head", None, None),
        P("row", "head", None, None),
        P("row", "head", None, None),
    )
    return jax.shard_map(shards, mesh=mesh, in_specs=in_specs, out_specs=out_specs, check_vma=False)
```

profile of v0, /device:TPU:2, one launch (start us, length us, event | category | flops | bytes accessed | tf_op | source)
XLA Modules:
  0.0 417.2 jit_solution(3499508530593847424)
XLA Ops:
  0.6 3.6 copy.80
  4.3 12.1 %all-to-all-start = ((bf16[4,4,64,4,1,128]{5,0,3,1,4,2:T(4,128)(2,1)}), bf16[4,4,64,4,1,128]{5,0,3,1,4,2:T(4,128)(2,1)S(1)}, u32[]{:S(2)}, u32[]{:S(2)}) async-start(bf16[4,4,64,4,1,128]{5,0,3,1,4,2:T(4,128)(2,1)} %copy.80), calls=%async_computation | async-start | bytes 2097152 | tf_op jit(solution)/shard_map/all_to_all | solution.py:62
  18.7 26.0 %all-to-all-done = bf16[4,4,64,4,1,128]{5,0,3,1,4,2:T(4,128)(2,1)S(1)} async-done(((bf16[4,4,64,4,1,128]{5,0,3,1,4,2:T(4,128)(2,1)}), bf16[4,4,64,4,1,128]{5,0,3,1,4,2:T(4,128)(2,1)S(1)}, u32[]{:S(2)}, u32[]{:S(2)}) %all-to-all-start) | async-done | bytes 1048608 | tf_op jit(solution)/shard_map/all_to_all | solution.py:62
  44.7 5.9 %all-to-all-start.1 = ((bf16[4,4,64,4,1,128]{5,0,3,1,4,2:T(4,128)(2,1)}), bf16[4,4,64,4,1,128]{5,0,3,1,4,2:T(4,128)(2,1)S(1)}, u32[]{:S(2)}, u32[]{:S(2)}) async-start(bf16[4,4,64,4,1,128]{5,0,3,1,4,2:T(4,128)(2,1)} %copy.82), calls=%async_computation.1 | async-start | bytes 2097152 | tf_op jit(solution)/shard_map/all_to_all | solution.py:63
  52.2 26.5 %all-to-all-done.1 = bf16[4,4,64,4,1,128]{5,0,3,1,4,2:T(4,128)(2,1)S(1)} async-done(((bf16[4,4,64,4,1,128]{5,0,3,1,4,2:T(4,128)(2,1)}), bf16[4,4,64,4,1,128]{5,0,3,1,4,2:T(4,128)(2,1)S(1)}, u32[]{:S(2)}, u32[]{:S(2)}) %all-to-all-start.1) | async-done | bytes 1048608 | tf_op jit(solution)/shard_map/all_to_all | solution.py:63
  78.7 5.9 %all-to-all-start.5 = ((bf16[4,4,64,4,1,128]{5,3,1,0,4,2:T(4,128)(2,1)}), bf16[4,4,64,4,1,128]{5,3,1,0,4,2:T(4,128)(2,1)S(1)}, u32[]{:S(2)}, u32[]{:S(2)}) async-start(bf16[4,4,64,4,1,128]{5,3,1,0,4,2:T(4,128)(2,1)} %copy.91), calls=%async_computation.5 | async-start | bytes 2097152 | tf_op jit(solution)/shard_map/all_to_all | solution.py:69
  84.7 2.8 copy.84
  87.4 25.3 %all-to-all-done.5 = bf16[4,4,64,4,1,128]{5,3,1,0,4,2:T(4,128)(2,1)S(1)} async-done(((bf16[4,4,64,4,1,128]{5,3,1,0,4,2:T(4,128)(2,1)}), bf16[4,4,64,4,1,128]{5,3,1,0,4,2:T(4,128)(2,1)S(1)}, u32[]{:S(2)}, u32[]{:S(2)}) %all-to-all-start.5) | async-done | bytes 1048608 | tf_op jit(solution)/shard_map/all_to_all | solution.py:69
  112.7 6.3 %all-to-all-start.2 = ((bf16[4,4,64,4,1,128]{5,3,1,0,4,2:T(4,128)(2,1)}), bf16[4,4,64,4,1,128]{5,3,1,0,4,2:T(4,128)(2,1)}, u32[]{:S(2)}, u32[]{:S(2)}) async-start(bf16[4,4,64,4,1,128]{5,3,1,0,4,2:T(4,128)(2,1)} %copy.84), calls=%async_computation.2 | async-start | bytes 2097152 | tf_op jit(solution)/shard_map/all_to_all | solution.py:66
  123.3 4.6 %fusion.12 = (f32[16,256]{1,0:T(8,128)S(1)}, f32[16,256,256]{1,2,0:T(8,128)}) fusion(pred[256,256]{0,1:T(8,128)(4,1)S(1)} %iota_compare_fusion, bf16[256,16,128]{2,0,1:T(8,128)(2,1)} %bitcast.108, bf16[256,16,128]{2,0,1:T(8,128)(2,1)S(1)} %bitcast.107), kind=kOutput, calls=%fused_computation.24 | convolution fusion | flops 272630016 | bytes 6373376 | tf_op jit(solution)/shard_map/sub | solution.py:19
  127.9 2.6 fusion.5
  133.0 13.8 %all-to-all-done.2 = bf16[4,4,64,4,1,128]{5,3,1,0,4,2:T(4,128)(2,1)} async-done(((bf16[4,4,64,4,1,128]{5,3,1,0,4,2:T(4,128)(2,1)}), bf16[4,4,64,4,1,128]{5,3,1,0,4,2:T(4,128)(2,1)}, u32[]{:S(2)}, u32[]{:S(2)}) %all-to-all-start.2) | async-done | bytes 1048608 | tf_op jit(solution)/shard_map/all_to_all | solution.py:66
  146.8 6.3 %all-to-all-start.10 = ((bf16[256,4,1,4,1,128]{5,3,1,4,2,0:T(4,128)(2,1)}), bf16[256,4,1,4,1,128]{5,3,1,4,2,0:T(4,128)(2,1)}, u32[]{:S(2)}, u32[]{:S(2)}) async-start(bf16[256,4,1,4,1,128]{5,3,1,4,2,0:T(4,128)(2,1)} %copy.102), calls=%async_computation.10 | async-start | bytes 2097152 | tf_op jit(solution)/shard_map/all_to_all | solution.py:97
  153.2 2.8 multiply_reduce_fusion
  155.9 2.6 copy.87
  158.6 22.2 %all-to-all-done.10 = bf16[256,4,1,4,1,128]{5,3,1,4,2,0:T(4,128)(2,1)} async-done(((bf16[256,4,1,4,1,128]{5,3,1,4,2,0:T(4,128)(2,1)}), bf16[256,4,1,4,1,128]{5,3,1,4,2,0:T(4,128)(2,1)}, u32[]{:S(2)}, u32[]{:S(2)}) %all-to-all-start.10) | async-done | bytes 1048608 | tf_op jit(solution)/shard_map/all_to_all | solution.py:97
  180.8 6.3 %all-to-all-start.3 = ((bf16[256,4,1,4,1,128]{5,3,1,4,2,0:T(4,128)(2,1)}), bf16[256,4,1,4,1,128]{5,3,1,4,2,0:T(4,128)(2,1)}, u32[]{:S(2)}, u32[]{:S(2)}) async-start(bf16[256,4,1,4,1,128]{5,3,1,4,2,0:T(4,128)(2,1)} %copy.87), calls=%async_computation.3 | async-start | bytes 2097152 | tf_op jit(solution)/shard_map/all_to_all | solution.py:76
  187.1 3.5 multiply_convert_fusion
  193.2 21.4 %all-to-all-done.3 = bf16[256,4,1,4,1,128]{5,3,1,4,2,0:T(4,128)(2,1)} async-done(((bf16[256,4,1,4,1,128]{5,3,1,4,2,0:T(4,128)(2,1)}), bf16[256,4,1,4,1,128]{5,3,1,4,2,0:T(4,128)(2,1)}, u32[]{:S(2)}, u32[]{:S(2)}) %all-to-all-start.3) | async-done | bytes 1048608 | tf_op jit(solution)/shard_map/all_to_all | solution.py:76
  214.6 6.0 %all-to-all-start.8 = ((bf16[256,4,1,4,1,128]{5,3,1,4,2,0:T(4,128)(2,1)}), bf16[256,4,1,4,1,128]{5,3,1,4,2,0:T(4,128)(2,1)S(1)}, u32[]{:S(2)}, u32[]{:S(2)}) async-start(bf16[256,4,1,4,1,128]{5,3,1,4,2,0:T(4,128)(2,1)} %copy.99), calls=%async_computation.8 | async-start | bytes 2097152 | tf_op jit(solution)/shard_map/all_to_all | solution.py:90
  224.3 24.0 %all-to-all-done.8 = bf16[256,4,1,4,1,128]{5,3,1,4,2,0:T(4,128)(2,1)S(1)} async-done(((bf16[256,4,1,4,1,128]{5,3,1,4,2,0:T(4,128)(2,1)}), bf16[256,4,1,4,1,128]{5,3,1,4,2,0:T(4,128)(2,1)S(1)}, u32[]{:S(2)}, u32[]{:S(2)}) %all-to-all-start.8) | async-done | bytes 1048608 | tf_op jit(solution)/shard_map/all_to_all | solution.py:90
  248.3 5.9 %all-to-all-start.6 = ((bf16[256,4,1,4,1,128]{5,3,1,4,2,0:T(4,128)(2,1)}), bf16[256,4,1,4,1,128]{5,3,1,4,2,0:T(4,128)(2,1)S(1)}, u32[]{:S(2)}, u32[]{:S(2)}) async-start(bf16[256,4,1,4,1,128]{5,3,1,4,2,0:T(4,128)(2,1)} %copy.97), calls=%async_computation.6 | async-start | bytes 2097152 | tf_op jit(solution)/shard_map/all_to_all | solution.py:83
  254.2 2.7 copy.120
  256.9 25.2 %all-to-all-done.6 = bf16[256,4,1,4,1,128]{5,3,1,4,2,0:T(4,128)(2,1)S(1)} async-done(((bf16[256,4,1,4,1,128]{5,3,1,4,2,0:T(4,128)(2,1)}), bf16[256,4,1,4,1,128]{5,3,1,4,2,0:T(4,128)(2,1)S(1)}, u32[]{:S(2)}, u32[]{:S(2)}) %all-to-all-start.6) | async-done | bytes 1048608 | tf_op jit(solution)/shard_map/all_to_all | solution.py:83
  282.2 5.8 %all-to-all-start.11 = ((bf16[4,4,64,4,1,128]{5,3,2,0,4,1:T(4,128)(2,1)}), bf16[4,4,64,4,1,128]{5,3,2,0,4,1:T(4,128)(2,1)S(1)}, u32[]{:S(2)}, u32[]{:S(2)}) async-start(bf16[4,4,64,4,1,128]{5,3,2,0,4,1:T(4,128)(2,1)} %bitcast.102), calls=%async_computation.11 | async-start | bytes 2097152 | tf_op jit(solution)/shard_map/all_to_all | solution.py:96
  290.4 25.2 %all-to-all-done.11 = bf16[4,4,64,4,1,128]{5,3,2,0,4,1:T(4,128)(2,1)S(1)} async-done(((bf16[4,4,64,4,1,128]{5,3,2,0,4,1:T(4,128)(2,1)}), bf16[4,4,64,4,1,128]{5,3,2,0,4,1:T(4,128)(2,1)S(1)}, u32[]{:S(2)}, u32[]{:S(2)}) %all-to-all-start.11) | async-done | bytes 1048608 | tf_op jit(solution)/shard_map/all_to_all | solution.py:96
  315.6 4.2 %all-to-all-start.4 = ((bf16[4,4,64,4,1,128]{5,0,2,3,4,1:T(4,128)(2,1)}), bf16[4,4,64,4,1,128]{5,0,2,3,4,1:T(4,128)(2,1)}, u32[]{:S(2)}, u32[]{:S(2)}) async-start(bf16[4,4,64,4,1,128]{5,0,2,3,4,1:T(4,128)(2,1)} %bitcast.103), calls=%async_computation.4 | async-start | bytes 2097152 | tf_op jit(solution)/shard_map/all_to_all | solution.py:75
  321.3 28.0 %all-to-all-done.4 = bf16[4,4,64,4,1,128]{5,0,2,3,4,1:T(4,128)(2,1)} async-done(((bf16[4,4,64,4,1,128]{5,0,2,3,4,1:T(4,128)(2,1)}), bf16[4,4,64,4,1,128]{5,0,2,3,4,1:T(4,128)(2,1)}, u32[]{:S(2)}, u32[]{:S(2)}) %all-to-all-start.4) | async-done | bytes 1048608 | tf_op jit(solution)/shard_map/all_to_all | solution.py:75
  349.4 3.5 all-to-all-start.9
  354.4 28.1 %all-to-all-done.9 = bf16[4,4,64,4,1,128]{5,3,2,0,4,1:T(4,128)(2,1)S(1)} async-done(((bf16[4,4,64,4,1,128]{5,3,2,0,4,1:T(4,128)(2,1)}), bf16[4,4,64,4,1,128]{5,3,2,0,4,1:T(4,128)(2,1)S(1)}, u32[]{:S(2)}, u32[]{:S(2)}) %all-to-all-start.9) | async-done | bytes 1048608 | tf_op jit(solution)/shard_map/all_to_all | solution.py:89
  382.5 3.5 all-to-all-start.7
  393.4 22.0 %all-to-all-done.7 = bf16[4,4,64,4,1,128]{5,3,2,0,4,1:T(4,128)(2,1)S(1)} async-done(((bf16[4,4,64,4,1,128]{5,3,2,0,4,1:T(4,128)(2,1)}), bf16[4,4,64,4,1,128]{5,3,2,0,4,1:T(4,128)(2,1)S(1)}, u32[]{:S(2)}, u32[]{:S(2)}) %all-to-all-start.7) | async-done | bytes 1048608 | tf_op jit(solution)/shard_map/all_to_all | solution.py:82
  (28 shorter events, 31.4 us)
Async XLA Ops:
  0.6 15.7 %copy-start.2 = (bf16[4,1024,1,128]{3,1,2,0:T(8,128)(2,1)S(1)}, bf16[4,1024,1,128]{3,1,2,0:T(8,128)(2,1)}, u32[]{:S(2)}) copy-start(bf16[4,1024,1,128]{3,1,2,0:T(8,128)(2,1)} %param.5) | copy-start | bytes 3145732
  4.3 40.4 %all-to-all-start = ((bf16[4,4,64,4,1,128]{5,0,3,1,4,2:T(4,128)(2,1)}), bf16[4,4,64,4,1,128]{5,0,3,1,4,2:T(4,128)(2,1)S(1)}, u32[]{:S(2)}, u32[]{:S(2)}) async-start(bf16[4,4,64,4,1,128]{5,0,3,1,4,2:T(4,128)(2,1)} %copy.80), calls=%async_computation | async-start | bytes 2097152 | tf_op jit(solution)/shard_map/all_to_all | solution.py:62
  16.4 34.3 %copy-start.3 = (bf16[4,1024,1,128]{3,1,2,0:T(8,128)(2,1)S(1)}, bf16[4,1024,1,128]{3,1,2,0:T(8,128)(2,1)}, u32[]{:S(2)}) copy-start(bf16[4,1024,1,128]{3,1,2,0:T(8,128)(2,1)} %param.7) | copy-start | bytes 3145732
  44.7 34.0 %all-to-all-start.1 = ((bf16[4,4,64,4,1,128]{5,0,3,1,4,2:T(4,128)(2,1)}), bf16[4,4,64,4,1,128]{5,0,3,1,4,2:T(4,128)(2,1)S(1)}, u32[]{:S(2)}, u32[]{:S(2)}) async-start(bf16[4,4,64,4,1,128]{5,0,3,1,4,2:T(4,128)(2,1)} %copy.82), calls=%async_computation.1 | async-start | bytes 2097152 | tf_op jit(solution)/shard_map/all_to_all | solution.py:63
  78.7 34.0 %all-to-all-start.5 = ((bf16[4,4,64,4,1,128]{5,3,1,0,4,2:T(4,128)(2,1)}), bf16[4,4,64,4,1,128]{5,3,1,0,4,2:T(4,128)(2,1)S(1)}, u32[]{:S(2)}, u32[]{:S(2)}) async-start(bf16[4,4,64,4,1,128]{5,3,1,0,4,2:T(4,128)(2,1)} %copy.91), calls=%async_computation.5 | async-start | bytes 2097152 | tf_op jit(solution)/shard_map/all_to_all | solution.py:69
  112.7 34.1 %all-to-all-start.2 = ((bf16[4,4,64,4,1,128]{5,3,1,0,4,2:T(4,128)(2,1)}), bf16[4,4,64,4,1,128]{5,3,1,0,4,2:T(4,128)(2,1)}, u32[]{:S(2)}, u32[]{:S(2)}) async-start(bf16[4,4,64,4,1,128]{5,3,1,0,4,2:T(4,128)(2,1)} %copy.84), calls=%async_computation.2 | async-start | bytes 2097152 | tf_op jit(solution)/shard_map/all_to_all | solution.py:66
  122.1 1.2 copy-start
  146.8 34.0 %all-to-all-start.10 = ((bf16[256,4,1,4,1,128]{5,3,1,4,2,0:T(4,128)(2,1)}), bf16[256,4,1,4,1,128]{5,3,1,4,2,0:T(4,128)(2,1)}, u32[]{:S(2)}, u32[]{:S(2)}) async-start(bf16[256,4,1,4,1,128]{5,3,1,4,2,0:T(4,128)(2,1)} %copy.102), calls=%async_computation.10 | async-start | bytes 2097152 | tf_op jit(solution)/shard_map/all_to_all | solution.py:97
  180.8 33.8 %all-to-all-start.3 = ((bf16[256,4,1,4,1,128]{5,3,1,4,2,0:T(4,128)(2,1)}), bf16[256,4,1,4,1,128]{5,3,1,4,2,0:T(4,128)(2,1)}, u32[]{:S(2)}, u32[]{:S(2)}) async-start(bf16[256,4,1,4,1,128]{5,3,1,4,2,0:T(4,128)(2,1)} %copy.87), calls=%async_computation.3 | async-start | bytes 2097152 | tf_op jit(solution)/shard_map/all_to_all | solution.py:76
  187.1 3.6 copy-start.1
  214.6 33.7 %all-to-all-start.8 = ((bf16[256,4,1,4,1,128]{5,3,1,4,2,0:T(4,128)(2,1)}), bf16[256,4,1,4,1,128]{5,3,1,4,2,0:T(4,128)(2,1)S(1)}, u32[]{:S(2)}, u32[]{:S(2)}) async-start(bf16[256,4,1,4,1,128]{5,3,1,4,2,0:T(4,128)(2,1)} %copy.99), calls=%async_computation.8 | async-start | bytes 2097152 | tf_op jit(solution)/shard_map/all_to_all | solution.py:90
  248.3 33.9 %all-to-all-start.6 = ((bf16[256,4,1,4,1,128]{5,3,1,4,2,0:T(4,128)(2,1)}), bf16[256,4,1,4,1,128]{5,3,1,4,2,0:T(4,128)(2,1)S(1)}, u32[]{:S(2)}, u32[]{:S(2)}) async-start(bf16[256,4,1,4,1,128]{5,3,1,4,2,0:T(4,128)(2,1)} %copy.97), calls=%async_computation.6 | async-start | bytes 2097152 | tf_op jit(solution)/shard_map/all_to_all | solution.py:83
  282.2 33.4 %all-to-all-start.11 = ((bf16[4,4,64,4,1,128]{5,3,2,0,4,1:T(4,128)(2,1)}), bf16[4,4,64,4,1,128]{5,3,2,0,4,1:T(4,128)(2,1)S(1)}, u32[]{:S(2)}, u32[]{:S(2)}) async-start(bf16[4,4,64,4,1,128]{5,3,2,0,4,1:T(4,128)(2,1)} %bitcast.102), calls=%async_computation.11 | async-start | bytes 2097152 | tf_op jit(solution)/shard_map/all_to_all | solution.py:96
  315.6 33.8 %all-to-all-start.4 = ((bf16[4,4,64,4,1,128]{5,0,2,3,4,1:T(4,128)(2,1)}), bf16[4,4,64,4,1,128]{5,0,2,3,4,1:T(4,128)(2,1)}, u32[]{:S(2)}, u32[]{:S(2)}) async-start(bf16[4,4,64,4,1,128]{5,0,2,3,4,1:T(4,128)(2,1)} %bitcast.103), calls=%async_computation.4 | async-start | bytes 2097152 | tf_op jit(solution)/shard_map/all_to_all | solution.py:75
  349.4 33.1 %all-to-all-start.9 = ((bf16[4,4,64,4,1,128]{5,3,2,0,4,1:T(4,128)(2,1)}), bf16[4,4,64,4,1,128]{5,3,2,0,4,1:T(4,128)(2,1)S(1)}, u32[]{:S(2)}, u32[]{:S(2)}) async-start(bf16[4,4,64,4,1,128]{5,3,2,0,4,1:T(4,128)(2,1)} %bitcast.104), calls=%async_computation.9 | async-start | bytes 2097152 | tf_op jit(solution)/shard_map/all_to_all | solution.py:89
  382.5 33.0 %all-to-all-start.7 = ((bf16[4,4,64,4,1,128]{5,3,2,0,4,1:T(4,128)(2,1)}), bf16[4,4,64,4,1,128]{5,3,2,0,4,1:T(4,128)(2,1)S(1)}, u32[]{:S(2)}, u32[]{:S(2)}) async-start(bf16[4,4,64,4,1,128]{5,3,2,0,4,1:T(4,128)(2,1)} %bitcast.100), calls=%async_computation.7 | async-start | bytes 2097152 | tf_op jit(solution)/shard_map/all_to_all | solution.py:82
where the time goes:
time: 419 us; the launch traced here: 417 us
  waiting for transfers between devices  288 us (69%)
  starting transfers between devices  71.9 us (17%)
  local copies, waits for them, and re-layouts  39.7 us (9%)
  matrix products  14.3 us (3%)
    all_to_all x1, waiting for transfers between devices, shards(): lax.all_to_all(lax.all_to_all(results[2], 'row', split_axis=0, concat_axi...  28.1 us
    all_to_all x1, waiting for transfers between devices, shards(): lax.all_to_all(lax.all_to_all(results[0], 'row', split_axis=0, concat_axi...  28 us
    all_to_all x1, waiting for transfers between devices, shards(): lax.all_to_all(split_columns(keys_proj), 'row', split_axis=2, concat_axis...  26.5 us
    all_to_all x1, waiting for transfers between devices, shards(): lax.all_to_all(split_columns(queries), 'row', split_axis=2, concat_axis=0...  26 us
    all_to_all x1, waiting for transfers between devices, shards(): lax.all_to_all(split_columns(grad_output), 'row', split_axis=2, concat_ax...  25.3 us
    all_to_all x1, waiting for transfers between devices, shards(): lax.all_to_all(results[1], 'row', split_axis=0, concat_axis=2, tiled=True)  25.2 us
    all_to_all x1, waiting for transfers between devices, shards(): lax.all_to_all(lax.all_to_all(results[3], 'row', split_axis=0, concat_axi...  25.2 us
    all_to_all x1, waiting for transfers between devices, shards(): lax.all_to_all(results[2], 'row', split_axis=0, concat_axis=2, tiled=True)  24 us
  transfers between devices with their start and end apart: 12, of which 12 were waited for; matrix products, arithmetic and copies ran while one was open for 12% of the time, Pallas kernels for 0%

commit v1 on v0

v1 whole, which is shorter than its diff:
```python
import jax
import jax.numpy as jnp
from jax import lax
from jax.experimental import pallas as pl
from jax.experimental.pallas import tpu as pltpu
from jax.sharding import PartitionSpec as P

NAMES = ("row", "head")
LAST = (((1,), (1,)), ((), ()))
FIRST = (((0,), (0,)), ((), ()))
F32 = jnp.float32
LIMIT = 48 * 2**20


def attend_column(query, key, value, cotangent):
    count = query.shape[0]
    scale = query.shape[-1] ** (-0.5)
    scores = lax.dot_general(key, query, LAST, preferred_element_type=F32)
    grad_weights = lax.dot_general(value, cotangent, LAST, preferred_element_type=F32)
    key_at = lax.broadcasted_iota(jnp.int32, (count, count), 0)
    query_at = lax.broadcasted_iota(jnp.int32, (count, count), 1)
    scores = jnp.where(key_at <= query_at, scores, -jnp.inf)
    largest = jnp.max(scores, axis=0, keepdims=True)
    raw = jnp.exp((scores - largest) * scale)
    weights = raw * (1.0 / jnp.sum(raw, axis=0, keepdims=True))
    dots = jnp.sum(weights * grad_weights, axis=0, keepdims=True)
    low = weights.astype(jnp.bfloat16)
    grad_scores = (weights * (grad_weights - dots) * scale).astype(jnp.bfloat16)
    return (
        lax.dot_general(low, value, FIRST, preferred_element_type=F32),
        lax.dot_general(grad_scores, key, FIRST, preferred_element_type=F32),
        jnp.dot(grad_scores, query, preferred_element_type=F32),
        jnp.dot(low, cotangent, preferred_element_type=F32),
    )


def pack_kernel(*refs):
    *in_refs, out_ref, sems = refs
    copies = []
    for array, ref in enumerate(in_refs):
        for row in range(ref.shape[0]):
            for part in range(ref.shape[1]):
                copies.append(
                    pltpu.make_async_copy(
                        ref.at[row, part], out_ref.at[:, array, row, part], sems.at[len(copies)]
                    )
                )
                copies[-1].start()
    for copy in copies:
        copy.wait()


def pack(arrays):
    row, part, owner, inner, feature = arrays[0].shape
    count = len(arrays)
    return pl.pallas_call(
        pack_kernel,
        out_shape=jax.ShapeDtypeStruct((owner, count, row, part, inner, feature), arrays[0].dtype),
        in_specs=[pl.BlockSpec(memory_space=pl.ANY)] * count,
        out_specs=pl.BlockSpec(memory_space=pl.ANY),
        scratch_shapes=[pltpu.SemaphoreType.DMA((count * row * part,))],
        name="pack",
    )(*arrays)


def attend_kernel(in_ref, out_ref, wide_in, wide_out):
    sources, arrays, row, columns, feature = in_ref.shape
    owners, parts, _, _, inner, _ = out_ref.shape
    rows = sources * row

    def widen(source, carry):
        for array in range(arrays):
            block = in_ref[source, array].reshape(row * columns, feature)
            start = pl.multiple_of(source * row * columns, row * columns)
            wide_in[array, pl.ds(start, row * columns), :] = block.astype(F32)
        return carry

    lax.fori_loop(0, sources, widen, 0)

    def column(at, carry):
        block = [
            wide_in[array, pl.ds(at, rows, stride=columns), :].astype(jnp.bfloat16)
            for array in range(arrays)
        ]
        for array, result in enumerate(attend_column(*block)):
            wide_out[array, pl.ds(at, rows, stride=columns), :] = result
        return carry

    lax.fori_loop(0, columns, column, 0)

    def narrow(owner, carry):
        for array in range(arrays):
            for r in range(row):
                for part in range(parts):
                    start = owner * row * columns + r * columns + part * inner
                    out_ref[owner, part, array, r] = wide_out[array, pl.ds(start, inner), :].astype(
                        out_ref.dtype
                    )
        return carry

    lax.fori_loop(0, owners, narrow, 0)


def attend(arrived, parts):
    sources, arrays, row, columns, feature = arrived.shape
    rows = sources * row
    whole = pl.BlockSpec(memory_space=pltpu.VMEM)
    return pl.pallas_call(
        attend_kernel,
        out_shape=jax.ShapeDtypeStruct(
            (sources, parts, arrays, row, columns // parts, feature), arrived.dtype
        ),
        in_specs=[whole],
        out_specs=whole,
        scratch_shapes=[pltpu.VMEM((arrays, rows * columns, feature), F32)] * 2,
        compiler_params=pltpu.CompilerParams(vmem_limit_bytes=LIMIT),
        cost_estimate=pl.CostEstimate(
            flops=12 * columns * rows * rows * feature,
            bytes_accessed=4 * arrived.size,
            transcendentals=columns * rows * rows,
        ),
        name="attend",
    )(arrived)


def unpack_kernel(in_ref, *refs):
    *out_refs, wide = refs
    sources, heads, arrays, rows, inner, feature = in_ref.shape

    def step(source, carry):
        for array in range(arrays):
            for row in range(rows):
                base = (array * rows + row) * heads * inner
                for head in range(heads):
                    wide[pl.ds(base + head * inner, inner), :] = in_ref[
                        source, head, array, row
                    ].astype(F32)
                for at in range(inner):
                    out_refs[array][row, source * inner + at] = wide[
                        pl.ds(base + at, heads, stride=inner), :
                    ].astype(in_ref.dtype)
        return carry

    lax.fori_loop(0, sources, step, 0)


def unpack(returned):
    sources, heads, arrays, rows, inner, feature = returned.shape
    whole = pl.BlockSpec(memory_space=pltpu.VMEM)
    return pl.pallas_call(
        unpack_kernel,
        out_shape=[jax.ShapeDtypeStruct((rows, sources * inner, heads, feature), returned.dtype)]
        * arrays,
        in_specs=[whole],
        out_specs=[whole] * arrays,
        scratch_shapes=[pltpu.VMEM((arrays * rows * heads * inner, feature), F32)],
        compiler_params=pltpu.CompilerParams(vmem_limit_bytes=LIMIT),
        name="unpack",
    )(returned)


def shards(*arrays):
    row_devs = lax.axis_size("row")
    head_devs = lax.axis_size("head")
    local_rows, columns, _, features = arrays[0].shape
    inner = columns // (row_devs * head_devs)
    count = len(arrays)

    packed = pack([a.reshape(local_rows, head_devs, row_devs, inner, features) for a in arrays])
    packed = packed.reshape(row_devs, count, local_rows, head_devs * inner, features)
    arrived = lax.all_to_all(packed, "row", 0, 0, tiled=True)
    results = attend(arrived, head_devs)
    results = results.reshape(row_devs * head_devs, count, local_rows, inner, features)
    returned = lax.all_to_all(results, NAMES, 0, 0, tiled=True)
    returned = returned.reshape(row_devs, head_devs, count, local_rows, inner, features)
    return tuple(unpack(returned))


def solution(mesh):
    spec_in = P("row", None, "head", None)
    spec_out = P("row", "head", None, None)
    return jax.shard_map(
        shards, mesh=mesh, in_specs=(spec_in,) * 4, out_specs=(spec_out,) * 4, check_vma=False
    )
```

time: 419 us -> 368 us (0.88)
  waiting for transfers between devices: 288 us -> 0 us
  blocking collectives: 0 us -> 212 us
  Pallas kernels: 0 us -> 153 us
  starting transfers between devices: 71.9 us -> 0 us
  local copies, waits for them, and re-layouts: 39.7 us -> 0 us
  matrix products: 14.3 us -> 0 us
    all_to_all x12 -> x0, waiting for transfers between devices: 288 us -> none  [the longest x1 28.1 us: shards(): lax.all_to_all(lax.all_to_all(results[2], 'row', split_axis=0, concat_axi...]
    all_to_all x0 -> x2, blocking collectives: none -> 212 us  [the longest x1 108 us: shards(): arrived = lax.all_to_all(packed, 'row', 0, 0, tiled=True)]
    pallas_call x0 -> x3, Pallas kernels: none -> 153 us  [the longest x1 129 us: pack(): pl.pallas_call(pack_kernel, out_shape=jax.ShapeDtypeStruct((owner, count,...]
    all_to_all x12 -> x0, starting transfers between devices: 71.9 us -> none  [the longest x1 12.1 us: shards(): lax.all_to_all(split_columns(queries), 'row', split_axis=2, concat_axis=0...]
    reshape x9 -> x0, local copies, waits for them, and re-layouts: 19.1 us -> none  [the longest x4 10.3 us: split_columns(): array.reshape(local_rows, head_devs, row_devs, inner_cols, local_heads, h...]
    all_to_all x7 -> x0, local copies, waits for them, and re-layouts: 13.1 us -> none  [the longest x1 2.68 us: shards(): lax.all_to_all(results[3], 'row', split_axis=0, concat_axis=2, tiled=True)]
    dot_general x5 -> x0, matrix products: 9.74 us -> none  [the longest x1 3.53 us: attend(): jnp.einsum('rbd,sbd->brs', grad_output, values_proj, preferred_element_ty...]
    unnamed x12 -> x0, local copies, waits for them, and re-layouts: 7.58 us -> none
  transfers between devices with their start and end apart: 12 -> 0, of which waited for: 12 -> 0; matrix products, arithmetic and copies ran while one was open for 12% -> 0% of each run, Pallas kernels for 0% -> 0%
where the time goes in v1:
time: 368 us; the launch traced here: 365 us
  blocking collectives  212 us (58%)
  Pallas kernels  153 us (42%)
    pallas_call x1, Pallas kernels, pack(): pl.pallas_call(pack_kernel, out_shape=jax.ShapeDtypeStruct((owner, count,...  129 us
    all_to_all x1, blocking collectives, shards(): arrived = lax.all_to_all(packed, 'row', 0, 0, tiled=True)  108 us
    all_to_all x1, blocking collectives, shards(): returned = lax.all_to_all(results, NAMES, 0, 0, tiled=True)  104 us
    pallas_call x1, Pallas kernels, attend(): pl.pallas_call(attend_kernel, out_shape=jax.ShapeDtypeStruct((sources, pa...  19.2 us

profile of v1, /device:TPU:2, one launch (start us, length us, event | category | flops | bytes accessed | tf_op | source)
XLA Modules:
  0.0 365.2 jit_solution(14301404251135237674)
XLA Ops:
  0.6 128.7 %pack.1 = bf16[64,4,4,4,4,128]{5,4,3,2,1,0:T(4,128)(2,1)} custom-call(bf16[4,4,64,4,128]{4,3,2,1,0:T(4,128)(2,1)} %bitcast.10, bf16[4,4,64,4,128]{4,3,2,1,0:T(4,128)(2,1)} %bitcast.11, bf16[4,4,64,4,128]{4,3,2,1,0:T(4,128)(2,1)} %bitcast.12, bf16[4,4,64,4,128]{4,3,2,1,0:T(4,128)(2,1)} %bitcast.13), custom_call_target="tpu_custom_call" | custom-call | tf_op jit(solution)/shard_map/pack/pallas_call | solution.py:56
  129.4 107.6 %all_to_all.10.in_ref = bf16[64,4,4,16,128]{4,3,2,1,0:T(8,128)(2,1)} all-to-all(bf16[64,4,4,16,128]{4,3,2,1,0:T(8,128)(2,1)} %bitcast.9), channel_id=1, replica_groups=mesh['row'=64,'head'=4] {'row'}, dimensions={0} | all-to-all | bytes 8388608 | tf_op jit(solution)/shard_map/all_to_all | solution.py:171
  237.0 19.2 %attend.1 = bf16[64,4,4,4,4,128]{5,4,3,2,1,0:T(4,128)(2,1)S(1)} custom-call(bf16[64,4,4,16,128]{4,3,2,1,0:T(8,128)(2,1)} %all_to_all.10.in_ref), custom_call_target="tpu_custom_call" | custom-call | flops 1610612736 | bytes 8388608 | tf_op jit(solution)/shard_map/attend/pallas_call | solution.py:108
  256.2 104.1 %all_to_all.11 = bf16[256,4,4,4,128]{4,3,2,1,0:T(4,128)(2,1)S(1)} all-to-all(bf16[256,4,4,4,128]{4,3,2,1,0:T(4,128)(2,1)S(1)} %bitcast.8), channel_id=1, replica_groups=mesh['row'=64,'head'=4] {'row','head'}, dimensions={0} | all-to-all | bytes 8388608 | tf_op jit(solution)/shard_map/all_to_all | solution.py:174
  360.4 4.8 %unpack.1 = (bf16[4,256,4,128]{3,2,1,0:T(4,128)(2,1)}, bf16[4,256,4,128]{3,2,1,0:T(4,128)(2,1)}, bf16[4,256,4,128]{3,2,1,0:T(4,128)(2,1)}, bf16[4,256,4,128]{3,2,1,0:T(4,128)(2,1)}) custom-call(bf16[64,4,4,4,4,128]{5,4,3,2,1,0:T(4,128)(2,1)S(1)} %bitcast.7), custom_call_target="tpu_custom_call" | custom-call | tf_op jit(solution)/shard_map/unpack/pallas_call | solution.py:150

commit v2 on v1

--- a/solution.py
+++ b/solution.py
@@ -35,30 +35,29 @@
 
 
 def pack_kernel(*refs):
-    *in_refs, out_ref, sems = refs
-    copies = []
-    for array, ref in enumerate(in_refs):
-        for row in range(ref.shape[0]):
-            for part in range(ref.shape[1]):
-                copies.append(
-                    pltpu.make_async_copy(
-                        ref.at[row, part], out_ref.at[:, array, row, part], sems.at[len(copies)]
-                    )
-                )
-                copies[-1].start()
-    for copy in copies:
-        copy.wait()
+    *in_refs, out_ref = refs
+    rows, parts, owners, _, _ = in_refs[0].shape
+
+    def step(owner, carry):
+        for array, ref in enumerate(in_refs):
+            for row in range(rows):
+                for part in range(parts):
+                    out_ref[owner, array, row, part] = ref[row, part, owner]
+        return carry
+
+    lax.fori_loop(0, owners, step, 0)
 
 
 def pack(arrays):
     row, part, owner, inner, feature = arrays[0].shape
     count = len(arrays)
+    whole = pl.BlockSpec(memory_space=pltpu.VMEM)
     return pl.pallas_call(
         pack_kernel,
         out_shape=jax.ShapeDtypeStruct((owner, count, row, part, inner, feature), arrays[0].dtype),
-        in_specs=[pl.BlockSpec(memory_space=pl.ANY)] * count,
-        out_specs=pl.BlockSpec(memory_space=pl.ANY),
-        scratch_shapes=[pltpu.SemaphoreType.DMA((count * row * part,))],
+        in_specs=[whole] * count,
+        out_specs=whole,
+        compiler_params=pltpu.CompilerParams(vmem_limit_bytes=LIMIT),
         name="pack",
     )(*arrays)
 

time: 368 us -> 248 us (0.67)
  Pallas kernels: 153 us -> 28.3 us
  local copies, waits for them, and re-layouts: 0 us -> 4.89 us
    pallas_call x1, Pallas kernels: 129 us -> 4.23 us  [pack(): pl.pallas_call(pack_kernel, out_shape=jax.ShapeDtypeStruct((owner, count,...]
    unnamed x0 -> x8, local copies, waits for them, and re-layouts: none -> 4.89 us
where the time goes in v2:
time: 248 us; the launch traced here: 246 us
  blocking collectives  212 us (85%)
  Pallas kernels  28.3 us (11%)
  local copies, waits for them, and re-layouts  4.89 us (2%)
    all_to_all x1, blocking collectives, shards(): arrived = lax.all_to_all(packed, 'row', 0, 0, tiled=True)  108 us
    all_to_all x1, blocking collectives, shards(): returned = lax.all_to_all(results, NAMES, 0, 0, tiled=True)  104 us
    pallas_call x1, Pallas kernels, attend(): pl.pallas_call(attend_kernel, out_shape=jax.ShapeDtypeStruct((sources, pa...  19.2 us

profile of v2, /device:TPU:2, one launch (start us, length us, event | category | flops | bytes accessed | tf_op | source)
XLA Modules:
  0.0 245.6 jit_solution(10564711047483101640)
XLA Ops:
  0.6 0.0 copy-start
  0.6 1.2 copy-done
  1.9 0.0 copy-start.1
  1.9 1.2 copy-done.1
  3.1 0.0 copy-start.2
  3.1 1.2 copy-done.2
  4.3 0.0 copy-start.3
  4.3 1.2 copy-done.3
  5.5 4.2 %pack.1 = bf16[64,4,4,4,4,128]{5,4,3,2,1,0:T(4,128)(2,1)} custom-call(bf16[4,4,64,4,128]{4,3,2,1,0:T(4,128)(2,1)S(1)} %bitcast.9, bf16[4,4,64,4,128]{4,3,2,1,0:T(4,128)(2,1)S(1)} %bitcast.10, bf16[4,4,64,4,128]{4,3,2,1,0:T(4,128)(2,1)S(1)} %bitcast.11, bf16[4,4,64,4,128]{4,3,2,1,0:T(4,128)(2,1)S(1)} %bitcast.12), custom_call_target="tpu_custom_call" | custom-call | tf_op jit(solution)/shard_map/pack/pallas_call | solution.py:55
  9.8 107.6 %all_to_all.10.in_ref = bf16[64,4,4,16,128]{4,3,2,1,0:T(8,128)(2,1)} all-to-all(bf16[64,4,4,16,128]{4,3,2,1,0:T(8,128)(2,1)} %bitcast.13), channel_id=1, replica_groups=mesh['row'=64,'head'=4] {'row'}, dimensions={0} | all-to-all | bytes 8388608 | tf_op jit(solution)/shard_map/all_to_all | solution.py:170
  117.4 19.2 %attend.1 = bf16[64,4,4,4,4,128]{5,4,3,2,1,0:T(4,128)(2,1)S(1)} custom-call(bf16[64,4,4,16,128]{4,3,2,1,0:T(8,128)(2,1)} %all_to_all.10.in_ref), custom_call_target="tpu_custom_call" | custom-call | flops 1610612736 | bytes 8388608 | tf_op jit(solution)/shard_map/attend/pallas_call | solution.py:107
  136.6 104.1 %all_to_all.11 = bf16[256,4,4,4,128]{4,3,2,1,0:T(4,128)(2,1)S(1)} all-to-all(bf16[256,4,4,4,128]{4,3,2,1,0:T(4,128)(2,1)S(1)} %bitcast.8), channel_id=1, replica_groups=mesh['row'=64,'head'=4] {'row','head'}, dimensions={0} | all-to-all | bytes 8388608 | tf_op jit(solution)/shard_map/all_to_all | solution.py:173
  240.7 4.8 %unpack.1 = (bf16[4,256,4,128]{3,2,1,0:T(4,128)(2,1)}, bf16[4,256,4,128]{3,2,1,0:T(4,128)(2,1)}, bf16[4,256,4,128]{3,2,1,0:T(4,128)(2,1)}, bf16[4,256,4,128]{3,2,1,0:T(4,128)(2,1)}) custom-call(bf16[64,4,4,4,4,128]{5,4,3,2,1,0:T(4,128)(2,1)S(1)} %bitcast.7), custom_call_target="tpu_custom_call" | custom-call | tf_op jit(solution)/shard_map/unpack/pallas_call | solution.py:149
Async XLA Ops:
  0.6 1.2 copy-start
  1.9 1.2 copy-start.1
  3.1 1.2 copy-start.2
  4.3 1.2 copy-start.3

commit v3 on v2

v3 whole, which is shorter than its diff:
```python
import jax
import jax.numpy as jnp
from jax import lax
from jax.experimental import pallas as pl
from jax.experimental.pallas import tpu as pltpu
from jax.sharding import Mesh, PartitionSpec as P

FINE = ("y", "z", "x", "w", "core")
SIZES = (4, 4, 4, 2, 2)
LAST = (((1,), (1,)), ((), ()))
FIRST = (((0,), (0,)), ((), ()))
F32 = jnp.float32
BF16 = jnp.bfloat16
LIMIT = 48 * 2**20
WHOLE = pl.BlockSpec(memory_space=pltpu.VMEM)


def edge(z, count):
    return jnp.where((z == 0) | (z == count - 1), 1, 0)


def other_run(w, chunk, z, count):
    return (w + chunk + edge(z, count)) % 2


def attend_column(query, key, value, cotangent):
    count = query.shape[0]
    scale = query.shape[-1] ** (-0.5)
    scores = lax.dot_general(key, query, LAST, preferred_element_type=F32)
    grad_weights = lax.dot_general(value, cotangent, LAST, preferred_element_type=F32)
    key_at = lax.broadcasted_iota(jnp.int32, (count, count), 0)
    query_at = lax.broadcasted_iota(jnp.int32, (count, count), 1)
    scores = jnp.where(key_at <= query_at, scores, -jnp.inf)
    largest = jnp.max(scores, axis=0, keepdims=True)
    raw = jnp.exp((scores - largest) * scale)
    weights = raw * (1.0 / jnp.sum(raw, axis=0, keepdims=True))
    dots = jnp.sum(weights * grad_weights, axis=0, keepdims=True)
    low = weights.astype(BF16)
    grad_scores = (weights * (grad_weights - dots) * scale).astype(BF16)
    return (
        lax.dot_general(low, value, FIRST, preferred_element_type=F32),
        lax.dot_general(grad_scores, key, FIRST, preferred_element_type=F32),
        jnp.dot(grad_scores, query, preferred_element_type=F32),
        jnp.dot(low, cotangent, preferred_element_type=F32),
    )


def pack_kernel(sizes, chunk, split, place_ref, *refs):
    ys, zs, xs, _, cores = sizes
    in_refs, out_refs = refs[:4], refs[4:]
    rows = in_refs[0].shape[0]
    my_z, my_w = place_ref[0], place_ref[1]
    for shift in range(zs):
        z = (my_z + shift) % zs
        run = other_run(my_w, chunk, z, zs)

        def step(at, carry, shift=shift, z=z, run=run):
            y, x = at // xs, at % xs
            owner = (y * zs + z) * xs + x
            for core in range(cores):
                for array, ref in enumerate(in_refs):
                    for row in range(rows):
                        tile = ref[row, run * cores + core, owner]
                        if split:
                            out_refs[shift][at * cores + core, array, row] = tile
                        else:
                            out_refs[0][at * cores + core, shift, array, row] = tile
            return carry

        lax.fori_loop(0, ys * xs, step, 0)


def pack(arrays, place, sizes, chunk, split):
    ys, zs, xs, _, cores = sizes
    rows, _, _, inner, feature = arrays[0].shape
    tail = (len(arrays), rows, inner, feature)
    if split:
        shapes = [jax.ShapeDtypeStruct((ys * xs * cores, *tail), BF16)] * zs
    else:
        shapes = [jax.ShapeDtypeStruct((ys * xs * cores, zs, *tail), BF16)]
    return pl.pallas_call(
        lambda *refs: pack_kernel(sizes, chunk, split, *refs),
        out_shape=shapes,
        in_specs=[pl.BlockSpec(memory_space=pltpu.SMEM)] + [WHOLE] * 4,
        out_specs=[WHOLE] * len(shapes),
        compiler_params=pltpu.CompilerParams(vmem_limit_bytes=LIMIT),
        name="pack",
    )(place, *arrays)


def attend_kernel(sizes, joined, split, place_ref, *refs):
    ys, zs, xs, _, cores = sizes
    in_refs, refs = (refs[:1], refs[1:]) if joined else (refs[:zs], refs[zs:])
    *out_refs, wide_in, wide_out = refs
    arrays, tile, feature = in_refs[0].shape[-3:]
    local = 4
    inner = tile // local
    rows = ys * zs * xs * local
    my_z = place_ref[0]
    for shift in range(zs):
        z = (my_z - shift + zs) % zs

        def widen(at, carry, shift=shift, z=z):
            y, x = at // xs, at % xs
            start = ((y * zs + z) * xs + x) * tile
            for core in range(cores):
                for array in range(arrays):
                    source = at * cores + core
                    block = in_refs[0][source, shift, array] if joined else in_refs[shift][source, array]
                    to = pl.multiple_of(core * rows * inner + start, tile)
                    wide_in[array, pl.ds(to, tile), :] = block.astype(F32)
            return carry

        lax.fori_loop(0, ys * xs, widen, 0)

    def column(at, carry):
        core, place = at // inner, at % inner
        block = [
            wide_in[array, pl.ds(core * rows * inner + place, rows, stride=inner), :].astype(BF16)
            for array in range(arrays)
        ]
        for array, result in enumerate(attend_column(*block)):
            wide_out[array, pl.ds(place * cores + core, rows, stride=inner * cores), :] = result
        return carry

    lax.fori_loop(0, cores * inner, column, 0)

    for shift in range(zs):
        z = (my_z + shift) % zs

        def narrow(at, carry, shift=shift, z=z):
            y, x = at // xs, at % xs
            start = pl.multiple_of(((y * zs + z) * xs + x) * tile * cores, tile * cores)
            for array in range(arrays):
                block = wide_out[array, pl.ds(start, tile * cores), :].astype(BF16)
                if split:
                    out_refs[shift][at, array] = block
                else:
                    out_refs[0][at, shift, array] = block
            return carry

        lax.fori_loop(0, ys * xs, narrow, 0)


def attend(pieces, place, sizes, joined, split):
    ys, zs, xs, _, cores = sizes
    arrays, tile, feature = pieces[0].shape[-3:]
    rows = ys * zs * xs * 4
    columns = tile // 4 * cores
    tail = (arrays, tile * cores, feature)
    if split:
        shapes = [jax.ShapeDtypeStruct((ys * xs, *tail), BF16)] * zs
    else:
        shapes = [jax.ShapeDtypeStruct((ys * xs, zs, *tail), BF16)]
    return pl.pallas_call(
        lambda *refs: attend_kernel(sizes, joined, split, *refs),
        out_shape=shapes,
        in_specs=[pl.BlockSpec(memory_space=pltpu.SMEM)] + [WHOLE] * len(pieces),
        out_specs=[WHOLE] * len(shapes),
        scratch_shapes=[pltpu.VMEM((arrays, rows * columns, feature), F32)] * 2,
        compiler_params=pltpu.CompilerParams(vmem_limit_bytes=LIMIT),
        cost_estimate=pl.CostEstimate(
            flops=12 * columns * rows * rows * feature,
            bytes_accessed=4 * arrays * rows * columns * feature,
            transcendentals=columns * rows * rows,
        ),
        name="attend",
    )(place, *pieces)


def join_kernel(*refs):
    *in_refs, out_ref = refs
    for shift, ref in enumerate(in_refs):
        out_ref[:, shift] = ref[...]


def join(pieces):
    first, *tail = pieces[0].shape
    return pl.pallas_call(
        join_kernel,
        out_shape=jax.ShapeDtypeStruct((first, len(pieces), *tail), BF16),
        in_specs=[WHOLE] * len(pieces),
        out_specs=WHOLE,
        compiler_params=pltpu.CompilerParams(vmem_limit_bytes=LIMIT),
        name="join",
    )(*pieces)


def part_kernel(in_ref, *out_refs):
    for shift, ref in enumerate(out_refs):
        ref[...] = in_ref[:, shift]


def part(joined):
    first, shifts, *tail = joined.shape
    return pl.pallas_call(
        part_kernel,
        out_shape=[jax.ShapeDtypeStruct((first, *tail), BF16)] * shifts,
        in_specs=[WHOLE],
        out_specs=[WHOLE] * shifts,
        compiler_params=pltpu.CompilerParams(vmem_limit_bytes=LIMIT),
        name="part",
    )(joined)


def unpack_kernel(sizes, place_ref, first_ref, *refs):
    ys, zs, xs, ws, cores = sizes
    second_refs, refs = refs[:zs], refs[zs:]
    *out_refs, narrow_in, wide = refs
    arrays, tile, feature = first_ref.shape[-3:]
    rows, width, _ = out_refs[0].shape
    heads = ws * cores
    inner = tile // cores // rows
    my_z, my_w = place_ref[0], place_ref[1]
    for shift in range(zs):
        z = (my_z - shift + zs) % zs
        runs = [other_run(my_w, chunk, z, zs) for chunk in range(2)]

        def step(at, carry, shift=shift, z=z, runs=runs):
            y, x = at // xs, at % xs
            owner = (y * zs + z) * xs + x
            for array in range(arrays):
                for chunk in range(2):
                    block = first_ref[at, shift, array] if chunk == 0 else second_refs[shift][at, array]
                    spot = (array * 2 + chunk) * tile
                    narrow_in[pl.ds(spot, tile), :] = block.astype(F32)
                    for core in range(cores):
                        to = array * tile * ws + runs[chunk] * cores + core
                        wide[pl.ds(to, tile // cores, stride=heads), :] = narrow_in[
                            pl.ds(spot + core, tile // cores, stride=cores), :
                        ]
                for row in range(rows):
                    size = inner * heads
                    block = wide[pl.ds(array * tile * ws + row * size, size), :].astype(BF16)
                    to = pl.multiple_of(owner * size, size)
                    out_refs[array][row, pl.ds(to, size), :] = block
            return carry

        lax.fori_loop(0, ys * xs, step, 0)


def unpack(first, second, place, sizes, rows):
    ys, zs, xs, ws, cores = sizes
    arrays, tile, feature = first.shape[-3:]
    inner = tile // cores // rows
    width = ys * zs * xs * inner * ws * cores
    return pl.pallas_call(
        lambda *refs: unpack_kernel(sizes, *refs),
        out_shape=[jax.ShapeDtypeStruct((rows, width, feature), BF16)] * arrays,
        in_specs=[pl.BlockSpec(memory_space=pltpu.SMEM)] + [WHOLE] * (1 + zs),
        out_specs=[WHOLE] * arrays,
        scratch_shapes=[
            pltpu.VMEM((arrays * tile * 2, feature), F32),
            pltpu.VMEM((arrays * tile * ws, feature), F32),
        ],
        compiler_params=pltpu.CompilerParams(vmem_limit_bytes=LIMIT),
        name="unpack",
    )(place, first, *second)


def z_in(pieces, zs):
    return [pieces[0]] + [
        lax.ppermute(pieces[k], "z", [(z, (z + k) % zs) for z in range(zs)]) for k in range(1, zs)
    ]


def z_out(pieces, zs, ws, chunk):
    def pairs(k):
        made = []
        for z in range(zs):
            for w in range(ws):
                to = (w + chunk + (z in (0, zs - 1))) % ws
                made.append((z * ws + w, (z + k) % zs * ws + to))
        return made

    return [lax.ppermute(pieces[k], ("z", "w"), pairs(k)) for k in range(zs)]


def shards(*arrays):
    sizes = tuple(lax.axis_size(name) for name in FINE)
    ys, zs, xs, ws, cores = sizes
    rows, columns, _, feature = arrays[0].shape
    owners = ys * zs * xs
    inner = columns // (owners * ws * cores)
    arrays = [a.reshape(rows, ws * cores, owners, inner, feature) for a in arrays]
    place = jnp.stack([lax.axis_index("z"), lax.axis_index("w")]).astype(jnp.int32)

    def flat(piece):
        return piece.reshape(*piece.shape[:-3], rows * inner, feature)

    def across(whole, names):
        return lax.all_to_all(whole, names, 0, 0, tiled=True)

    first = z_in([flat(p) for p in pack(arrays, place, sizes, 0, True)], zs)
    second = across(flat(pack(arrays, place, sizes, 1, False)[0]), ("y", "x", "core"))
    second = z_in(part(second), zs)
    first = across(join(first), ("y", "x", "core"))

    first = attend([first], place, sizes, True, True)
    first = z_out(first, zs, ws, 0)
    second = attend(second, place, sizes, False, False)[0]
    second = z_out(part(across(second, ("y", "x"))), zs, ws, 1)
    first = across(join(first), ("y", "x"))

    results = unpack(first, second, place, sizes, rows)
    return tuple(r.reshape(rows, columns // (ws * cores), ws * cores, feature) for r in results)


def solution(mesh):
    fine = Mesh(mesh.devices.reshape(SIZES), FINE)
    row, head = FINE[:3], FINE[3:]
    spec_in = P(row, None, head, None)
    spec_out = P(row, head, None, None)
    return jax.shard_map(
        shards, mesh=fine, in_specs=(spec_in,) * 4, out_specs=(spec_out,) * 4, check_vma=False
    )
```

time: 248 us -> 284 us (1.15)
  blocking collectives: 212 us -> 0 us
  waiting for transfers between devices: 0 us -> 160 us
  starting transfers between devices: 0 us -> 79 us
  local copies, waits for them, and re-layouts: 4.89 us -> 11.3 us
    all_to_all x2 -> x0, blocking collectives: 212 us -> none  [the longest x1 108 us: shards(): arrived = lax.all_to_all(packed, 'row', 0, 0, tiled=True)]
    ppermute x0 -> x14, waiting for transfers between devices: none -> 160 us  [the longest x8 93.6 us: z_out(): return [lax.ppermute(pieces[k], ('z', 'w'), pairs(k)) for k in range(zs)]]
    ppermute x0 -> x14, starting transfers between devices: none -> 49.3 us  [the longest x8 28.8 us: z_out(): return [lax.ppermute(pieces[k], ('z', 'w'), pairs(k)) for k in range(zs)]]
    all_to_all x0 -> x4, starting transfers between devices: none -> 29.7 us  [across(): return lax.all_to_all(whole, names, 0, 0, tiled=True)]
    unnamed x8 -> x20, local copies, waits for them, and re-layouts: 4.89 us -> 11.3 us
    pallas_call x3 -> x9, Pallas kernels: 28.3 us -> 30.8 us  [the longest x2 16.8 us: attend(): pl.pallas_call(lambda *refs: attend_kernel(sizes, joined, split, *refs),...]
  transfers between devices with their start and end apart: 0 -> 18, of which waited for: 0 -> 11; matrix products, arithmetic and copies ran while one was open for 0% -> 0% of each run, Pallas kernels for 0% -> 7%
where the time goes in v3:
time: 284 us; the launch traced here: 282 us
  waiting for transfers between devices  160 us (56%)
  starting transfers between devices  79 us (28%)
  Pallas kernels  30.8 us (11%)
  local copies, waits for them, and re-layouts  11.3 us (4%)
    ppermute x8, waiting for transfers between devices, z_out(): return [lax.ppermute(pieces[k], ('z', 'w'), pairs(k)) for k in range(zs)]  93.6 us
    ppermute x6, waiting for transfers between devices, z_in(): lax.ppermute(pieces[k], 'z', [(z, (z + k) % zs) for z in range(zs)])  66.3 us
    all_to_all x4, starting transfers between devices, across(): return lax.all_to_all(whole, names, 0, 0, tiled=True)  29.7 us
    ppermute x8, starting transfers between devices, z_out(): return [lax.ppermute(pieces[k], ('z', 'w'), pairs(k)) for k in range(zs)]  28.8 us
    ppermute x6, starting transfers between devices, z_in(): lax.ppermute(pieces[k], 'z', [(z, (z + k) % zs) for z in range(zs)])  20.5 us
    pallas_call x2, Pallas kernels, attend(): pl.pallas_call(lambda *refs: attend_kernel(sizes, joined, split, *refs),...  16.8 us
    unnamed x20, local copies, waits for them, and re-layouts  11.3 us
    pallas_call x1, Pallas kernels, unpack(): pl.pallas_call(lambda *refs: unpack_kernel(sizes, *refs), out_shape=[jax....  6.77 us
  transfers between devices with their start and end apart: 18, of which 11 were waited for; matrix products, arithmetic and copies ran while one was open for 0% of the time, Pallas kernels for 7%

profile of v3, /device:TPU:2, one launch (start us, length us, event | category | flops | bytes accessed | tf_op | source)
XLA Modules:
  0.0 281.9 jit_solution(12549079163667999009)
XLA Ops:
  0.7 1.2 copy-done.3
  5.6 3.7 %pack.3 = bf16[32,4,4,4,4,128]{5,4,3,2,1,0:T(4,128)(2,1)} custom-call(s32[2]{0:T(128)S(1)} %pad_add_fusion.refs_0_, bf16[4,4,64,4,128]{4,3,2,1,0:T(4,128)(2,1)S(1)} %bitcast.15, bf16[4,4,64,4,128]{4,3,2,1,0:T(4,128)(2,1)S(1)} %bitcast.17, bf16[4,4,64,4,128]{4,3,2,1,0:T(4,128)(2,1)S(1)} %bitcast.19, bf16[4,4,64,4,128]{4,3,2,1,0:T(4,128)(2,1)S(1)} %bitcast.22), custom_call_target="tpu_custom_call" | custom-call | tf_op jit(solution)/shard_map/pack/pallas_call | solution.py:81
  9.3 7.8 %all-to-all-start.2 = ((bf16[32,4,4,16,128]{4,3,2,1,0:T(8,128)(2,1)}), bf16[32,4,4,16,128]{4,3,2,1,0:T(8,128)(2,1)S(1)}, u32[]{:S(2)}, u32[]{:S(2)}) async-start(bf16[32,4,4,16,128]{4,3,2,1,0:T(8,128)(2,1)} %bitcast.27), calls=%async_computation.2 | async-start | bytes 4194304 | tf_op jit(solution)/shard_map/all_to_all | solution.py:292
  19.5 3.0 %pack.2 = (bf16[32,4,4,4,128]{4,3,2,1,0:T(4,128)(2,1)S(1)}, bf16[32,4,4,4,128]{4,3,2,1,0:T(4,128)(2,1)S(1)}, bf16[32,4,4,4,128]{4,3,2,1,0:T(4,128)(2,1)S(1)}, bf16[32,4,4,4,128]{4,3,2,1,0:T(4,128)(2,1)S(1)}) custom-call(s32[2]{0:T(128)S(1)} %pad_add_fusion.refs_0_, bf16[4,4,64,4,128]{4,3,2,1,0:T(4,128)(2,1)S(1)} %bitcast.16, ...), custom_call_target="tpu_custom_call" | custom-call | tf_op jit(solution)/shard_map/pack/pallas_call | solution.py:81
  22.6 2.0 collective-permute-start
  24.6 3.3 %collective-permute-start.1 = (bf16[32,4,16,128]{3,2,1,0:T(8,128)(2,1)S(1)}, bf16[32,4,16,128]{3,2,1,0:T(8,128)(2,1)S(1)}, u32[]{:S(2)}, u32[]{:S(2)}) collective-permute-start(bf16[32,4,16,128]{3,2,1,0:T(8,128)(2,1)S(1)} %bitcast.25), channel_id=1, source_target_pairs={{0,32},{16,48},{32,0},{48,16},{1,33},{17,49},{33,1},{49,17},{2,34}... | collective-permute-start | bytes 1572872 | tf_op jit(solution)/shard_map/ppermute | solution.py:263
  28.8 11.3 %collective-permute-done.refs_1_ = bf16[32,4,16,128]{3,2,1,0:T(8,128)(2,1)S(1)} collective-permute-done((bf16[32,4,16,128]{3,2,1,0:T(8,128)(2,1)S(1)}, bf16[32,4,16,128]{3,2,1,0:T(8,128)(2,1)S(1)}, u32[]{:S(2)}, u32[]{:S(2)}) %collective-permute-start) | collective-permute-done | bytes 524320 | tf_op jit(solution)/shard_map/ppermute | solution.py:263
  40.1 22.0 %collective-permute-done.1.refs_2_ = bf16[32,4,16,128]{3,2,1,0:T(8,128)(2,1)S(1)} collective-permute-done((bf16[32,4,16,128]{3,2,1,0:T(8,128)(2,1)S(1)}, bf16[32,4,16,128]{3,2,1,0:T(8,128)(2,1)S(1)}, u32[]{:S(2)}, u32[]{:S(2)}) %collective-permute-start.1) | collective-permute-done | bytes 524320 | tf_op jit(solution)/shard_map/ppermute | solution.py:263
  62.2 1.3 copy-done.2
  63.6 7.4 %all-to-all-start = ((bf16[32,4,4,16,128]{4,3,2,1,0:T(8,128)(2,1)}), bf16[32,4,4,16,128]{4,3,2,1,0:T(8,128)(2,1)}, u32[]{:S(2)}, u32[]{:S(2)}) async-start(bf16[32,4,4,16,128]{4,3,2,1,0:T(8,128)(2,1)} %copy-done.2), calls=%async_computation | async-start | bytes 4194304 | tf_op jit(solution)/shard_map/all_to_all | solution.py:292
  71.2 11.8 %collective-permute-start.7 = (bf16[32,4,16,128]{3,2,1,0:T(8,128)(2,1)S(1)}, bf16[32,4,16,128]{3,2,1,0:T(8,128)(2,1)S(1)}, u32[]{:S(2)}, u32[]{:S(2)}) collective-permute-start(bf16[32,4,16,128]{3,2,1,0:T(8,128)(2,1)S(1)} %get-tuple-element.33), channel_id=1, source_target_pairs={{0,16},{16,32},{32,48},{48,0},{1,17},{17,33},{33,49},{49,1},{2,18}... | collective-permute-start | bytes 1572872 | tf_op jit(solution)/shard_map/ppermute | solution.py:263
  83.0 1.2 collective-permute-start.8
  85.4 11.1 %collective-permute-done.7.refs_2_ = bf16[32,4,16,128]{3,2,1,0:T(8,128)(2,1)S(1)} collective-permute-done((bf16[32,4,16,128]{3,2,1,0:T(8,128)(2,1)S(1)}, bf16[32,4,16,128]{3,2,1,0:T(8,128)(2,1)S(1)}, u32[]{:S(2)}, u32[]{:S(2)}) %collective-permute-start.7) | collective-permute-done | bytes 524320 | tf_op jit(solution)/shard_map/ppermute | solution.py:263
  96.5 22.0 %collective-permute-done.8.refs_3_ = bf16[32,4,16,128]{3,2,1,0:T(8,128)(2,1)S(1)} collective-permute-done((bf16[32,4,16,128]{3,2,1,0:T(8,128)(2,1)S(1)}, bf16[32,4,16,128]{3,2,1,0:T(8,128)(2,1)S(1)}, u32[]{:S(2)}, u32[]{:S(2)}) %collective-permute-start.8) | collective-permute-done | bytes 524320 | tf_op jit(solution)/shard_map/ppermute | solution.py:263
  118.5 7.9 %attend.3 = bf16[16,4,4,32,128]{4,3,2,1,0:T(8,128)(2,1)S(1)} custom-call(s32[2]{0:T(128)S(1)} %pad_add_fusion.refs_0_, bf16[32,4,16,128]{3,2,1,0:T(8,128)(2,1)S(1)} %get-tuple-element.32.refs_1_, bf16[32,4,16,128]{3,2,1,0:T(8,128)(2,1)S(1)} %collective-permute-done.7.refs_2_, bf16[32,4,16,128]{3,2,1,0:T(8,128)(2,1)S(1)} %collective-permute-done.8.refs_3_, ...), custom_call_target="tpu_custom_call" | custom-call | flops 805306368 | bytes 4194304 | tf_op jit(solution)/shard_map/attend/pallas_call | solution.py:155
  126.4 1.3 copy-done
  127.7 7.2 %all-to-all-start.3 = ((bf16[16,4,4,32,128]{4,3,2,1,0:T(8,128)(2,1)}), bf16[16,4,4,32,128]{4,3,2,1,0:T(8,128)(2,1)S(1)}, u32[]{:S(2)}, u32[]{:S(2)}) async-start(bf16[16,4,4,32,128]{4,3,2,1,0:T(8,128)(2,1)} %copy-done), calls=%async_computation.3 | async-start | bytes 4194304 | tf_op jit(solution)/shard_map/all_to_all | solution.py:292
  134.9 8.9 %attend.2 = (bf16[16,4,32,128]{3,2,1,0:T(8,128)(2,1)S(1)}, bf16[16,4,32,128]{3,2,1,0:T(8,128)(2,1)S(1)}, bf16[16,4,32,128]{3,2,1,0:T(8,128)(2,1)S(1)}, bf16[16,4,32,128]{3,2,1,0:T(8,128)(2,1)S(1)}) custom-call(s32[2]{0:T(128)S(1)} %pad_add_fusion.refs_0_, bf16[32,4,4,16,128]{4,3,2,1,0:T(8,128)(2,1)} %all-to-all-done.refs_1_), custom_call_target="tpu_custom_call" | custom-call | flops 805306368 | bytes 4194304 | tf_op jit(solution)/shard_map/attend/pallas_call | solution.py:155
  143.8 7.3 %collective-permute-start.3 = (bf16[16,4,32,128]{3,2,1,0:T(8,128)(2,1)S(1)}, bf16[16,4,32,128]{3,2,1,0:T(8,128)(2,1)S(1)}, u32[]{:S(2)}, u32[]{:S(2)}) collective-permute-start(bf16[16,4,32,128]{3,2,1,0:T(8,128)(2,1)S(1)} %get-tuple-element.28), channel_id=1, source_target_pairs={{0,2},{2,0},{16,16},{18,18},{32,32},{34,34},{48,50},{50,48},{1,3},... | collective-permute-start | bytes 1572872 | tf_op jit(solution)/shard_map/ppermute | solution.py:276
  151.1 9.1 %collective-permute-start.4 = (bf16[16,4,32,128]{3,2,1,0:T(8,128)(2,1)S(1)}, bf16[16,4,32,128]{3,2,1,0:T(8,128)(2,1)S(1)}, u32[]{:S(2)}, u32[]{:S(2)}) collective-permute-start(bf16[16,4,32,128]{3,2,1,0:T(8,128)(2,1)S(1)} %get-tuple-element.29), channel_id=1, source_target_pairs={{0,18},{2,16},{16,32},{18,34},{32,48},{34,50},{48,2},{50,0},{1,19}... | collective-permute-start | bytes 1572872 | tf_op jit(solution)/shard_map/ppermute | solution.py:276
  160.2 2.5 collective-permute-start.5
  163.0 15.1 %collective-permute-done.4.refs_1_ = bf16[16,4,32,128]{3,2,1,0:T(8,128)(2,1)S(1)} collective-permute-done((bf16[16,4,32,128]{3,2,1,0:T(8,128)(2,1)S(1)}, bf16[16,4,32,128]{3,2,1,0:T(8,128)(2,1)S(1)}, u32[]{:S(2)}, u32[]{:S(2)}) %collective-permute-start.4) | collective-permute-done | bytes 524320 | tf_op jit(solution)/shard_map/ppermute | solution.py:276
  178.2 17.2 %collective-permute-done.5.refs_2_ = bf16[16,4,32,128]{3,2,1,0:T(8,128)(2,1)S(1)} collective-permute-done((bf16[16,4,32,128]{3,2,1,0:T(8,128)(2,1)S(1)}, bf16[16,4,32,128]{3,2,1,0:T(8,128)(2,1)S(1)}, u32[]{:S(2)}, u32[]{:S(2)}) %collective-permute-start.5) | collective-permute-done | bytes 524320 | tf_op jit(solution)/shard_map/ppermute | solution.py:276
  195.4 9.6 %collective-permute-done.6.refs_3_ = bf16[16,4,32,128]{3,2,1,0:T(8,128)(2,1)S(1)} collective-permute-done((bf16[16,4,32,128]{3,2,1,0:T(8,128)(2,1)S(1)}, bf16[16,4,32,128]{3,2,1,0:T(8,128)(2,1)S(1)}, u32[]{:S(2)}, u32[]{:S(2)}) %collective-permute-start.6) | collective-permute-done | bytes 524320 | tf_op jit(solution)/shard_map/ppermute | solution.py:276
  205.2 1.3 copy-done.1
  206.5 7.3 %all-to-all-start.1 = ((bf16[16,4,4,32,128]{4,3,2,1,0:T(8,128)(2,1)}), bf16[16,4,4,32,128]{4,3,2,1,0:T(8,128)(2,1)}, u32[]{:S(2)}, u32[]{:S(2)}) async-start(bf16[16,4,4,32,128]{4,3,2,1,0:T(8,128)(2,1)} %copy-done.1), calls=%async_computation.1 | async-start | bytes 4194304 | tf_op jit(solution)/shard_map/all_to_all | solution.py:292
  214.6 6.2 %collective-permute-start.11 = (bf16[16,4,32,128]{3,2,1,0:T(8,128)(2,1)S(1)}, bf16[16,4,32,128]{3,2,1,0:T(8,128)(2,1)S(1)}, u32[]{:S(2)}, u32[]{:S(2)}) collective-permute-start(bf16[16,4,32,128]{3,2,1,0:T(8,128)(2,1)S(1)} %get-tuple-element.37), channel_id=1, source_target_pairs={{0,16},{2,18},{16,34},{18,32},{32,50},{34,48},{48,0},{50,2},{1,17}... | collective-permute-start | bytes 1572872 | tf_op jit(solution)/shard_map/ppermute | solution.py:276
  220.9 2.9 %collective-permute-start.13 = (bf16[16,4,32,128]{3,2,1,0:T(8,128)(2,1)S(1)}, bf16[16,4,32,128]{3,2,1,0:T(8,128)(2,1)S(1)}, u32[]{:S(2)}, u32[]{:S(2)}) collective-permute-start(bf16[16,4,32,128]{3,2,1,0:T(8,128)(2,1)S(1)} %get-tuple-element.39), channel_id=1, source_target_pairs={{0,48},{2,50},{16,2},{18,0},{32,18},{34,16},{48,32},{50,34},{1,49}... | collective-permute-start | bytes 1572872 | tf_op jit(solution)/shard_map/ppermute | solution.py:276
  223.8 21.2 %collective-permute-done.11.refs_3_ = bf16[16,4,32,128]{3,2,1,0:T(8,128)(2,1)S(1)} collective-permute-done((bf16[16,4,32,128]{3,2,1,0:T(8,128)(2,1)S(1)}, bf16[16,4,32,128]{3,2,1,0:T(8,128)(2,1)S(1)}, u32[]{:S(2)}, u32[]{:S(2)}) %collective-permute-start.11) | collective-permute-done | bytes 524320 | tf_op jit(solution)/shard_map/ppermute | solution.py:276
  245.0 10.3 %collective-permute-done.12.refs_4_ = bf16[16,4,32,128]{3,2,1,0:T(8,128)(2,1)S(1)} collective-permute-done((bf16[16,4,32,128]{3,2,1,0:T(8,128)(2,1)S(1)}, bf16[16,4,32,128]{3,2,1,0:T(8,128)(2,1)S(1)}, u32[]{:S(2)}, u32[]{:S(2)}) %collective-permute-start.12) | collective-permute-done | bytes 524320 | tf_op jit(solution)/shard_map/ppermute | solution.py:276
  255.2 19.9 %collective-permute-done.13.refs_5_ = bf16[16,4,32,128]{3,2,1,0:T(8,128)(2,1)S(1)} collective-permute-done((bf16[16,4,32,128]{3,2,1,0:T(8,128)(2,1)S(1)}, bf16[16,4,32,128]{3,2,1,0:T(8,128)(2,1)S(1)}, u32[]{:S(2)}, u32[]{:S(2)}) %collective-permute-start.13) | collective-permute-done | bytes 524320 | tf_op jit(solution)/shard_map/ppermute | solution.py:276
  275.1 6.8 %unpack.1 = (bf16[4,1024,128]{2,1,0:T(8,128)(2,1)}, bf16[4,1024,128]{2,1,0:T(8,128)(2,1)}, bf16[4,1024,128]{2,1,0:T(8,128)(2,1)}, bf16[4,1024,128]{2,1,0:T(8,128)(2,1)}) custom-call(s32[2]{0:T(128)S(1)} %pad_add_fusion.refs_0_, bf16[16,4,4,32,128]{4,3,2,1,0:T(8,128)(2,1)} %all-to-all-done.1.refs_1_, ...), custom_call_target="tpu_custom_call" | custom-call | tf_op jit(solution)/shard_map/unpack/pallas_call | solution.py:247
  (34 shorter events, 10.0 us)
Async XLA Ops:
  0.7 1.2 copy-start.3
  1.9 1.2 copy-start.5
  3.2 1.2 copy-start.7
  4.4 1.2 copy-start.9
  9.3 7.8 %copy-start.4 = (bf16[4,1024,1,128]{3,1,2,0:T(8,128)(2,1)S(1)}, bf16[4,1024,1,128]{3,1,2,0:T(8,128)(2,1)}, u32[]{:S(2)}) copy-start(bf16[4,1024,1,128]{3,1,2,0:T(8,128)(2,1)} %param.4) | copy-start | bytes 3145732
  9.3 54.3 %all-to-all-start.2 = ((bf16[32,4,4,16,128]{4,3,2,1,0:T(8,128)(2,1)}), bf16[32,4,4,16,128]{4,3,2,1,0:T(8,128)(2,1)S(1)}, u32[]{:S(2)}, u32[]{:S(2)}) async-start(bf16[32,4,4,16,128]{4,3,2,1,0:T(8,128)(2,1)} %bitcast.27), calls=%async_computation.2 | async-start | bytes 4194304 | tf_op jit(solution)/shard_map/all_to_all | solution.py:292
  17.1 1.2 copy-start.6
  18.3 1.2 copy-start.8
  22.6 17.6 %collective-permute-start = (bf16[32,4,16,128]{3,2,1,0:T(8,128)(2,1)S(1)}, bf16[32,4,16,128]{3,2,1,0:T(8,128)(2,1)S(1)}, u32[]{:S(2)}, u32[]{:S(2)}) collective-permute-start(bf16[32,4,16,128]{3,2,1,0:T(8,128)(2,1)S(1)} %bitcast.26), channel_id=1, source_target_pairs={{0,16},{16,32},{32,48},{48,0},{1,17},{17,33},{33,49},{49,1},{2,18}... | collective-permute-start | bytes 1572872 | tf_op jit(solution)/shard_map/ppermute | solution.py:263
  24.6 37.5 %collective-permute-start.1 = (bf16[32,4,16,128]{3,2,1,0:T(8,128)(2,1)S(1)}, bf16[32,4,16,128]{3,2,1,0:T(8,128)(2,1)S(1)}, u32[]{:S(2)}, u32[]{:S(2)}) collective-permute-start(bf16[32,4,16,128]{3,2,1,0:T(8,128)(2,1)S(1)} %bitcast.25), channel_id=1, source_target_pairs={{0,32},{16,48},{32,0},{48,16},{1,33},{17,49},{33,1},{49,17},{2,34}... | collective-permute-start | bytes 1572872 | tf_op jit(solution)/shard_map/ppermute | solution.py:263
  27.8 34.3 %collective-permute-start.2 = (bf16[32,4,16,128]{3,2,1,0:T(8,128)(2,1)S(1)}, bf16[32,4,16,128]{3,2,1,0:T(8,128)(2,1)S(1)}, u32[]{:S(2)}, u32[]{:S(2)}) collective-permute-start(bf16[32,4,16,128]{3,2,1,0:T(8,128)(2,1)S(1)} %bitcast.24), channel_id=1, source_target_pairs={{0,48},{16,0},{32,16},{48,32},{1,49},{17,1},{33,17},{49,33},{2,50}... | collective-permute-start | bytes 1572872 | tf_op jit(solution)/shard_map/ppermute | solution.py:263
  62.2 1.3 copy-start.2
  63.6 64.1 %all-to-all-start = ((bf16[32,4,4,16,128]{4,3,2,1,0:T(8,128)(2,1)}), bf16[32,4,4,16,128]{4,3,2,1,0:T(8,128)(2,1)}, u32[]{:S(2)}, u32[]{:S(2)}) async-start(bf16[32,4,4,16,128]{4,3,2,1,0:T(8,128)(2,1)} %copy-done.2), calls=%async_computation | async-start | bytes 4194304 | tf_op jit(solution)/shard_map/all_to_all | solution.py:292
  71.2 25.3 %collective-permute-start.7 = (bf16[32,4,16,128]{3,2,1,0:T(8,128)(2,1)S(1)}, bf16[32,4,16,128]{3,2,1,0:T(8,128)(2,1)S(1)}, u32[]{:S(2)}, u32[]{:S(2)}) collective-permute-start(bf16[32,4,16,128]{3,2,1,0:T(8,128)(2,1)S(1)} %get-tuple-element.33), channel_id=1, source_target_pairs={{0,16},{16,32},{32,48},{48,0},{1,17},{17,33},{33,49},{49,1},{2,18}... | collective-permute-start | bytes 1572872 | tf_op jit(solution)/shard_map/ppermute | solution.py:263
  83.0 35.5 %collective-permute-start.8 = (bf16[32,4,16,128]{3,2,1,0:T(8,128)(2,1)S(1)}, bf16[32,4,16,128]{3,2,1,0:T(8,128)(2,1)S(1)}, u32[]{:S(2)}, u32[]{:S(2)}) collective-permute-start(bf16[32,4,16,128]{3,2,1,0:T(8,128)(2,1)S(1)} %get-tuple-element.34), channel_id=1, source_target_pairs={{0,32},{16,48},{32,0},{48,16},{1,33},{17,49},{33,1},{49,17},{2,34}... | collective-permute-start | bytes 1572872 | tf_op jit(solution)/shard_map/ppermute | solution.py:263
  84.2 34.3 %collective-permute-start.9 = (bf16[32,4,16,128]{3,2,1,0:T(8,128)(2,1)S(1)}, bf16[32,4,16,128]{3,2,1,0:T(8,128)(2,1)S(1)}, u32[]{:S(2)}, u32[]{:S(2)}) collective-permute-start(bf16[32,4,16,128]{3,2,1,0:T(8,128)(2,1)S(1)} %get-tuple-element.35), channel_id=1, source_target_pairs={{0,48},{16,0},{32,16},{48,32},{1,49},{17,1},{33,17},{49,33},{2,50}... | collective-permute-start | bytes 1572872 | tf_op jit(solution)/shard_map/ppermute | solution.py:263
  126.4 1.3 copy-start
  127.7 78.8 %all-to-all-start.3 = ((bf16[16,4,4,32,128]{4,3,2,1,0:T(8,128)(2,1)}), bf16[16,4,4,32,128]{4,3,2,1,0:T(8,128)(2,1)S(1)}, u32[]{:S(2)}, u32[]{:S(2)}) async-start(bf16[16,4,4,32,128]{4,3,2,1,0:T(8,128)(2,1)} %copy-done), calls=%async_computation.3 | async-start | bytes 4194304 | tf_op jit(solution)/shard_map/all_to_all | solution.py:292
  143.8 19.2 %collective-permute-start.3 = (bf16[16,4,32,128]{3,2,1,0:T(8,128)(2,1)S(1)}, bf16[16,4,32,128]{3,2,1,0:T(8,128)(2,1)S(1)}, u32[]{:S(2)}, u32[]{:S(2)}) collective-permute-start(bf16[16,4,32,128]{3,2,1,0:T(8,128)(2,1)S(1)} %get-tuple-element.28), channel_id=1, source_target_pairs={{0,2},{2,0},{16,16},{18,18},{32,32},{34,34},{48,50},{50,48},{1,3},... | collective-permute-start | bytes 1572872 | tf_op jit(solution)/shard_map/ppermute | solution.py:276
  151.1 27.0 %collective-permute-start.4 = (bf16[16,4,32,128]{3,2,1,0:T(8,128)(2,1)S(1)}, bf16[16,4,32,128]{3,2,1,0:T(8,128)(2,1)S(1)}, u32[]{:S(2)}, u32[]{:S(2)}) collective-permute-start(bf16[16,4,32,128]{3,2,1,0:T(8,128)(2,1)S(1)} %get-tuple-element.29), channel_id=1, source_target_pairs={{0,18},{2,16},{16,32},{18,34},{32,48},{34,50},{48,2},{50,0},{1,19}... | collective-permute-start | bytes 1572872 | tf_op jit(solution)/shard_map/ppermute | solution.py:276
  160.2 35.2 %collective-permute-start.5 = (bf16[16,4,32,128]{3,2,1,0:T(8,128)(2,1)S(1)}, bf16[16,4,32,128]{3,2,1,0:T(8,128)(2,1)S(1)}, u32[]{:S(2)}, u32[]{:S(2)}) collective-permute-start(bf16[16,4,32,128]{3,2,1,0:T(8,128)(2,1)S(1)} %get-tuple-element.30), channel_id=1, source_target_pairs={{0,34},{2,32},{16,48},{18,50},{32,0},{34,2},{48,18},{50,16},{1,35}... | collective-permute-start | bytes 1572872 | tf_op jit(solution)/shard_map/ppermute | solution.py:276
  162.8 42.3 %collective-permute-start.6 = (bf16[16,4,32,128]{3,2,1,0:T(8,128)(2,1)S(1)}, bf16[16,4,32,128]{3,2,1,0:T(8,128)(2,1)S(1)}, u32[]{:S(2)}, u32[]{:S(2)}) collective-permute-start(bf16[16,4,32,128]{3,2,1,0:T(8,128)(2,1)S(1)} %get-tuple-element.31), channel_id=1, source_target_pairs={{0,50},{2,48},{16,0},{18,2},{32,16},{34,18},{48,34},{50,32},{1,51}... | collective-permute-start | bytes 1572872 | tf_op jit(solution)/shard_map/ppermute | solution.py:276
  205.2 1.3 copy-start.1
  206.5 68.6 %all-to-all-start.1 = ((bf16[16,4,4,32,128]{4,3,2,1,0:T(8,128)(2,1)}), bf16[16,4,4,32,128]{4,3,2,1,0:T(8,128)(2,1)}, u32[]{:S(2)}, u32[]{:S(2)}) async-start(bf16[16,4,4,32,128]{4,3,2,1,0:T(8,128)(2,1)} %copy-done.1), calls=%async_computation.1 | async-start | bytes 4194304 | tf_op jit(solution)/shard_map/all_to_all | solution.py:292
  213.9 9.9 %collective-permute-start.10 = (bf16[16,4,32,128]{3,2,1,0:T(8,128)(2,1)S(1)}, bf16[16,4,32,128]{3,2,1,0:T(8,128)(2,1)S(1)}, u32[]{:S(2)}, u32[]{:S(2)}) collective-permute-start(bf16[16,4,32,128]{3,2,1,0:T(8,128)(2,1)S(1)} %get-tuple-element.36), channel_id=1, source_target_pairs={{0,0},{2,2},{16,18},{18,16},{32,34},{34,32},{48,48},{50,50},{1,1},... | collective-permute-start | bytes 1572872 | tf_op jit(solution)/shard_map/ppermute | solution.py:276
  214.6 30.4 %collective-permute-start.11 = (bf16[16,4,32,128]{3,2,1,0:T(8,128)(2,1)S(1)}, bf16[16,4,32,128]{3,2,1,0:T(8,128)(2,1)S(1)}, u32[]{:S(2)}, u32[]{:S(2)}) collective-permute-start(bf16[16,4,32,128]{3,2,1,0:T(8,128)(2,1)S(1)} %get-tuple-element.37), channel_id=1, source_target_pairs={{0,16},{2,18},{16,34},{18,32},{32,50},{34,48},{48,0},{50,2},{1,17}... | collective-permute-start | bytes 1572872 | tf_op jit(solution)/shard_map/ppermute | solution.py:276
  220.9 34.4 %collective-permute-start.12 = (bf16[16,4,32,128]{3,2,1,0:T(8,128)(2,1)S(1)}, bf16[16,4,32,128]{3,2,1,0:T(8,128)(2,1)S(1)}, u32[]{:S(2)}, u32[]{:S(2)}) collective-permute-start(bf16[16,4,32,128]{3,2,1,0:T(8,128)(2,1)S(1)} %get-tuple-element.38), channel_id=1, source_target_pairs={{0,32},{2,34},{16,50},{18,48},{32,2},{34,0},{48,16},{50,18},{1,33}... | collective-permute-start | bytes 1572872 | tf_op jit(solution)/shard_map/ppermute | solution.py:276
  220.9 54.3 %collective-permute-start.13 = (bf16[16,4,32,128]{3,2,1,0:T(8,128)(2,1)S(1)}, bf16[16,4,32,128]{3,2,1,0:T(8,128)(2,1)S(1)}, u32[]{:S(2)}, u32[]{:S(2)}) collective-permute-start(bf16[16,4,32,128]{3,2,1,0:T(8,128)(2,1)S(1)} %get-tuple-element.39), channel_id=1, source_target_pairs={{0,48},{2,50},{16,2},{18,0},{32,18},{34,16},{48,32},{50,34},{1,49}... | collective-permute-start | bytes 1572872 | tf_op jit(solution)/shard_map/ppermute | solution.py:276

commit v4 on v2

v4 whole, which is shorter than its diff:
```python
import jax
import jax.numpy as jnp
from jax import lax
from jax.experimental import pallas as pl
from jax.experimental.pallas import tpu as pltpu
from jax.sharding import PartitionSpec as P

NAMES = ("row", "head")
LAST = (((1,), (1,)), ((), ()))
FIRST = (((0,), (0,)), ((), ()))
F32 = jnp.float32
BF16 = jnp.bfloat16
LIMIT = 48 * 2**20
ALL = 58 * 2**20
LOG2E = 1.4426950408889634
FAR = pl.BlockSpec(memory_space=pltpu.HBM)
WHOLE = pl.BlockSpec(memory_space=pltpu.VMEM)


def dot(a, b, dims):
    return lax.dot_general(a, b, dims, preferred_element_type=F32)


def attend_column(query, key, value, cotangent):
    half = query.shape[0] // 2
    scale = query.shape[-1] ** (-0.5)
    causal = lax.broadcasted_iota(jnp.int32, (half, half), 0) <= lax.broadcasted_iota(
        jnp.int32, (half, half), 1
    )
    lows, grads = [], []
    for at in range(2):
        mine, keys = slice(at * half, (at + 1) * half), slice(0, (at + 1) * half)
        scores = dot(key[keys], query[mine], LAST) * (scale * LOG2E)
        grad_weights = dot(value[keys], cotangent[mine], LAST)
        diagonal = jnp.where(causal, scores[mine], -jnp.inf)
        scores = jnp.concatenate([scores[:half], diagonal], 0) if at else diagonal
        raw = jnp.exp2(scores - jnp.max(scores, axis=0, keepdims=True))
        weights = raw * (1.0 / jnp.sum(raw, axis=0, keepdims=True))
        dots = jnp.sum(weights * grad_weights, axis=0, keepdims=True)
        lows.append(weights.astype(BF16))
        grads.append(((grad_weights - dots) * (weights * scale)).astype(BF16))

    def to_queries(parts, other):
        return jnp.concatenate(
            [dot(parts[0], other[:half], FIRST), dot(parts[1], other, FIRST)], axis=0
        )

    def to_keys(parts, other):
        upper = jnp.concatenate([parts[0], jnp.zeros((half, half), BF16)], axis=0)
        both = jnp.concatenate([upper, parts[1]], axis=1)
        return jnp.dot(both, other, preferred_element_type=F32)

    return (
        to_queries(lows, value),
        to_queries(grads, key),
        to_keys(grads, query),
        to_keys(lows, cotangent),
    )


def pack_kernel(*refs):
    *far_refs, out_ref, held, sems = refs
    rows, parts, owners, _, _ = far_refs[0].shape
    copies = [
        [
            pltpu.make_async_copy(ref.at[row], held.at[array, row], sems.at[array, row])
            for array, ref in enumerate(far_refs)
        ]
        for row in range(rows)
    ]
    for some in copies:
        for copy in some:
            copy.start()
    for row in range(rows):
        for copy in copies[row]:
            copy.wait()

        def step(owner, carry, row=row):
            for array in range(len(far_refs)):
                for part in range(parts):
                    out_ref[owner, array, row, part] = held[array, row, part, owner]
            return carry

        lax.fori_loop(0, owners, step, 0, unroll=2)


def pack(arrays):
    row, part, owner, inner, feature = arrays[0].shape
    count = len(arrays)
    return pl.pallas_call(
        pack_kernel,
        out_shape=jax.ShapeDtypeStruct((owner, count, row, part, inner, feature), BF16),
        in_specs=[FAR] * count,
        out_specs=WHOLE,
        scratch_shapes=[
            pltpu.VMEM((count, *arrays[0].shape), BF16),
            pltpu.SemaphoreType.DMA((count, row)),
        ],
        compiler_params=pltpu.CompilerParams(vmem_limit_bytes=ALL),
        name="pack",
    )(*arrays)


def attend_kernel(together, in_ref, out_ref, wide_in, wide_out):
    sources, arrays, row, columns, feature = in_ref.shape
    owners, parts, _, tile, _ = out_ref.shape
    inner = tile // row
    rows = sources * row

    def widen(source, carry):
        for array in range(arrays):
            block = in_ref[source, array].reshape(row * columns, feature)
            start = pl.multiple_of(source * row * columns, row * columns)
            wide_in[array, pl.ds(start, row * columns), :] = block.astype(F32)
        return carry

    lax.fori_loop(0, sources, widen, 0, unroll=2)

    def step(at, carry):
        for place in range(together):
            column = at * together + place
            block = [
                wide_in[array, pl.ds(column, rows, stride=columns), :].astype(BF16)
                for array in range(arrays)
            ]
            start = (column // inner) * rows * inner + column % inner
            for array, result in enumerate(attend_column(*block)):
                wide_out[array, pl.ds(start, rows, stride=inner), :] = result
        return carry

    lax.fori_loop(0, columns // together, step, 0)

    def narrow(owner, carry):
        for array in range(arrays):
            for part in range(parts):
                start = pl.multiple_of(part * rows * inner + owner * tile, tile)
                out_ref[owner, part, array] = wide_out[array, pl.ds(start, tile), :].astype(BF16)
        return carry

    lax.fori_loop(0, owners, narrow, 0, unroll=2)


def attend(arrived, parts, together=4):
    sources, arrays, row, columns, feature = arrived.shape
    rows = sources * row
    return pl.pallas_call(
        lambda *refs: attend_kernel(together, *refs),
        out_shape=jax.ShapeDtypeStruct(
            (sources, parts, arrays, row * columns // parts, feature), BF16
        ),
        in_specs=[WHOLE],
        out_specs=WHOLE,
        scratch_shapes=[pltpu.VMEM((arrays, rows * columns, feature), F32)] * 2,
        compiler_params=pltpu.CompilerParams(vmem_limit_bytes=LIMIT),
        cost_estimate=pl.CostEstimate(
            flops=12 * columns * rows * rows * feature,
            bytes_accessed=4 * arrived.size,
            transcendentals=columns * rows * rows,
        ),
        name="attend",
    )(arrived)


def unpack_kernel(rows, in_ref, *refs):
    *out_refs, wide = refs
    sources, heads, arrays, tile, feature = in_ref.shape
    size = tile // rows * heads

    def step(source, carry):
        for array in range(arrays):
            base = array * tile * heads
            for head in range(heads):
                block = in_ref[source, head, array].astype(F32)
                wide[pl.ds(base + head, tile, stride=heads), :] = block
            for row in range(rows):
                to = pl.multiple_of(source * size, size)
                block = wide[pl.ds(base + row * size, size), :].astype(BF16)
                out_refs[array][row, pl.ds(to, size), :] = block
        return carry

    lax.fori_loop(0, sources, step, 0)


def unpack(returned, rows, steps=4):
    sources, heads, arrays, tile, feature = returned.shape
    width = sources * tile // rows * heads
    return pl.pallas_call(
        lambda *refs: unpack_kernel(rows, *refs),
        out_shape=[jax.ShapeDtypeStruct((rows, width, feature), BF16)] * arrays,
        grid=(steps,),
        in_specs=[
            pl.BlockSpec((sources // steps, heads, arrays, tile, feature), lambda i: (i, 0, 0, 0, 0))
        ],
        out_specs=[pl.BlockSpec((rows, width // steps, feature), lambda i: (0, i, 0))] * arrays,
        scratch_shapes=[pltpu.VMEM((arrays * tile * heads, feature), F32)],
        compiler_params=pltpu.CompilerParams(vmem_limit_bytes=LIMIT),
        name="unpack",
    )(returned)


def shards(*arrays):
    row_devs = lax.axis_size("row")
    head_devs = lax.axis_size("head")
    rows, columns, _, features = arrays[0].shape
    inner = columns // (row_devs * head_devs)
    count = len(arrays)

    packed = pack([a.reshape(rows, head_devs, row_devs, inner, features) for a in arrays])
    packed = packed.reshape(row_devs, count, rows, head_devs * inner, features)
    arrived = lax.all_to_all(packed, "row", 0, 0, tiled=True)
    results = attend(arrived, head_devs)
    results = results.reshape(row_devs * head_devs, count, rows * inner, features)
    returned = lax.all_to_all(results, NAMES, 0, 0, tiled=True)
    returned = returned.reshape(row_devs, head_devs, count, rows * inner, features)
    outs = unpack(returned, rows)
    return tuple(out.reshape(rows, columns // head_devs, head_devs, features) for out in outs)


def solution(mesh):
    spec_in = P("row", None, "head", None)
    spec_out = P("row", "head", None, None)
    return jax.shard_map(
        shards, mesh=mesh, in_specs=(spec_in,) * 4, out_specs=(spec_out,) * 4, check_vma=False
    )
```

time: 248 us -> 236 us (0.952)
  Pallas kernels: 28.3 us -> 20.7 us
  local copies, waits for them, and re-layouts: 4.89 us -> 0 us
    pallas_call x2, Pallas kernels: 24 us -> 15.6 us  [the longest x1 12.6 us: attend(): pl.pallas_call(lambda *refs: attend_kernel(together, *refs), out_shape=ja...]
    unnamed x8 -> x0, local copies, waits for them, and re-layouts: 4.89 us -> none
where the time goes in v4:
time: 236 us; the launch traced here: 233 us
  blocking collectives  212 us (90%)
  Pallas kernels  20.7 us (9%)
    all_to_all x1, blocking collectives, shards(): arrived = lax.all_to_all(packed, 'row', 0, 0, tiled=True)  108 us
    all_to_all x1, blocking collectives, shards(): returned = lax.all_to_all(results, NAMES, 0, 0, tiled=True)  104 us
    pallas_call x1, Pallas kernels, attend(): pl.pallas_call(lambda *refs: attend_kernel(together, *refs), out_shape=ja...  12.6 us
    pallas_call x1, Pallas kernels, pack(): pl.pallas_call(pack_kernel, out_shape=jax.ShapeDtypeStruct((owner, count,...  5.11 us

profile of v4, /device:TPU:2, one launch (start us, length us, event | category | flops | bytes accessed | tf_op | source)
XLA Modules:
  0.0 233.1 jit_solution(12419429390076107116)
XLA Ops:
  0.6 5.1 %pack.1 = bf16[64,4,4,4,4,128]{5,4,3,2,1,0:T(4,128)(2,1)} custom-call(bf16[4,4,64,4,128]{4,3,2,1,0:T(4,128)(2,1)} %bitcast.14, bf16[4,4,64,4,128]{4,3,2,1,0:T(4,128)(2,1)} %bitcast.15, bf16[4,4,64,4,128]{4,3,2,1,0:T(4,128)(2,1)} %bitcast.16, bf16[4,4,64,4,128]{4,3,2,1,0:T(4,128)(2,1)} %bitcast.17), custom_call_target="tpu_custom_call" | custom-call | tf_op jit(solution)/shard_map/pack/pallas_call | solution.py:90
  5.7 107.6 %all_to_all.10.refs_0_ = bf16[64,4,4,16,128]{4,3,2,1,0:T(8,128)(2,1)} all-to-all(bf16[64,4,4,16,128]{4,3,2,1,0:T(8,128)(2,1)} %bitcast.13), channel_id=1, replica_groups=mesh['row'=64,'head'=4] {'row'}, dimensions={0} | all-to-all | bytes 8388608 | tf_op jit(solution)/shard_map/all_to_all | solution.py:210
  113.4 12.6 %attend.1 = bf16[64,4,4,16,128]{4,3,2,1,0:T(8,128)(2,1)S(1)} custom-call(bf16[64,4,4,16,128]{4,3,2,1,0:T(8,128)(2,1)} %all_to_all.10.refs_0_), custom_call_target="tpu_custom_call" | custom-call | flops 1610612736 | bytes 8388608 | tf_op jit(solution)/shard_map/attend/pallas_call | solution.py:146
  126.0 104.1 %all_to_all.11 = bf16[256,4,16,128]{3,2,1,0:T(8,128)(2,1)S(1)} all-to-all(bf16[256,4,16,128]{3,2,1,0:T(8,128)(2,1)S(1)} %bitcast.12), channel_id=1, replica_groups=mesh['row'=64,'head'=4] {'row','head'}, dimensions={0} | all-to-all | bytes 8388608 | tf_op jit(solution)/shard_map/all_to_all | solution.py:213
  230.2 3.0 %unpack.1 = (bf16[4,1024,128]{2,1,0:T(8,128)(2,1)}, bf16[4,1024,128]{2,1,0:T(8,128)(2,1)}, bf16[4,1024,128]{2,1,0:T(8,128)(2,1)}, bf16[4,1024,128]{2,1,0:T(8,128)(2,1)}) custom-call(bf16[64,4,4,16,128]{4,3,2,1,0:T(8,128)(2,1)S(1)} %bitcast.11), custom_call_target="tpu_custom_call" | custom-call | tf_op jit(solution)/shard_map/unpack/pallas_call | solution.py:187

commit v5 on v4

v5 whole, which is shorter than its diff:
```python
import functools

import jax
import jax.numpy as jnp
from jax import lax
from jax.experimental import pallas as pl
from jax.experimental.pallas import tpu as pltpu
from jax.sharding import Mesh, PartitionSpec as P

FINE = ("y", "z1", "z0", "x", "w", "core")
SIZES = (4, 2, 2, 4, 2, 2)
NEAR = ("y", "x", "core")
LAST = (((1,), (1,)), ((), ()))
FIRST = (((0,), (0,)), ((), ()))
F32 = jnp.float32
BF16 = jnp.bfloat16
LIMIT = 24 * 2**20
ALL = 58 * 2**20
LOG2E = 1.4426950408889634
ANY = pl.BlockSpec(memory_space=pl.ANY)
FAR = pl.BlockSpec(memory_space=pltpu.HBM)
WHOLE = pl.BlockSpec(memory_space=pltpu.VMEM)
SCALARS = pl.BlockSpec(memory_space=pltpu.SMEM)
ZS = 4


def other_run(w, chunk, z):
    return (w + chunk + jnp.where((z == 0) | (z == ZS - 1), 1, 0)) % 2


def dot(a, b, dims):
    return lax.dot_general(a, b, dims, preferred_element_type=F32)


def attend_column(query, key, value, cotangent):
    half = query.shape[0] // 2
    scale = query.shape[-1] ** (-0.5)
    causal = lax.broadcasted_iota(jnp.int32, (half, half), 0) <= lax.broadcasted_iota(
        jnp.int32, (half, half), 1
    )
    lows, grads = [], []
    for at in range(2):
        mine, keys = slice(at * half, (at + 1) * half), slice(0, (at + 1) * half)
        scores = dot(key[keys], query[mine], LAST) * (scale * LOG2E)
        grad_weights = dot(value[keys], cotangent[mine], LAST)
        diagonal = jnp.where(causal, scores[mine], -jnp.inf)
        scores = jnp.concatenate([scores[:half], diagonal], 0) if at else diagonal
        raw = jnp.exp2(scores - jnp.max(scores, axis=0, keepdims=True))
        weights = raw * (1.0 / jnp.sum(raw, axis=0, keepdims=True))
        dots = jnp.sum(weights * grad_weights, axis=0, keepdims=True)
        lows.append(weights.astype(BF16))
        grads.append(((grad_weights - dots) * (weights * scale)).astype(BF16))

    def to_queries(parts, other):
        return jnp.concatenate(
            [dot(parts[0], other[:half], FIRST), dot(parts[1], other, FIRST)], axis=0
        )

    def to_keys(parts, other):
        upper = jnp.concatenate([parts[0], jnp.zeros((half, half), BF16)], axis=0)
        both = jnp.concatenate([upper, parts[1]], axis=1)
        return jnp.dot(both, other, preferred_element_type=F32)

    return (
        to_queries(lows, value),
        to_queries(grads, key),
        to_keys(grads, query),
        to_keys(lows, cotangent),
    )


def pack_kernel(sizes, chunk, split, place_ref, *refs):
    ys, _, z0s, xs, _, cores = sizes
    *refs, held, sems = refs
    far_refs, out_refs = refs[:4], refs[4 + (not split) :]
    rows = far_refs[0].shape[0]
    my_z, my_w = place_ref[0] * z0s + place_ref[1], place_ref[2]
    copies = []
    for shift in range(ZS):
        z = (my_z + shift) % ZS
        quarter = other_run(my_w, chunk, z) * cores
        for array, ref in enumerate(far_refs):
            copy = pltpu.make_async_copy(
                ref.at[:, pl.ds(quarter, cores), :, z],
                held.at[shift, array],
                sems.at[shift, array],
            )
            copy.start()
            copies.append(copy)
    for shift in range(ZS):
        for copy in copies[shift * 4 : shift * 4 + 4]:
            copy.wait()

        def step(y, carry, shift=shift):
            for x in range(xs):
                for core in range(cores):
                    for array in range(4):
                        for row in range(rows):
                            tile = held[shift, array, row, core, y, x]
                            to = (y * xs + x) * cores + core
                            if split:
                                out_refs[shift][to, array, row] = tile
                            else:
                                out_refs[0][to, shift, array, row] = tile
            return carry

        lax.fori_loop(0, ys, step, 0)


def pack(arrays, place, sizes, chunk, split, after=()):
    ys, _, _, xs, _, cores = sizes
    rows, _, _, _, _, inner, feature = arrays[0].shape
    first, tail = ys * xs * cores, (len(arrays), rows, inner, feature)
    if split:
        shapes = [jax.ShapeDtypeStruct((first, *tail), BF16)] * ZS
    else:
        shapes = [jax.ShapeDtypeStruct((first, ZS, *tail), BF16)]
    return pl.pallas_call(
        lambda *refs: pack_kernel(sizes, chunk, split, *refs),
        out_shape=shapes,
        in_specs=[SCALARS] + [FAR] * 4 + [ANY] * len(after),
        out_specs=[WHOLE] * len(shapes),
        scratch_shapes=[
            pltpu.VMEM((ZS, 4, rows, cores, ys, xs, inner, feature), BF16),
            pltpu.SemaphoreType.DMA((ZS, 4)),
        ],
        compiler_params=pltpu.CompilerParams(vmem_limit_bytes=ALL),
        name="pack",
    )(place, *arrays, *after)


def attend_kernel(sizes, pieces, split, place_ref, *refs):
    ys, _, z0s, xs, _, cores = sizes
    in_refs, refs = refs[:pieces], refs[pieces + 1 :]
    *out_refs, wide_in, wide_out = refs
    sources = in_refs[0].shape[0]
    arrays, tile, feature = in_refs[0].shape[-3:]
    inner = tile // 4
    rows = ys * ZS * xs * 4
    my_z = place_ref[0] * z0s + place_ref[1]

    for shift in range(ZS):
        z = (my_z - shift + ZS) % ZS

        def widen(at, carry, shift=shift, z=z):
            y, x = at // xs, at % xs
            start = ((y * ZS + z) * xs + x) * tile
            for core in range(cores):
                for array in range(arrays):
                    source = at * cores + core
                    if pieces == 1:
                        block = in_refs[0][source, shift, array]
                    else:
                        block = in_refs[shift][source, array]
                    to = pl.multiple_of(core * rows * inner + start, tile)
                    wide_in[array, pl.ds(to, tile), :] = block.astype(F32)
            return carry

        lax.fori_loop(0, sources // cores, widen, 0, unroll=2)

    def column(core, carry):
        for place in range(inner):
            spot = pl.ds(core * rows * inner + place, rows, stride=inner)
            block = [wide_in[array, spot, :].astype(BF16) for array in range(arrays)]
            for array, result in enumerate(attend_column(*block)):
                wide_out[array, spot, :] = result
        return carry

    lax.fori_loop(0, cores, column, 0)

    for shift in range(ZS):
        z = my_z ^ shift

        def narrow(at, carry, shift=shift, z=z):
            y, x = at // xs, at % xs
            start = ((y * ZS + z) * xs + x) * tile
            for array in range(arrays):
                for core in range(cores):
                    spot = pl.ds(pl.multiple_of(core * rows * inner + start, tile), tile)
                    block = wide_out[array, spot, :].astype(BF16)
                    to = slice(core * tile, (core + 1) * tile)
                    if split:
                        out_refs[shift][at, array, to] = block
                    else:
                        out_refs[0][at, shift, array, to] = block
            return carry

        lax.fori_loop(0, ys * xs, narrow, 0, unroll=2)


def attend(pieces, place, sizes, split, after):
    ys, _, _, xs, _, cores = sizes
    arrays, tile, feature = pieces[0].shape[-3:]
    rows = ys * ZS * xs * 4
    columns = tile // 4 * cores
    tail = (arrays, tile * cores, feature)
    if split:
        shapes = [jax.ShapeDtypeStruct((ys * xs, *tail), BF16)] * ZS
    else:
        shapes = [jax.ShapeDtypeStruct((ys * xs, ZS, *tail), BF16)]
    return pl.pallas_call(
        lambda *refs: attend_kernel(sizes, len(pieces), split, *refs),
        out_shape=shapes,
        in_specs=[SCALARS] + [WHOLE] * len(pieces) + [ANY],
        out_specs=[WHOLE] * len(shapes),
        scratch_shapes=[pltpu.VMEM((arrays, rows * columns, feature), F32)] * 2,
        compiler_params=pltpu.CompilerParams(vmem_limit_bytes=LIMIT),
        cost_estimate=pl.CostEstimate(flops=0, bytes_accessed=0, transcendentals=0),
        name="attend",
    )(place, *pieces, after)


def join_kernel(*refs):
    *in_refs, _, out_ref = refs
    for side, ref in enumerate(in_refs):
        out_ref[:, side] = ref[...]


def join(pieces, after):
    first, *tail = pieces[0].shape
    return pl.pallas_call(
        join_kernel,
        out_shape=jax.ShapeDtypeStruct((first, len(pieces), *tail), BF16),
        in_specs=[WHOLE] * len(pieces) + [ANY],
        out_specs=WHOLE,
        compiler_params=pltpu.CompilerParams(vmem_limit_bytes=LIMIT),
        name="join",
    )(*pieces, after)


def part_kernel(in_ref, _, *refs):
    *out_refs, sems = refs
    copies = [
        pltpu.make_async_copy(in_ref.at[:, shift], ref, sems.at[shift])
        for shift, ref in enumerate(out_refs)
    ]
    for copy in copies:
        copy.start()
    for copy in copies:
        copy.wait()


def part(joined, after):
    first, shifts, *tail = joined.shape
    return pl.pallas_call(
        part_kernel,
        out_shape=[jax.ShapeDtypeStruct((first, *tail), BF16)] * shifts,
        in_specs=[FAR, ANY],
        out_specs=[WHOLE] * shifts,
        scratch_shapes=[pltpu.SemaphoreType.DMA((shifts,))],
        compiler_params=pltpu.CompilerParams(vmem_limit_bytes=ALL),
        name="part",
    )(joined, after)


def hold_kernel(*refs):
    refs[-1][...] = jnp.zeros_like(refs[-1])


def hold(waited, flops=10**12):
    return pl.pallas_call(
        hold_kernel,
        out_shape=jax.ShapeDtypeStruct((8, 128), F32),
        in_specs=[ANY] * len(waited),
        out_specs=WHOLE,
        cost_estimate=pl.CostEstimate(flops=flops, bytes_accessed=4096, transcendentals=0),
        name="hold",
    )(*waited)


def unpack_kernel(sizes, place_ref, _, first_ref, *refs):
    _, _, z0s, xs, ws, cores = sizes
    second_refs, refs = refs[:ZS], refs[ZS:]
    *out_refs, wide = refs
    arrays, tile, feature = first_ref.shape[-3:]
    rows = out_refs[0].shape[0]
    heads = ws * cores
    some = tile // cores
    size = some // rows * heads
    my_z, my_w = place_ref[0] * z0s + place_ref[1], place_ref[2]
    for shift in range(ZS):
        z = my_z ^ shift
        run = other_run(my_w, 0, z)

        def step(x, carry, shift=shift, z=z, runs=(0, 1)):
            for array in range(arrays):
                base = array * some * heads
                for chunk in range(2):
                    ref = first_ref if chunk == 0 else second_refs[shift]
                    block = (ref[x, shift, array] if chunk == 0 else ref[x, array]).astype(F32)
                    for core in range(cores):
                        spot = pl.ds(base + runs[chunk] * cores + core, some, stride=heads)
                        wide[spot, :] = block[core * some : (core + 1) * some]
                for row in range(rows):
                    to = pl.multiple_of((z * xs + x) * size, size)
                    block = wide[pl.ds(base + row * size, size), :].astype(BF16)
                    out_refs[array][row, pl.ds(to, size), :] = block
            return carry

        for which in range(ws):

            @pl.when(run == which)
            def _(step=step, which=which):
                lax.fori_loop(0, xs, functools.partial(step, runs=(which, 1 - which)), 0)


def unpack(first, second, place, sizes, rows, after):
    ys, _, _, xs, ws, cores = sizes
    arrays, tile, feature = first.shape[-3:]
    width = ys * ZS * xs * tile // rows * ws
    return pl.pallas_call(
        lambda *refs: unpack_kernel(sizes, *refs),
        out_shape=[jax.ShapeDtypeStruct((rows, width, feature), BF16)] * arrays,
        grid=(ys,),
        in_specs=[SCALARS, ANY]
        + [pl.BlockSpec((xs, ZS, arrays, tile, feature), lambda i: (i, 0, 0, 0, 0))]
        + [pl.BlockSpec((xs, arrays, tile, feature), lambda i: (i, 0, 0, 0))] * ZS,
        out_specs=[pl.BlockSpec((rows, width // ys, feature), lambda i: (0, i, 0))] * arrays,
        scratch_shapes=[pltpu.VMEM((arrays * tile * ws, feature), F32)],
        compiler_params=pltpu.CompilerParams(vmem_limit_bytes=ALL),
        name="unpack",
    )(place, after, first, *second)


def z_in(pieces):
    return [pieces[0]] + [
        lax.ppermute(
            pieces[k], ("z1", "z0"), [(z, (z + k) % ZS) for z in range(ZS)]
        )
        for k in range(1, ZS)
    ]


def z_out(pieces, chunk):
    def pairs(shift):
        made = []
        for z in range(ZS):
            for w in range(2):
                to = (w + chunk + (z in (0, ZS - 1))) % 2
                made.append((z * 2 + w, (z ^ shift) * 2 + to))
        return made

    return [lax.ppermute(pieces[k], ("z1", "z0", "w"), pairs(k)) for k in range(ZS)]


def shards(*arrays):
    sizes = tuple(lax.axis_size(name) for name in FINE)
    ys, z1s, z0s, xs, ws, cores = sizes
    rows, columns, _, feature = arrays[0].shape
    owners = ys * z1s * z0s * xs
    inner = columns // (owners * ws * cores)
    arrays = [a.reshape(rows, ws * cores, ys, ZS, xs, inner, feature) for a in arrays]
    place = jnp.stack([lax.axis_index(name) for name in ("z1", "z0", "w")]).astype(jnp.int32)

    def flat(piece):
        return piece.reshape(*piece.shape[:-3], rows * inner, feature)

    def across(whole, names):
        return lax.all_to_all(whole, names, 0, 0, tiled=True)

    packed = [flat(p) for p in pack(arrays, place, sizes, 0, True)]
    second = flat(pack(arrays, place, sizes, 1, False, packed[:1])[0])
    first = z_in(packed)
    pieces = part(across(second, NEAR), hold(first[1:]))
    second = z_in(pieces)
    first = across(join(first, pieces[0]), NEAR)

    done = attend([first], place, sizes, True, hold(second[2:3]))
    first = z_out(done, 0)
    second = attend(second, place, sizes, False, done[0])[0]
    pieces = part(across(second, ("y", "x")), hold(first))
    second = z_out(pieces, 1)
    first = across(join(first, pieces[0]), ("y", "x"))

    results = unpack(first, second, place, sizes, rows, hold(second))
    return tuple(r.reshape(rows, columns // (ws * cores), ws * cores, feature) for r in results)


def solution(mesh):
    fine = Mesh(mesh.devices.reshape(SIZES), FINE)
    row, head = FINE[:4], FINE[4:]
    spec_in = P(row, None, head, None)
    spec_out = P(row, head, None, None)
    return jax.shard_map(
        shards, mesh=fine, in_specs=(spec_in,) * 4, out_specs=(spec_out,) * 4, check_vma=False
    )
```

time: 236 us -> 233 us (0.987)
  the two profiles are of different devices: /device:TPU:2 before, /device:TPU:41 now
where the time goes in v5:
time: 233 us; the launch traced here: 232 us
  waiting for transfers between devices  129 us (55%)
  starting transfers between devices  54.3 us (23%)
  Pallas kernels  41 us (18%)
  local copies, waits for them, and re-layouts  5.98 us (3%)
    ppermute x8, waiting for transfers between devices, z_out(): lax.ppermute(pieces[k], ('z1', 'z0', 'w'), pairs(k))  72.8 us
    ppermute x6, waiting for transfers between devices, z_in(): lax.ppermute(pieces[k], ('z1', 'z0'), [(z, (z + k) % ZS) for z in range(Z...  41.7 us
    all_to_all x4, starting transfers between devices, across(): return lax.all_to_all(whole, names, 0, 0, tiled=True)  28.6 us
    ppermute x8, starting transfers between devices, z_out(): lax.ppermute(pieces[k], ('z1', 'z0', 'w'), pairs(k))  18.8 us
    pallas_call x2, Pallas kernels, attend(): pl.pallas_call(lambda *refs: attend_kernel(sizes, len(pieces), split, *re...  16.1 us
    all_to_all x4, waiting for transfers between devices, across(): return lax.all_to_all(whole, names, 0, 0, tiled=True)  14.5 us
    pallas_call x2, Pallas kernels, pack(): pl.pallas_call(lambda *refs: pack_kernel(sizes, chunk, split, *refs), out...  8.11 us
    ppermute x6, starting transfers between devices, z_in(): lax.ppermute(pieces[k], ('z1', 'z0'), [(z, (z + k) % ZS) for z in range(Z...  6.85 us
  transfers between devices with their start and end apart: 18, of which 9 were waited for; matrix products, arithmetic and copies ran while one was open for 0% of the time, Pallas kernels for 11%

profile of v5, /device:TPU:41, one launch (start us, length us, event | category | flops | bytes accessed | tf_op | source)
XLA Modules:
  0.0 231.7 jit_solution(3245037155755388776)
XLA Ops:
  1.2 4.0 %pack.2 = (bf16[32,4,4,4,128]{4,3,2,1,0:T(4,128)(2,1)}, bf16[32,4,4,4,128]{4,3,2,1,0:T(4,128)(2,1)}, bf16[32,4,4,4,128]{4,3,2,1,0:T(4,128)(2,1)}, bf16[32,4,4,4,128]{4,3,2,1,0:T(4,128)(2,1)}) custom-call(s32[3]{0:T(128)} %pad_add_fusion.refs_0_, bf16[4,4,4,4,4,4,128]{6,5,4,3,2,1,0:T(4,128)(2,1)} %bitcast.19, bf16[4,4,4,4,4,4,128]{6,5,4,3,2,1,0:T(4,128)(2,1)} %bitcast.21, ...), custom_call_target="tpu_custom_call" | custom-call | tf_op jit(solution)/shard_map/pack/pallas_call | solution.py:118
  5.3 1.7 collective-permute-start
  7.0 1.5 collective-permute-start.1
  8.4 1.4 collective-permute-start.2
  9.8 4.1 %pack.3 = bf16[32,4,4,4,4,128]{5,4,3,2,1,0:T(4,128)(2,1)} custom-call(s32[3]{0:T(128)} %pad_add_fusion.refs_0_, bf16[4,4,4,4,4,4,128]{6,5,4,3,2,1,0:T(4,128)(2,1)} %bitcast.20, bf16[4,4,4,4,4,4,128]{6,5,4,3,2,1,0:T(4,128)(2,1)} %bitcast.22, bf16[4,4,4,4,4,4,128]{6,5,4,3,2,1,0:T(4,128)(2,1)} %bitcast.24, bf16[4,4,4,4,4,4,128]{6,5,4,3,2,1,0:T(4,128)(2,1)} %bitcast.26, ...), custom_call_target="tpu_custom_call" | custom-call | tf_op jit(solution)/shard_map/pack/pallas_call | solution.py:118
  13.9 8.8 %all-to-all-start = ((bf16[32,4,4,16,128]{4,3,2,1,0:T(8,128)(2,1)}), bf16[32,4,4,16,128]{4,3,2,1,0:T(8,128)(2,1)}, u32[]{:S(2)}, u32[]{:S(2)}) async-start(bf16[32,4,4,16,128]{4,3,2,1,0:T(8,128)(2,1)} %bitcast.18), calls=%async_computation | async-start | bytes 4194304 | tf_op jit(solution)/shard_map/all_to_all | solution.py:359
  22.7 28.9 %collective-permute-done.1.refs_1_.refs_2_ = bf16[32,4,16,128]{3,2,1,0:T(8,128)(2,1)S(1)} collective-permute-done((bf16[32,4,16,128]{3,2,1,0:T(8,128)(2,1)}, bf16[32,4,16,128]{3,2,1,0:T(8,128)(2,1)S(1)}, u32[]{:S(2)}, u32[]{:S(2)}) %collective-permute-start.1) | collective-permute-done | bytes 524320 | tf_op jit(solution)/shard_map/ppermute | solution.py:327
  51.6 3.1 %collective-permute-done.2.refs_2_.refs_3_ = bf16[32,4,16,128]{3,2,1,0:T(8,128)(2,1)S(1)} collective-permute-done((bf16[32,4,16,128]{3,2,1,0:T(8,128)(2,1)}, bf16[32,4,16,128]{3,2,1,0:T(8,128)(2,1)S(1)}, u32[]{:S(2)}, u32[]{:S(2)}) %collective-permute-start.2) | collective-permute-done | bytes 524320 | tf_op jit(solution)/shard_map/ppermute | solution.py:327
  56.1 3.0 %part.2 = (bf16[32,4,16,128]{3,2,1,0:T(8,128)(2,1)}, bf16[32,4,16,128]{3,2,1,0:T(8,128)(2,1)}, bf16[32,4,16,128]{3,2,1,0:T(8,128)(2,1)}, bf16[32,4,16,128]{3,2,1,0:T(8,128)(2,1)}) custom-call(bf16[32,4,4,16,128]{4,3,2,1,0:T(8,128)(2,1)} %all-to-all-done.in_ref, f32[8,128]{1,0:T(8,128)} %hold.4._), custom_call_target="tpu_custom_call" | custom-call | tf_op jit(solution)/shard_map/part/pallas_call | solution.py:245
  61.0 1.5 join.2
  62.4 9.1 %all-to-all-start.1 = ((bf16[32,4,4,16,128]{4,3,2,1,0:T(8,128)(2,1)}), bf16[32,4,4,16,128]{4,3,2,1,0:T(8,128)(2,1)}, u32[]{:S(2)}, u32[]{:S(2)}) async-start(bf16[32,4,4,16,128]{4,3,2,1,0:T(8,128)(2,1)} %join.2), calls=%async_computation.1 | async-start | bytes 4194304 | tf_op jit(solution)/shard_map/all_to_all | solution.py:359
  71.6 1.5 collective-permute-start.5
  73.0 9.7 %collective-permute-done.4.refs_0_.refs_3_ = bf16[32,4,16,128]{3,2,1,0:T(8,128)(2,1)S(1)} collective-permute-done((bf16[32,4,16,128]{3,2,1,0:T(8,128)(2,1)}, bf16[32,4,16,128]{3,2,1,0:T(8,128)(2,1)S(1)}, u32[]{:S(2)}, u32[]{:S(2)}) %collective-permute-start.4) | collective-permute-done | bytes 524320 | tf_op jit(solution)/shard_map/ppermute | solution.py:327
  84.1 14.5 %all-to-all-done.1.refs_1_ = bf16[32,4,4,16,128]{4,3,2,1,0:T(8,128)(2,1)} async-done(((bf16[32,4,4,16,128]{4,3,2,1,0:T(8,128)(2,1)}), bf16[32,4,4,16,128]{4,3,2,1,0:T(8,128)(2,1)}, u32[]{:S(2)}, u32[]{:S(2)}) %all-to-all-start.1) | async-done | bytes 2097184 | tf_op jit(solution)/shard_map/all_to_all | solution.py:359
  99.3 8.2 %attend.2 = (bf16[16,4,32,128]{3,2,1,0:T(8,128)(2,1)}, bf16[16,4,32,128]{3,2,1,0:T(8,128)(2,1)}, bf16[16,4,32,128]{3,2,1,0:T(8,128)(2,1)}, bf16[16,4,32,128]{3,2,1,0:T(8,128)(2,1)}) custom-call(s32[3]{0:T(128)S(1)} %copy-done.20, bf16[32,4,4,16,128]{4,3,2,1,0:T(8,128)(2,1)} %all-to-all-done.1.refs_1_, f32[8,128]{1,0:T(8,128)S(1)} %copy-done.21), custom_call_target="tpu_custom_call" | custom-call | tf_op jit(solution)/shard_map/attend/pallas_call | solution.py:201
  107.6 3.0 %collective-permute-start.8 = (bf16[16,4,32,128]{3,2,1,0:T(8,128)(2,1)}, bf16[16,4,32,128]{3,2,1,0:T(8,128)(2,1)S(1)}, u32[]{:S(2)}, u32[]{:S(2)}) collective-permute-start(bf16[16,4,32,128]{3,2,1,0:T(8,128)(2,1)} %get-tuple-element.34), channel_id=1, source_target_pairs={{0,34},{2,32},{16,48},{18,50},{32,0},{34,2},{48,18},{50,16},{1,35}... | collective-permute-start | bytes 1572872 | tf_op jit(solution)/shard_map/ppermute | solution.py:343
  110.6 3.5 %collective-permute-start.9 = (bf16[16,4,32,128]{3,2,1,0:T(8,128)(2,1)}, bf16[16,4,32,128]{3,2,1,0:T(8,128)(2,1)S(1)}, u32[]{:S(2)}, u32[]{:S(2)}) collective-permute-start(bf16[16,4,32,128]{3,2,1,0:T(8,128)(2,1)} %get-tuple-element.35), channel_id=1, source_target_pairs={{0,50},{2,48},{16,32},{18,34},{32,16},{34,18},{48,2},{50,0},{1,51}... | collective-permute-start | bytes 1572872 | tf_op jit(solution)/shard_map/ppermute | solution.py:343
  114.1 1.7 collective-permute-start.6
  115.8 7.8 %attend.3 = bf16[16,4,4,32,128]{4,3,2,1,0:T(8,128)(2,1)} custom-call(s32[3]{0:T(128)S(1)} %copy-done.20, bf16[32,4,16,128]{3,2,1,0:T(8,128)(2,1)S(1)} %copy-done.1, bf16[32,4,16,128]{3,2,1,0:T(8,128)(2,1)} %collective-permute-done.3.refs_2_, bf16[32,4,16,128]{3,2,1,0:T(8,128)(2,1)S(1)} %copy-done.12, ...), custom_call_target="tpu_custom_call" | custom-call | tf_op jit(solution)/shard_map/attend/pallas_call | solution.py:201
  123.7 5.5 %all-to-all-start.2 = ((bf16[16,4,4,32,128]{4,3,2,1,0:T(8,128)(2,1)}), bf16[16,4,4,32,128]{4,3,2,1,0:T(8,128)(2,1)}, u32[]{:S(2)}, u32[]{:S(2)}) async-start(bf16[16,4,4,32,128]{4,3,2,1,0:T(8,128)(2,1)} %attend.3), calls=%async_computation.2 | async-start | bytes 4194304 | tf_op jit(solution)/shard_map/all_to_all | solution.py:359
  129.2 6.6 %collective-permute-done.8.refs_2_ = bf16[16,4,32,128]{3,2,1,0:T(8,128)(2,1)S(1)} collective-permute-done((bf16[16,4,32,128]{3,2,1,0:T(8,128)(2,1)}, bf16[16,4,32,128]{3,2,1,0:T(8,128)(2,1)S(1)}, u32[]{:S(2)}, u32[]{:S(2)}) %collective-permute-start.8) | collective-permute-done | bytes 524320 | tf_op jit(solution)/shard_map/ppermute | solution.py:343
  135.8 22.6 %collective-permute-done.9.refs_3_ = bf16[16,4,32,128]{3,2,1,0:T(8,128)(2,1)S(1)} collective-permute-done((bf16[16,4,32,128]{3,2,1,0:T(8,128)(2,1)}, bf16[16,4,32,128]{3,2,1,0:T(8,128)(2,1)S(1)}, u32[]{:S(2)}, u32[]{:S(2)}) %collective-permute-start.9) | collective-permute-done | bytes 524320 | tf_op jit(solution)/shard_map/ppermute | solution.py:343
  160.6 3.0 %part.3 = (bf16[16,4,32,128]{3,2,1,0:T(8,128)(2,1)}, bf16[16,4,32,128]{3,2,1,0:T(8,128)(2,1)}, bf16[16,4,32,128]{3,2,1,0:T(8,128)(2,1)}, bf16[16,4,32,128]{3,2,1,0:T(8,128)(2,1)}) custom-call(bf16[16,4,4,32,128]{4,3,2,1,0:T(8,128)(2,1)} %all-to-all-done.2.in_ref, f32[8,128]{1,0:T(8,128)} %hold.6._), custom_call_target="tpu_custom_call" | custom-call | tf_op jit(solution)/shard_map/part/pallas_call | solution.py:245
  164.4 2.5 %collective-permute-start.12 = (bf16[16,4,32,128]{3,2,1,0:T(8,128)(2,1)}, bf16[16,4,32,128]{3,2,1,0:T(8,128)(2,1)S(1)}, u32[]{:S(2)}, u32[]{:S(2)}) collective-permute-start(bf16[16,4,32,128]{3,2,1,0:T(8,128)(2,1)} %get-tuple-element.38), channel_id=1, source_target_pairs={{0,32},{2,34},{16,50},{18,48},{32,2},{34,0},{48,16},{50,18},{1,33}... | collective-permute-start | bytes 1572872 | tf_op jit(solution)/shard_map/ppermute | solution.py:343
  167.0 1.5 collective-permute-start.13
  168.5 5.7 %collective-permute-start.10 = (bf16[16,4,32,128]{3,2,1,0:T(8,128)(2,1)}, bf16[16,4,32,128]{3,2,1,0:T(8,128)(2,1)}, u32[]{:S(2)}, u32[]{:S(2)}) collective-permute-start(bf16[16,4,32,128]{3,2,1,0:T(8,128)(2,1)} %get-tuple-element.36.refs_4_), channel_id=1, source_target_pairs={{0,0},{2,2},{16,18},{18,16},{32,34},{34,32},{48,48},{50,50},{1,1},... | collective-permute-start | bytes 1572872 | tf_op jit(solution)/shard_map/ppermute | solution.py:343
  175.3 1.5 join.3
  176.7 5.3 %all-to-all-start.3 = ((bf16[16,4,4,32,128]{4,3,2,1,0:T(8,128)(2,1)}), bf16[16,4,4,32,128]{4,3,2,1,0:T(8,128)(2,1)}, u32[]{:S(2)}, u32[]{:S(2)}) async-start(bf16[16,4,4,32,128]{4,3,2,1,0:T(8,128)(2,1)} %join.3), calls=%async_computation.3 | async-start | bytes 4194304 | tf_op jit(solution)/shard_map/all_to_all | solution.py:359
  182.1 5.0 %collective-permute-done.12.refs_2_.refs_5_ = bf16[16,4,32,128]{3,2,1,0:T(8,128)(2,1)S(1)} collective-permute-done((bf16[16,4,32,128]{3,2,1,0:T(8,128)(2,1)}, bf16[16,4,32,128]{3,2,1,0:T(8,128)(2,1)S(1)}, u32[]{:S(2)}, u32[]{:S(2)}) %collective-permute-start.12) | collective-permute-done | bytes 524320 | tf_op jit(solution)/shard_map/ppermute | solution.py:343
  187.1 27.4 %collective-permute-done.13.refs_3_.refs_6_ = bf16[16,4,32,128]{3,2,1,0:T(8,128)(2,1)} collective-permute-done((bf16[16,4,32,128]{3,2,1,0:T(8,128)(2,1)}, bf16[16,4,32,128]{3,2,1,0:T(8,128)(2,1)}, u32[]{:S(2)}, u32[]{:S(2)}) %collective-permute-start.13) | collective-permute-done | bytes 524320 | tf_op jit(solution)/shard_map/ppermute | solution.py:343
  214.5 11.1 %collective-permute-done.10.refs_0_.refs_3_ = bf16[16,4,32,128]{3,2,1,0:T(8,128)(2,1)} collective-permute-done((bf16[16,4,32,128]{3,2,1,0:T(8,128)(2,1)}, bf16[16,4,32,128]{3,2,1,0:T(8,128)(2,1)}, u32[]{:S(2)}, u32[]{:S(2)}) %collective-permute-start.10) | collective-permute-done | bytes 524320 | tf_op jit(solution)/shard_map/ppermute | solution.py:343
  226.2 5.4 %unpack.1 = (bf16[4,1024,128]{2,1,0:T(8,128)(2,1)}, bf16[4,1024,128]{2,1,0:T(8,128)(2,1)}, bf16[4,1024,128]{2,1,0:T(8,128)(2,1)}, bf16[4,1024,128]{2,1,0:T(8,128)(2,1)}) custom-call(s32[3]{0:T(128)} %pad_add_fusion.refs_0_, f32[8,128]{1,0:T(8,128)} %hold.7.refs_1_, bf16[16,4,4,32,128]{4,3,2,1,0:T(8,128)(2,1)} %all-to-all-done.3.refs_2_, ...), custom_call_target="tpu_custom_call" | custom-call | tf_op jit(solution)/shard_map/unpack/pallas_call | solution.py:311
  (66 shorter events, 10.6 us)
Async XLA Ops:
  5.3 17.4 %collective-permute-start = (bf16[32,4,16,128]{3,2,1,0:T(8,128)(2,1)}, bf16[32,4,16,128]{3,2,1,0:T(8,128)(2,1)S(1)}, u32[]{:S(2)}, u32[]{:S(2)}) collective-permute-start(bf16[32,4,16,128]{3,2,1,0:T(8,128)(2,1)} %bitcast.33), channel_id=1, source_target_pairs={{0,16},{16,32},{32,48},{48,0},{1,17},{17,33},{33,49},{49,1},{2,18}... | collective-permute-start | bytes 1572872 | tf_op jit(solution)/shard_map/ppermute | solution.py:327
  7.0 44.6 %collective-permute-start.1 = (bf16[32,4,16,128]{3,2,1,0:T(8,128)(2,1)}, bf16[32,4,16,128]{3,2,1,0:T(8,128)(2,1)S(1)}, u32[]{:S(2)}, u32[]{:S(2)}) collective-permute-start(bf16[32,4,16,128]{3,2,1,0:T(8,128)(2,1)} %bitcast.32), channel_id=1, source_target_pairs={{0,32},{16,48},{32,0},{48,16},{1,33},{17,49},{33,1},{49,17},{2,34}... | collective-permute-start | bytes 1572872 | tf_op jit(solution)/shard_map/ppermute | solution.py:327
  8.4 46.2 %collective-permute-start.2 = (bf16[32,4,16,128]{3,2,1,0:T(8,128)(2,1)}, bf16[32,4,16,128]{3,2,1,0:T(8,128)(2,1)S(1)}, u32[]{:S(2)}, u32[]{:S(2)}) collective-permute-start(bf16[32,4,16,128]{3,2,1,0:T(8,128)(2,1)} %bitcast.31), channel_id=1, source_target_pairs={{0,48},{16,0},{32,16},{48,32},{1,49},{17,1},{33,17},{49,33},{2,50}... | collective-permute-start | bytes 1572872 | tf_op jit(solution)/shard_map/ppermute | solution.py:327
  13.9 42.2 %all-to-all-start = ((bf16[32,4,4,16,128]{4,3,2,1,0:T(8,128)(2,1)}), bf16[32,4,4,16,128]{4,3,2,1,0:T(8,128)(2,1)}, u32[]{:S(2)}, u32[]{:S(2)}) async-start(bf16[32,4,4,16,128]{4,3,2,1,0:T(8,128)(2,1)} %bitcast.18), calls=%async_computation | async-start | bytes 4194304 | tf_op jit(solution)/shard_map/all_to_all | solution.py:359
  22.7 32.0 %copy-start.13 = (bf16[32,4,16,128]{3,2,1,0:T(8,128)(2,1)}, bf16[32,4,16,128]{3,2,1,0:T(8,128)(2,1)S(1)}, u32[]{:S(2)}) copy-start(bf16[32,4,16,128]{3,2,1,0:T(8,128)(2,1)S(1)} %collective-permute-done.refs_0_.refs_1_) | copy-start | bytes 1572868
  56.1 3.8 %copy-start.16 = (bf16[32,4,16,128]{3,2,1,0:T(8,128)(2,1)S(1)}, bf16[32,4,16,128]{3,2,1,0:T(8,128)(2,1)}, u32[]{:S(2)}) copy-start(bf16[32,4,16,128]{3,2,1,0:T(8,128)(2,1)} %copy-done.15) | copy-start | bytes 1572868
  56.1 3.8 %copy-start.19 = (bf16[32,4,16,128]{3,2,1,0:T(8,128)(2,1)S(1)}, bf16[32,4,16,128]{3,2,1,0:T(8,128)(2,1)}, u32[]{:S(2)}) copy-start(bf16[32,4,16,128]{3,2,1,0:T(8,128)(2,1)} %copy-done.18) | copy-start | bytes 1572868
  59.1 23.6 %collective-permute-start.4 = (bf16[32,4,16,128]{3,2,1,0:T(8,128)(2,1)}, bf16[32,4,16,128]{3,2,1,0:T(8,128)(2,1)S(1)}, u32[]{:S(2)}, u32[]{:S(2)}) collective-permute-start(bf16[32,4,16,128]{3,2,1,0:T(8,128)(2,1)} %get-tuple-element.30), channel_id=1, source_target_pairs={{0,32},{16,48},{32,0},{48,16},{1,33},{17,49},{33,1},{49,17},{2,34}... | collective-permute-start | bytes 1572872 | tf_op jit(solution)/shard_map/ppermute | solution.py:327
  62.4 36.2 %all-to-all-start.1 = ((bf16[32,4,4,16,128]{4,3,2,1,0:T(8,128)(2,1)}), bf16[32,4,4,16,128]{4,3,2,1,0:T(8,128)(2,1)}, u32[]{:S(2)}, u32[]{:S(2)}) async-start(bf16[32,4,4,16,128]{4,3,2,1,0:T(8,128)(2,1)} %join.2), calls=%async_computation.1 | async-start | bytes 4194304 | tf_op jit(solution)/shard_map/all_to_all | solution.py:359
  71.5 42.6 %collective-permute-start.3 = (bf16[32,4,16,128]{3,2,1,0:T(8,128)(2,1)}, bf16[32,4,16,128]{3,2,1,0:T(8,128)(2,1)}, u32[]{:S(2)}, u32[]{:S(2)}) collective-permute-start(bf16[32,4,16,128]{3,2,1,0:T(8,128)(2,1)} %get-tuple-element.29), channel_id=1, source_target_pairs={{0,16},{16,32},{32,48},{48,0},{1,17},{17,33},{33,49},{49,1},{2,18}... | collective-permute-start | bytes 1572872 | tf_op jit(solution)/shard_map/ppermute | solution.py:327
  71.6 44.2 %collective-permute-start.5 = (bf16[32,4,16,128]{3,2,1,0:T(8,128)(2,1)}, bf16[32,4,16,128]{3,2,1,0:T(8,128)(2,1)}, u32[]{:S(2)}, u32[]{:S(2)}) collective-permute-start(bf16[32,4,16,128]{3,2,1,0:T(8,128)(2,1)} %get-tuple-element.31), channel_id=1, source_target_pairs={{0,48},{16,0},{32,16},{48,32},{1,49},{17,1},{33,17},{49,33},{2,50}... | collective-permute-start | bytes 1572872 | tf_op jit(solution)/shard_map/ppermute | solution.py:327
  83.5 15.1 %copy-start.20 = (s32[3]{0:T(128)S(1)}, s32[3]{0:T(128)}, u32[]{:S(2)}) copy-start(s32[3]{0:T(128)} %pad_add_fusion.refs_0_) | copy-start | bytes 40
  84.1 31.7 %copy-start.1 = (bf16[32,4,16,128]{3,2,1,0:T(8,128)(2,1)S(1)}, bf16[32,4,16,128]{3,2,1,0:T(8,128)(2,1)}, u32[]{:S(2)}) copy-start(bf16[32,4,16,128]{3,2,1,0:T(8,128)(2,1)} %get-tuple-element.28.refs_4_.refs_1_) | copy-start | bytes 1572868
  84.1 31.7 %copy-start.12 = (bf16[32,4,16,128]{3,2,1,0:T(8,128)(2,1)S(1)}, bf16[32,4,16,128]{3,2,1,0:T(8,128)(2,1)}, u32[]{:S(2)}) copy-start(bf16[32,4,16,128]{3,2,1,0:T(8,128)(2,1)} %copy-done.11) | copy-start | bytes 1572868
  107.6 21.6 %collective-permute-start.7 = (bf16[16,4,32,128]{3,2,1,0:T(8,128)(2,1)}, bf16[16,4,32,128]{3,2,1,0:T(8,128)(2,1)S(1)}, u32[]{:S(2)}, u32[]{:S(2)}) collective-permute-start(bf16[16,4,32,128]{3,2,1,0:T(8,128)(2,1)} %get-tuple-element.33), channel_id=1, source_target_pairs={{0,18},{2,16},{16,0},{18,2},{32,48},{34,50},{48,34},{50,32},{1,19}... | collective-permute-start | bytes 1572872 | tf_op jit(solution)/shard_map/ppermute | solution.py:343
  107.6 28.2 %collective-permute-start.8 = (bf16[16,4,32,128]{3,2,1,0:T(8,128)(2,1)}, bf16[16,4,32,128]{3,2,1,0:T(8,128)(2,1)S(1)}, u32[]{:S(2)}, u32[]{:S(2)}) collective-permute-start(bf16[16,4,32,128]{3,2,1,0:T(8,128)(2,1)} %get-tuple-element.34), channel_id=1, source_target_pairs={{0,34},{2,32},{16,48},{18,50},{32,0},{34,2},{48,18},{50,16},{1,35}... | collective-permute-start | bytes 1572872 | tf_op jit(solution)/shard_map/ppermute | solution.py:343
  110.6 47.8 %collective-permute-start.9 = (bf16[16,4,32,128]{3,2,1,0:T(8,128)(2,1)}, bf16[16,4,32,128]{3,2,1,0:T(8,128)(2,1)S(1)}, u32[]{:S(2)}, u32[]{:S(2)}) collective-permute-start(bf16[16,4,32,128]{3,2,1,0:T(8,128)(2,1)} %get-tuple-element.35), channel_id=1, source_target_pairs={{0,50},{2,48},{16,32},{18,34},{32,16},{34,18},{48,2},{50,0},{1,51}... | collective-permute-start | bytes 1572872 | tf_op jit(solution)/shard_map/ppermute | solution.py:343
  114.1 44.2 %collective-permute-start.6 = (bf16[16,4,32,128]{3,2,1,0:T(8,128)(2,1)}, bf16[16,4,32,128]{3,2,1,0:T(8,128)(2,1)S(1)}, u32[]{:S(2)}, u32[]{:S(2)}) collective-permute-start(bf16[16,4,32,128]{3,2,1,0:T(8,128)(2,1)} %get-tuple-element.32.refs_5_), channel_id=1, source_target_pairs={{0,2},{2,0},{16,16},{18,18},{32,32},{34,34},{48,50},{50,48},{1,3},... | collective-permute-start | bytes 1572872 | tf_op jit(solution)/shard_map/ppermute | solution.py:343
  123.7 36.9 %all-to-all-start.2 = ((bf16[16,4,4,32,128]{4,3,2,1,0:T(8,128)(2,1)}), bf16[16,4,4,32,128]{4,3,2,1,0:T(8,128)(2,1)}, u32[]{:S(2)}, u32[]{:S(2)}) async-start(bf16[16,4,4,32,128]{4,3,2,1,0:T(8,128)(2,1)} %attend.3), calls=%async_computation.2 | async-start | bytes 4194304 | tf_op jit(solution)/shard_map/all_to_all | solution.py:359
  129.2 29.2 %copy-start.3 = (bf16[16,4,32,128]{3,2,1,0:T(8,128)(2,1)}, bf16[16,4,32,128]{3,2,1,0:T(8,128)(2,1)S(1)}, u32[]{:S(2)}) copy-start(bf16[16,4,32,128]{3,2,1,0:T(8,128)(2,1)S(1)} %collective-permute-done.7.refs_1_) | copy-start | bytes 1572868
  135.8 22.6 %copy-start.5 = (bf16[16,4,32,128]{3,2,1,0:T(8,128)(2,1)}, bf16[16,4,32,128]{3,2,1,0:T(8,128)(2,1)S(1)}, u32[]{:S(2)}) copy-start(bf16[16,4,32,128]{3,2,1,0:T(8,128)(2,1)S(1)} %collective-permute-done.8.refs_2_) | copy-start | bytes 1572868
  160.6 13.6 %copy-start.4 = (bf16[16,4,32,128]{3,2,1,0:T(8,128)(2,1)S(1)}, bf16[16,4,32,128]{3,2,1,0:T(8,128)(2,1)}, u32[]{:S(2)}) copy-start(bf16[16,4,32,128]{3,2,1,0:T(8,128)(2,1)} %copy-done.3) | copy-start | bytes 1572868
  160.6 13.6 %copy-start.6 = (bf16[16,4,32,128]{3,2,1,0:T(8,128)(2,1)S(1)}, bf16[16,4,32,128]{3,2,1,0:T(8,128)(2,1)}, u32[]{:S(2)}) copy-start(bf16[16,4,32,128]{3,2,1,0:T(8,128)(2,1)} %copy-done.5) | copy-start | bytes 1572868
  160.6 13.6 %copy-start.8 = (bf16[16,4,32,128]{3,2,1,0:T(8,128)(2,1)S(1)}, bf16[16,4,32,128]{3,2,1,0:T(8,128)(2,1)}, u32[]{:S(2)}) copy-start(bf16[16,4,32,128]{3,2,1,0:T(8,128)(2,1)} %copy-done.7) | copy-start | bytes 1572868
  160.6 13.6 %copy-start.10 = (bf16[16,4,32,128]{3,2,1,0:T(8,128)(2,1)S(1)}, bf16[16,4,32,128]{3,2,1,0:T(8,128)(2,1)}, u32[]{:S(2)}) copy-start(bf16[16,4,32,128]{3,2,1,0:T(8,128)(2,1)} %copy-done.9) | copy-start | bytes 1572868
  163.6 18.4 %collective-permute-start.11 = (bf16[16,4,32,128]{3,2,1,0:T(8,128)(2,1)}, bf16[16,4,32,128]{3,2,1,0:T(8,128)(2,1)S(1)}, u32[]{:S(2)}, u32[]{:S(2)}) collective-permute-start(bf16[16,4,32,128]{3,2,1,0:T(8,128)(2,1)} %get-tuple-element.37), channel_id=1, source_target_pairs={{0,16},{2,18},{16,2},{18,0},{32,50},{34,48},{48,32},{50,34},{1,17}... | collective-permute-start | bytes 1572872 | tf_op jit(solution)/shard_map/ppermute | solution.py:343
  164.4 22.7 %collective-permute-start.12 = (bf16[16,4,32,128]{3,2,1,0:T(8,128)(2,1)}, bf16[16,4,32,128]{3,2,1,0:T(8,128)(2,1)S(1)}, u32[]{:S(2)}, u32[]{:S(2)}) collective-permute-start(bf16[16,4,32,128]{3,2,1,0:T(8,128)(2,1)} %get-tuple-element.38), channel_id=1, source_target_pairs={{0,32},{2,34},{16,50},{18,48},{32,2},{34,0},{48,16},{50,18},{1,33}... | collective-permute-start | bytes 1572872 | tf_op jit(solution)/shard_map/ppermute | solution.py:343
  167.0 47.5 %collective-permute-start.13 = (bf16[16,4,32,128]{3,2,1,0:T(8,128)(2,1)}, bf16[16,4,32,128]{3,2,1,0:T(8,128)(2,1)}, u32[]{:S(2)}, u32[]{:S(2)}) collective-permute-start(bf16[16,4,32,128]{3,2,1,0:T(8,128)(2,1)} %get-tuple-element.39), channel_id=1, source_target_pairs={{0,48},{2,50},{16,34},{18,32},{32,18},{34,16},{48,0},{50,2},{1,49}... | collective-permute-start | bytes 1572872 | tf_op jit(solution)/shard_map/ppermute | solution.py:343
  168.5 57.2 %collective-permute-start.10 = (bf16[16,4,32,128]{3,2,1,0:T(8,128)(2,1)}, bf16[16,4,32,128]{3,2,1,0:T(8,128)(2,1)}, u32[]{:S(2)}, u32[]{:S(2)}) collective-permute-start(bf16[16,4,32,128]{3,2,1,0:T(8,128)(2,1)} %get-tuple-element.36.refs_4_), channel_id=1, source_target_pairs={{0,0},{2,2},{16,18},{18,16},{32,34},{34,32},{48,48},{50,50},{1,1},... | collective-permute-start | bytes 1572872 | tf_op jit(solution)/shard_map/ppermute | solution.py:343
  176.7 49.5 %all-to-all-start.3 = ((bf16[16,4,4,32,128]{4,3,2,1,0:T(8,128)(2,1)}), bf16[16,4,4,32,128]{4,3,2,1,0:T(8,128)(2,1)}, u32[]{:S(2)}, u32[]{:S(2)}) async-start(bf16[16,4,4,32,128]{4,3,2,1,0:T(8,128)(2,1)} %join.3), calls=%async_computation.3 | async-start | bytes 4194304 | tf_op jit(solution)/shard_map/all_to_all | solution.py:359
  182.0 43.6 %copy-start.22 = (bf16[16,4,32,128]{3,2,1,0:T(8,128)(2,1)}, bf16[16,4,32,128]{3,2,1,0:T(8,128)(2,1)S(1)}, u32[]{:S(2)}) copy-start(bf16[16,4,32,128]{3,2,1,0:T(8,128)(2,1)S(1)} %collective-permute-done.11.refs_1_.refs_4_) | copy-start | bytes 1572868
  187.1 38.5 %copy-start.23 = (bf16[16,4,32,128]{3,2,1,0:T(8,128)(2,1)}, bf16[16,4,32,128]{3,2,1,0:T(8,128)(2,1)S(1)}, u32[]{:S(2)}) copy-start(bf16[16,4,32,128]{3,2,1,0:T(8,128)(2,1)S(1)} %collective-permute-done.12.refs_2_.refs_5_) | copy-start | bytes 1572868
  (10 other events, 16.7 us)

commit v6 on v5

--- a/solution.py
+++ b/solution.py
@@ -24,8 +24,8 @@
 ZS = 4
 
 
-def other_run(w, chunk, z):
-    return (w + chunk + jnp.where((z == 0) | (z == ZS - 1), 1, 0)) % 2
+def other_run(w, z):
+    return (w + jnp.where((z == 0) | (z == ZS - 1), 1, 0)) % 2
 
 
 def dot(a, b, dims):
@@ -78,10 +78,10 @@
     copies = []
     for shift in range(ZS):
         z = (my_z + shift) % ZS
-        quarter = other_run(my_w, chunk, z) * cores
+        quarter, slot = other_run(my_w, z) * cores, z // 2 * 2 + chunk
         for array, ref in enumerate(far_refs):
             copy = pltpu.make_async_copy(
-                ref.at[:, pl.ds(quarter, cores), :, z],
+                ref.at[:, pl.ds(quarter, cores), :, slot],
                 held.at[shift, array],
                 sems.at[shift, array],
             )
@@ -278,23 +278,26 @@
     some = tile // cores
     size = some // rows * heads
     my_z, my_w = place_ref[0] * z0s + place_ref[1], place_ref[2]
-    for shift in range(ZS):
-        z = my_z ^ shift
-        run = other_run(my_w, 0, z)
-
-        def step(x, carry, shift=shift, z=z, runs=(0, 1)):
-            for array in range(arrays):
-                base = array * some * heads
-                for chunk in range(2):
-                    ref = first_ref if chunk == 0 else second_refs[shift]
-                    block = (ref[x, shift, array] if chunk == 0 else ref[x, array]).astype(F32)
-                    for core in range(cores):
-                        spot = pl.ds(base + runs[chunk] * cores + core, some, stride=heads)
-                        wide[spot, :] = block[core * some : (core + 1) * some]
-                for row in range(rows):
-                    to = pl.multiple_of((z * xs + x) * size, size)
-                    block = wide[pl.ds(base + row * size, size), :].astype(BF16)
-                    out_refs[array][row, pl.ds(to, size), :] = block
+    for pair in range(ZS // 2):
+        z = my_z ^ (2 * pair)
+        run = other_run(my_w, z)
+
+        def step(x, carry, pair=pair, z=z, runs=(0, 1)):
+            for chunk in range(2):
+                slot = z // 2 * 2 + chunk
+                for array in range(arrays):
+                    base = (chunk * arrays + array) * some * heads
+                    for side in range(2):
+                        at = 2 * pair + side
+                        block = first_ref[x, at, array] if chunk == 0 else second_refs[at][x, array]
+                        block = block.astype(F32)
+                        for core in range(cores):
+                            spot = pl.ds(base + runs[side] * cores + core, some, stride=heads)
+                            wide[spot, :] = block[core * some : (core + 1) * some]
+                    for row in range(rows):
+                        to = pl.multiple_of((slot * xs + x) * size, size)
+                        block = wide[pl.ds(base + row * size, size), :].astype(BF16)
+                        out_refs[array][row, pl.ds(to, size), :] = block
             return carry
 
         for which in range(ws):
@@ -316,7 +319,7 @@
         + [pl.BlockSpec((xs, ZS, arrays, tile, feature), lambda i: (i, 0, 0, 0, 0))]
         + [pl.BlockSpec((xs, arrays, tile, feature), lambda i: (i, 0, 0, 0))] * ZS,
         out_specs=[pl.BlockSpec((rows, width // ys, feature), lambda i: (0, i, 0))] * arrays,
-        scratch_shapes=[pltpu.VMEM((arrays * tile * ws, feature), F32)],
+        scratch_shapes=[pltpu.VMEM((2 * arrays * tile * ws, feature), F32)],
         compiler_params=pltpu.CompilerParams(vmem_limit_bytes=ALL),
         name="unpack",
     )(place, after, first, *second)
@@ -331,12 +334,12 @@
     ]
 
 
-def z_out(pieces, chunk):
+def z_out(pieces):
     def pairs(shift):
         made = []
         for z in range(ZS):
             for w in range(2):
-                to = (w + chunk + (z in (0, ZS - 1))) % 2
+                to = (w + (z in (0, ZS - 1))) % 2
                 made.append((z * 2 + w, (z ^ shift) * 2 + to))
         return made
 
@@ -366,10 +369,10 @@
     first = across(join(first, pieces[0]), NEAR)
 
     done = attend([first], place, sizes, True, hold(second[2:3]))
-    first = z_out(done, 0)
+    first = z_out(done)
     second = attend(second, place, sizes, False, done[0])[0]
     pieces = part(across(second, ("y", "x")), hold(first))
-    second = z_out(pieces, 1)
+    second = z_out(pieces)
     first = across(join(first, pieces[0]), ("y", "x"))
 
     results = unpack(first, second, place, sizes, rows, hold(second))

time: 233 us -> 221 us (0.948)
  the two profiles are of different devices: /device:TPU:41 before, /device:TPU:2 now
where the time goes in v6:
time: 221 us; the launch traced here: 219 us
  waiting for transfers between devices  104 us (47%)
  starting transfers between devices  66.2 us (30%)
  Pallas kernels  40.6 us (18%)
  local copies, waits for them, and re-layouts  6.77 us (3%)
    ppermute x8, waiting for transfers between devices, z_out(): lax.ppermute(pieces[k], ('z1', 'z0', 'w'), pairs(k))  55.6 us
    ppermute x6, waiting for transfers between devices, z_in(): lax.ppermute(pieces[k], ('z1', 'z0'), [(z, (z + k) % ZS) for z in range(Z...  42.7 us
    all_to_all x4, starting transfers between devices, across(): return lax.all_to_all(whole, names, 0, 0, tiled=True)  27.9 us
    ppermute x8, starting transfers between devices, z_out(): lax.ppermute(pieces[k], ('z1', 'z0', 'w'), pairs(k))  22.1 us
    ppermute x6, starting transfers between devices, z_in(): lax.ppermute(pieces[k], ('z1', 'z0'), [(z, (z + k) % ZS) for z in range(Z...  16.1 us
    pallas_call x2, Pallas kernels, attend(): pl.pallas_call(lambda *refs: attend_kernel(sizes, len(pieces), split, *re...  16.1 us
    pallas_call x2, Pallas kernels, pack(): pl.pallas_call(lambda *refs: pack_kernel(sizes, chunk, split, *refs), out...  8.11 us
    unnamed x48, local copies, waits for them, and re-layouts  6.77 us
  transfers between devices with their start and end apart: 18, of which 8 were waited for; matrix products, arithmetic and copies ran while one was open for 0% of the time, Pallas kernels for 12%

profile of v6, /device:TPU:2, one launch (start us, length us, event | category | flops | bytes accessed | tf_op | source)
XLA Modules:
  0.0 219.1 jit_solution(5793293671410272754)
XLA Ops:
  1.2 4.0 %pack.2 = (bf16[32,4,4,4,128]{4,3,2,1,0:T(4,128)(2,1)}, bf16[32,4,4,4,128]{4,3,2,1,0:T(4,128)(2,1)}, bf16[32,4,4,4,128]{4,3,2,1,0:T(4,128)(2,1)}, bf16[32,4,4,4,128]{4,3,2,1,0:T(4,128)(2,1)}) custom-call(s32[3]{0:T(128)} %pad_add_fusion.refs_0_, bf16[4,4,4,4,4,4,128]{6,5,4,3,2,1,0:T(4,128)(2,1)} %bitcast.19, bf16[4,4,4,4,4,4,128]{6,5,4,3,2,1,0:T(4,128)(2,1)} %bitcast.21, ...), custom_call_target="tpu_custom_call" | custom-call | tf_op jit(solution)/shard_map/pack/pallas_call | solution.py:118
  5.3 2.0 collective-permute-start
  7.3 3.3 %collective-permute-start.1 = (bf16[32,4,16,128]{3,2,1,0:T(8,128)(2,1)}, bf16[32,4,16,128]{3,2,1,0:T(8,128)(2,1)S(1)}, u32[]{:S(2)}, u32[]{:S(2)}) collective-permute-start(bf16[32,4,16,128]{3,2,1,0:T(8,128)(2,1)} %bitcast.32), channel_id=1, source_target_pairs={{0,32},{16,48},{32,0},{48,16},{1,33},{17,49},{33,1},{49,17},{2,34}... | collective-permute-start | bytes 1572872 | tf_op jit(solution)/shard_map/ppermute | solution.py:330
  11.5 4.1 %pack.3 = bf16[32,4,4,4,4,128]{5,4,3,2,1,0:T(4,128)(2,1)} custom-call(s32[3]{0:T(128)} %pad_add_fusion.refs_0_, bf16[4,4,4,4,4,4,128]{6,5,4,3,2,1,0:T(4,128)(2,1)} %bitcast.20, bf16[4,4,4,4,4,4,128]{6,5,4,3,2,1,0:T(4,128)(2,1)} %bitcast.22, bf16[4,4,4,4,4,4,128]{6,5,4,3,2,1,0:T(4,128)(2,1)} %bitcast.24, bf16[4,4,4,4,4,4,128]{6,5,4,3,2,1,0:T(4,128)(2,1)} %bitcast.26, ...), custom_call_target="tpu_custom_call" | custom-call | tf_op jit(solution)/shard_map/pack/pallas_call | solution.py:118
  15.6 7.7 %all-to-all-start = ((bf16[32,4,4,16,128]{4,3,2,1,0:T(8,128)(2,1)}), bf16[32,4,4,16,128]{4,3,2,1,0:T(8,128)(2,1)}, u32[]{:S(2)}, u32[]{:S(2)}) async-start(bf16[32,4,4,16,128]{4,3,2,1,0:T(8,128)(2,1)} %bitcast.18), calls=%async_computation | async-start | bytes 4194304 | tf_op jit(solution)/shard_map/all_to_all | solution.py:362
  23.3 21.4 %collective-permute-done.1.refs_1_.refs_2_ = bf16[32,4,16,128]{3,2,1,0:T(8,128)(2,1)S(1)} collective-permute-done((bf16[32,4,16,128]{3,2,1,0:T(8,128)(2,1)}, bf16[32,4,16,128]{3,2,1,0:T(8,128)(2,1)S(1)}, u32[]{:S(2)}, u32[]{:S(2)}) %collective-permute-start.1) | collective-permute-done | bytes 524320 | tf_op jit(solution)/shard_map/ppermute | solution.py:330
  46.9 4.3 %all-to-all-done.in_ref = bf16[32,4,4,16,128]{4,3,2,1,0:T(8,128)(2,1)} async-done(((bf16[32,4,4,16,128]{4,3,2,1,0:T(8,128)(2,1)}), bf16[32,4,4,16,128]{4,3,2,1,0:T(8,128)(2,1)}, u32[]{:S(2)}, u32[]{:S(2)}) %all-to-all-start) | async-done | bytes 2097184 | tf_op jit(solution)/shard_map/all_to_all | solution.py:362
  51.2 2.9 %part.2 = (bf16[32,4,16,128]{3,2,1,0:T(8,128)(2,1)}, bf16[32,4,16,128]{3,2,1,0:T(8,128)(2,1)}, bf16[32,4,16,128]{3,2,1,0:T(8,128)(2,1)}, bf16[32,4,16,128]{3,2,1,0:T(8,128)(2,1)}) custom-call(bf16[32,4,4,16,128]{4,3,2,1,0:T(8,128)(2,1)} %all-to-all-done.in_ref, f32[8,128]{1,0:T(8,128)} %hold.4._), custom_call_target="tpu_custom_call" | custom-call | tf_op jit(solution)/shard_map/part/pallas_call | solution.py:245
  54.1 5.9 %collective-permute-start.4 = (bf16[32,4,16,128]{3,2,1,0:T(8,128)(2,1)}, bf16[32,4,16,128]{3,2,1,0:T(8,128)(2,1)S(1)}, u32[]{:S(2)}, u32[]{:S(2)}) collective-permute-start(bf16[32,4,16,128]{3,2,1,0:T(8,128)(2,1)} %get-tuple-element.30), channel_id=1, source_target_pairs={{0,32},{16,48},{32,0},{48,16},{1,33},{17,49},{33,1},{49,17},{2,34}... | collective-permute-start | bytes 1572872 | tf_op jit(solution)/shard_map/ppermute | solution.py:330
  60.1 1.0 copy-done
  61.1 1.5 join.2
  62.6 7.7 %all-to-all-start.1 = ((bf16[32,4,4,16,128]{4,3,2,1,0:T(8,128)(2,1)}), bf16[32,4,4,16,128]{4,3,2,1,0:T(8,128)(2,1)}, u32[]{:S(2)}, u32[]{:S(2)}) async-start(bf16[32,4,4,16,128]{4,3,2,1,0:T(8,128)(2,1)} %join.2), calls=%async_computation.1 | async-start | bytes 4194304 | tf_op jit(solution)/shard_map/all_to_all | solution.py:362
  70.2 3.0 %collective-permute-start.3 = (bf16[32,4,16,128]{3,2,1,0:T(8,128)(2,1)}, bf16[32,4,16,128]{3,2,1,0:T(8,128)(2,1)}, u32[]{:S(2)}, u32[]{:S(2)}) collective-permute-start(bf16[32,4,16,128]{3,2,1,0:T(8,128)(2,1)} %get-tuple-element.29), channel_id=1, source_target_pairs={{0,16},{16,32},{32,48},{48,0},{1,17},{17,33},{33,49},{49,1},{2,18}... | collective-permute-start | bytes 1572872 | tf_op jit(solution)/shard_map/ppermute | solution.py:330
  74.2 21.3 %collective-permute-done.4.refs_0_.refs_3_ = bf16[32,4,16,128]{3,2,1,0:T(8,128)(2,1)S(1)} collective-permute-done((bf16[32,4,16,128]{3,2,1,0:T(8,128)(2,1)}, bf16[32,4,16,128]{3,2,1,0:T(8,128)(2,1)S(1)}, u32[]{:S(2)}, u32[]{:S(2)}) %collective-permute-start.4) | collective-permute-done | bytes 524320 | tf_op jit(solution)/shard_map/ppermute | solution.py:330
  96.9 1.3 all-to-all-done.1.refs_1_
  98.9 8.2 %attend.2 = (bf16[16,4,32,128]{3,2,1,0:T(8,128)(2,1)}, bf16[16,4,32,128]{3,2,1,0:T(8,128)(2,1)}, bf16[16,4,32,128]{3,2,1,0:T(8,128)(2,1)}, bf16[16,4,32,128]{3,2,1,0:T(8,128)(2,1)}) custom-call(s32[3]{0:T(128)S(1)} %copy-done.20, bf16[32,4,4,16,128]{4,3,2,1,0:T(8,128)(2,1)} %all-to-all-done.1.refs_1_, f32[8,128]{1,0:T(8,128)S(1)} %copy-done.21), custom_call_target="tpu_custom_call" | custom-call | tf_op jit(solution)/shard_map/attend/pallas_call | solution.py:201
  107.1 6.9 %collective-permute-start.7 = (bf16[16,4,32,128]{3,2,1,0:T(8,128)(2,1)}, bf16[16,4,32,128]{3,2,1,0:T(8,128)(2,1)S(1)}, u32[]{:S(2)}, u32[]{:S(2)}) collective-permute-start(bf16[16,4,32,128]{3,2,1,0:T(8,128)(2,1)} %get-tuple-element.33), channel_id=1, source_target_pairs={{0,18},{2,16},{16,0},{18,2},{32,48},{34,50},{48,34},{50,32},{1,19}... | collective-permute-start | bytes 1572872 | tf_op jit(solution)/shard_map/ppermute | solution.py:346
  114.5 5.7 %collective-permute-start.6 = (bf16[16,4,32,128]{3,2,1,0:T(8,128)(2,1)}, bf16[16,4,32,128]{3,2,1,0:T(8,128)(2,1)S(1)}, u32[]{:S(2)}, u32[]{:S(2)}) collective-permute-start(bf16[16,4,32,128]{3,2,1,0:T(8,128)(2,1)} %get-tuple-element.32.refs_5_), channel_id=1, source_target_pairs={{0,2},{2,0},{16,16},{18,18},{32,32},{34,34},{48,50},{50,48},{1,3},... | collective-permute-start | bytes 1572872 | tf_op jit(solution)/shard_map/ppermute | solution.py:346
  120.2 7.8 %attend.3 = bf16[16,4,4,32,128]{4,3,2,1,0:T(8,128)(2,1)} custom-call(s32[3]{0:T(128)S(1)} %copy-done.20, bf16[32,4,16,128]{3,2,1,0:T(8,128)(2,1)S(1)} %copy-done.1, bf16[32,4,16,128]{3,2,1,0:T(8,128)(2,1)} %collective-permute-done.3.refs_2_, bf16[32,4,16,128]{3,2,1,0:T(8,128)(2,1)S(1)} %copy-done.12, ...), custom_call_target="tpu_custom_call" | custom-call | tf_op jit(solution)/shard_map/attend/pallas_call | solution.py:201
  128.1 6.5 %all-to-all-start.2 = ((bf16[16,4,4,32,128]{4,3,2,1,0:T(8,128)(2,1)}), bf16[16,4,4,32,128]{4,3,2,1,0:T(8,128)(2,1)}, u32[]{:S(2)}, u32[]{:S(2)}) async-start(bf16[16,4,4,32,128]{4,3,2,1,0:T(8,128)(2,1)} %attend.3), calls=%async_computation.2 | async-start | bytes 4194304 | tf_op jit(solution)/shard_map/all_to_all | solution.py:362
  134.6 14.6 %collective-permute-done.8.refs_2_ = bf16[16,4,32,128]{3,2,1,0:T(8,128)(2,1)S(1)} collective-permute-done((bf16[16,4,32,128]{3,2,1,0:T(8,128)(2,1)}, bf16[16,4,32,128]{3,2,1,0:T(8,128)(2,1)S(1)}, u32[]{:S(2)}, u32[]{:S(2)}) %collective-permute-start.8) | collective-permute-done | bytes 524320 | tf_op jit(solution)/shard_map/ppermute | solution.py:346
  149.2 9.7 %collective-permute-done.9.refs_3_ = bf16[16,4,32,128]{3,2,1,0:T(8,128)(2,1)S(1)} collective-permute-done((bf16[16,4,32,128]{3,2,1,0:T(8,128)(2,1)}, bf16[16,4,32,128]{3,2,1,0:T(8,128)(2,1)S(1)}, u32[]{:S(2)}, u32[]{:S(2)}) %collective-permute-start.9) | collective-permute-done | bytes 524320 | tf_op jit(solution)/shard_map/ppermute | solution.py:346
  161.1 3.0 %part.3 = (bf16[16,4,32,128]{3,2,1,0:T(8,128)(2,1)}, bf16[16,4,32,128]{3,2,1,0:T(8,128)(2,1)}, bf16[16,4,32,128]{3,2,1,0:T(8,128)(2,1)}, bf16[16,4,32,128]{3,2,1,0:T(8,128)(2,1)}) custom-call(bf16[16,4,4,32,128]{4,3,2,1,0:T(8,128)(2,1)} %all-to-all-done.2.in_ref, f32[8,128]{1,0:T(8,128)} %hold.6._), custom_call_target="tpu_custom_call" | custom-call | tf_op jit(solution)/shard_map/part/pallas_call | solution.py:245
  164.1 2.7 %collective-permute-start.11 = (bf16[16,4,32,128]{3,2,1,0:T(8,128)(2,1)}, bf16[16,4,32,128]{3,2,1,0:T(8,128)(2,1)S(1)}, u32[]{:S(2)}, u32[]{:S(2)}) collective-permute-start(bf16[16,4,32,128]{3,2,1,0:T(8,128)(2,1)} %get-tuple-element.37), channel_id=1, source_target_pairs={{0,18},{2,16},{16,0},{18,2},{32,48},{34,50},{48,34},{50,32},{1,19}... | collective-permute-start | bytes 1572872 | tf_op jit(solution)/shard_map/ppermute | solution.py:346
  166.8 2.5 %collective-permute-start.12 = (bf16[16,4,32,128]{3,2,1,0:T(8,128)(2,1)}, bf16[16,4,32,128]{3,2,1,0:T(8,128)(2,1)S(1)}, u32[]{:S(2)}, u32[]{:S(2)}) collective-permute-start(bf16[16,4,32,128]{3,2,1,0:T(8,128)(2,1)} %get-tuple-element.38), channel_id=1, source_target_pairs={{0,34},{2,32},{16,48},{18,50},{32,0},{34,2},{48,18},{50,16},{1,35}... | collective-permute-start | bytes 1572872 | tf_op jit(solution)/shard_map/ppermute | solution.py:346
  169.2 3.9 %collective-permute-start.10 = (bf16[16,4,32,128]{3,2,1,0:T(8,128)(2,1)}, bf16[16,4,32,128]{3,2,1,0:T(8,128)(2,1)}, u32[]{:S(2)}, u32[]{:S(2)}) collective-permute-start(bf16[16,4,32,128]{3,2,1,0:T(8,128)(2,1)} %get-tuple-element.36.refs_4_), channel_id=1, source_target_pairs={{0,2},{2,0},{16,16},{18,18},{32,32},{34,34},{48,50},{50,48},{1,3},... | collective-permute-start | bytes 1572872 | tf_op jit(solution)/shard_map/ppermute | solution.py:346
  173.2 1.0 copy-done.17
  174.3 1.5 join.3
  175.7 6.1 %all-to-all-start.3 = ((bf16[16,4,4,32,128]{4,3,2,1,0:T(8,128)(2,1)}), bf16[16,4,4,32,128]{4,3,2,1,0:T(8,128)(2,1)}, u32[]{:S(2)}, u32[]{:S(2)}) async-start(bf16[16,4,4,32,128]{4,3,2,1,0:T(8,128)(2,1)} %join.3), calls=%async_computation.3 | async-start | bytes 4194304 | tf_op jit(solution)/shard_map/all_to_all | solution.py:362
  181.8 22.9 %collective-permute-done.12.refs_2_.refs_5_ = bf16[16,4,32,128]{3,2,1,0:T(8,128)(2,1)S(1)} collective-permute-done((bf16[16,4,32,128]{3,2,1,0:T(8,128)(2,1)}, bf16[16,4,32,128]{3,2,1,0:T(8,128)(2,1)S(1)}, u32[]{:S(2)}, u32[]{:S(2)}) %collective-permute-start.12) | collective-permute-done | bytes 524320 | tf_op jit(solution)/shard_map/ppermute | solution.py:346
  204.7 8.5 %collective-permute-done.13.refs_3_.refs_6_ = bf16[16,4,32,128]{3,2,1,0:T(8,128)(2,1)} collective-permute-done((bf16[16,4,32,128]{3,2,1,0:T(8,128)(2,1)}, bf16[16,4,32,128]{3,2,1,0:T(8,128)(2,1)}, u32[]{:S(2)}, u32[]{:S(2)}) %collective-permute-start.13) | collective-permute-done | bytes 524320 | tf_op jit(solution)/shard_map/ppermute | solution.py:346
  213.8 5.3 %unpack.1 = (bf16[4,1024,128]{2,1,0:T(8,128)(2,1)}, bf16[4,1024,128]{2,1,0:T(8,128)(2,1)}, bf16[4,1024,128]{2,1,0:T(8,128)(2,1)}, bf16[4,1024,128]{2,1,0:T(8,128)(2,1)}) custom-call(s32[3]{0:T(128)} %pad_add_fusion.refs_0_, f32[8,128]{1,0:T(8,128)} %hold.7.refs_1_, bf16[16,4,4,32,128]{4,3,2,1,0:T(8,128)(2,1)} %all-to-all-done.3.refs_2_, ...), custom_call_target="tpu_custom_call" | custom-call | tf_op jit(solution)/shard_map/unpack/pallas_call | solution.py:314
  (66 shorter events, 10.1 us)
Async XLA Ops:
  5.3 18.0 %collective-permute-start = (bf16[32,4,16,128]{3,2,1,0:T(8,128)(2,1)}, bf16[32,4,16,128]{3,2,1,0:T(8,128)(2,1)S(1)}, u32[]{:S(2)}, u32[]{:S(2)}) collective-permute-start(bf16[32,4,16,128]{3,2,1,0:T(8,128)(2,1)} %bitcast.33), channel_id=1, source_target_pairs={{0,16},{16,32},{32,48},{48,0},{1,17},{17,33},{33,49},{49,1},{2,18}... | collective-permute-start | bytes 1572872 | tf_op jit(solution)/shard_map/ppermute | solution.py:330
  7.3 37.4 %collective-permute-start.1 = (bf16[32,4,16,128]{3,2,1,0:T(8,128)(2,1)}, bf16[32,4,16,128]{3,2,1,0:T(8,128)(2,1)S(1)}, u32[]{:S(2)}, u32[]{:S(2)}) collective-permute-start(bf16[32,4,16,128]{3,2,1,0:T(8,128)(2,1)} %bitcast.32), channel_id=1, source_target_pairs={{0,32},{16,48},{32,0},{48,16},{1,33},{17,49},{33,1},{49,17},{2,34}... | collective-permute-start | bytes 1572872 | tf_op jit(solution)/shard_map/ppermute | solution.py:330
  10.5 34.2 %collective-permute-start.2 = (bf16[32,4,16,128]{3,2,1,0:T(8,128)(2,1)}, bf16[32,4,16,128]{3,2,1,0:T(8,128)(2,1)S(1)}, u32[]{:S(2)}, u32[]{:S(2)}) collective-permute-start(bf16[32,4,16,128]{3,2,1,0:T(8,128)(2,1)} %bitcast.31), channel_id=1, source_target_pairs={{0,48},{16,0},{32,16},{48,32},{1,49},{17,1},{33,17},{49,33},{2,50}... | collective-permute-start | bytes 1572872 | tf_op jit(solution)/shard_map/ppermute | solution.py:330
  15.6 35.6 %all-to-all-start = ((bf16[32,4,4,16,128]{4,3,2,1,0:T(8,128)(2,1)}), bf16[32,4,4,16,128]{4,3,2,1,0:T(8,128)(2,1)}, u32[]{:S(2)}, u32[]{:S(2)}) async-start(bf16[32,4,4,16,128]{4,3,2,1,0:T(8,128)(2,1)} %bitcast.18), calls=%async_computation | async-start | bytes 4194304 | tf_op jit(solution)/shard_map/all_to_all | solution.py:362
  23.3 21.4 %copy-start.13 = (bf16[32,4,16,128]{3,2,1,0:T(8,128)(2,1)}, bf16[32,4,16,128]{3,2,1,0:T(8,128)(2,1)S(1)}, u32[]{:S(2)}) copy-start(bf16[32,4,16,128]{3,2,1,0:T(8,128)(2,1)S(1)} %collective-permute-done.refs_0_.refs_1_) | copy-start | bytes 1572868
  46.9 13.2 %copy-start.2 = (bf16[32,4,4,4,128]{4,3,2,1,0:T(4,128)(2,1)S(1)}, bf16[32,4,4,4,128]{4,3,2,1,0:T(4,128)(2,1)}, u32[]{:S(2)}) copy-start(bf16[32,4,4,4,128]{4,3,2,1,0:T(4,128)(2,1)} %get-tuple-element.24) | copy-start | bytes 1572868
  46.9 13.2 %copy-start.14 = (bf16[32,4,16,128]{3,2,1,0:T(8,128)(2,1)S(1)}, bf16[32,4,16,128]{3,2,1,0:T(8,128)(2,1)}, u32[]{:S(2)}) copy-start(bf16[32,4,16,128]{3,2,1,0:T(8,128)(2,1)} %copy-done.13) | copy-start | bytes 1572868
  46.9 13.2 %copy-start.16 = (bf16[32,4,16,128]{3,2,1,0:T(8,128)(2,1)S(1)}, bf16[32,4,16,128]{3,2,1,0:T(8,128)(2,1)}, u32[]{:S(2)}) copy-start(bf16[32,4,16,128]{3,2,1,0:T(8,128)(2,1)} %copy-done.15) | copy-start | bytes 1572868
  46.9 13.2 %copy-start.19 = (bf16[32,4,16,128]{3,2,1,0:T(8,128)(2,1)S(1)}, bf16[32,4,16,128]{3,2,1,0:T(8,128)(2,1)}, u32[]{:S(2)}) copy-start(bf16[32,4,16,128]{3,2,1,0:T(8,128)(2,1)} %copy-done.18) | copy-start | bytes 1572868
  54.1 41.4 %collective-permute-start.4 = (bf16[32,4,16,128]{3,2,1,0:T(8,128)(2,1)}, bf16[32,4,16,128]{3,2,1,0:T(8,128)(2,1)S(1)}, u32[]{:S(2)}, u32[]{:S(2)}) collective-permute-start(bf16[32,4,16,128]{3,2,1,0:T(8,128)(2,1)} %get-tuple-element.30), channel_id=1, source_target_pairs={{0,32},{16,48},{32,0},{48,16},{1,33},{17,49},{33,1},{49,17},{2,34}... | collective-permute-start | bytes 1572872 | tf_op jit(solution)/shard_map/ppermute | solution.py:330
  62.6 35.6 %all-to-all-start.1 = ((bf16[32,4,4,16,128]{4,3,2,1,0:T(8,128)(2,1)}), bf16[32,4,4,16,128]{4,3,2,1,0:T(8,128)(2,1)}, u32[]{:S(2)}, u32[]{:S(2)}) async-start(bf16[32,4,4,16,128]{4,3,2,1,0:T(8,128)(2,1)} %join.2), calls=%async_computation.1 | async-start | bytes 4194304 | tf_op jit(solution)/shard_map/all_to_all | solution.py:362
  70.2 44.3 %collective-permute-start.3 = (bf16[32,4,16,128]{3,2,1,0:T(8,128)(2,1)}, bf16[32,4,16,128]{3,2,1,0:T(8,128)(2,1)}, u32[]{:S(2)}, u32[]{:S(2)}) collective-permute-start(bf16[32,4,16,128]{3,2,1,0:T(8,128)(2,1)} %get-tuple-element.29), channel_id=1, source_target_pairs={{0,16},{16,32},{32,48},{48,0},{1,17},{17,33},{33,49},{49,1},{2,18}... | collective-permute-start | bytes 1572872 | tf_op jit(solution)/shard_map/ppermute | solution.py:330
  73.3 46.9 %collective-permute-start.5 = (bf16[32,4,16,128]{3,2,1,0:T(8,128)(2,1)}, bf16[32,4,16,128]{3,2,1,0:T(8,128)(2,1)}, u32[]{:S(2)}, u32[]{:S(2)}) collective-permute-start(bf16[32,4,16,128]{3,2,1,0:T(8,128)(2,1)} %get-tuple-element.31), channel_id=1, source_target_pairs={{0,48},{16,0},{32,16},{48,32},{1,49},{17,1},{33,17},{49,33},{2,50}... | collective-permute-start | bytes 1572872 | tf_op jit(solution)/shard_map/ppermute | solution.py:330
  96.9 23.3 %copy-start.1 = (bf16[32,4,16,128]{3,2,1,0:T(8,128)(2,1)S(1)}, bf16[32,4,16,128]{3,2,1,0:T(8,128)(2,1)}, u32[]{:S(2)}) copy-start(bf16[32,4,16,128]{3,2,1,0:T(8,128)(2,1)} %get-tuple-element.28.refs_4_.refs_1_) | copy-start | bytes 1572868
  96.9 23.3 %copy-start.12 = (bf16[32,4,16,128]{3,2,1,0:T(8,128)(2,1)S(1)}, bf16[32,4,16,128]{3,2,1,0:T(8,128)(2,1)}, u32[]{:S(2)}) copy-start(bf16[32,4,16,128]{3,2,1,0:T(8,128)(2,1)} %copy-done.11) | copy-start | bytes 1572868
  107.1 27.5 %collective-permute-start.7 = (bf16[16,4,32,128]{3,2,1,0:T(8,128)(2,1)}, bf16[16,4,32,128]{3,2,1,0:T(8,128)(2,1)S(1)}, u32[]{:S(2)}, u32[]{:S(2)}) collective-permute-start(bf16[16,4,32,128]{3,2,1,0:T(8,128)(2,1)} %get-tuple-element.33), channel_id=1, source_target_pairs={{0,18},{2,16},{16,0},{18,2},{32,48},{34,50},{48,34},{50,32},{1,19}... | collective-permute-start | bytes 1572872 | tf_op jit(solution)/shard_map/ppermute | solution.py:346
  114.0 35.3 %collective-permute-start.8 = (bf16[16,4,32,128]{3,2,1,0:T(8,128)(2,1)}, bf16[16,4,32,128]{3,2,1,0:T(8,128)(2,1)S(1)}, u32[]{:S(2)}, u32[]{:S(2)}) collective-permute-start(bf16[16,4,32,128]{3,2,1,0:T(8,128)(2,1)} %get-tuple-element.34), channel_id=1, source_target_pairs={{0,34},{2,32},{16,48},{18,50},{32,0},{34,2},{48,18},{50,16},{1,35}... | collective-permute-start | bytes 1572872 | tf_op jit(solution)/shard_map/ppermute | solution.py:346
  114.5 44.4 %collective-permute-start.9 = (bf16[16,4,32,128]{3,2,1,0:T(8,128)(2,1)}, bf16[16,4,32,128]{3,2,1,0:T(8,128)(2,1)S(1)}, u32[]{:S(2)}, u32[]{:S(2)}) collective-permute-start(bf16[16,4,32,128]{3,2,1,0:T(8,128)(2,1)} %get-tuple-element.35), channel_id=1, source_target_pairs={{0,50},{2,48},{16,32},{18,34},{32,16},{34,18},{48,2},{50,0},{1,51}... | collective-permute-start | bytes 1572872 | tf_op jit(solution)/shard_map/ppermute | solution.py:346
  114.5 44.4 %collective-permute-start.6 = (bf16[16,4,32,128]{3,2,1,0:T(8,128)(2,1)}, bf16[16,4,32,128]{3,2,1,0:T(8,128)(2,1)S(1)}, u32[]{:S(2)}, u32[]{:S(2)}) collective-permute-start(bf16[16,4,32,128]{3,2,1,0:T(8,128)(2,1)} %get-tuple-element.32.refs_5_), channel_id=1, source_target_pairs={{0,2},{2,0},{16,16},{18,18},{32,32},{34,34},{48,50},{50,48},{1,3},... | collective-permute-start | bytes 1572872 | tf_op jit(solution)/shard_map/ppermute | solution.py:346
  128.1 33.0 %all-to-all-start.2 = ((bf16[16,4,4,32,128]{4,3,2,1,0:T(8,128)(2,1)}), bf16[16,4,4,32,128]{4,3,2,1,0:T(8,128)(2,1)}, u32[]{:S(2)}, u32[]{:S(2)}) async-start(bf16[16,4,4,32,128]{4,3,2,1,0:T(8,128)(2,1)} %attend.3), calls=%async_computation.2 | async-start | bytes 4194304 | tf_op jit(solution)/shard_map/all_to_all | solution.py:362
  134.6 24.3 %copy-start.3 = (bf16[16,4,32,128]{3,2,1,0:T(8,128)(2,1)}, bf16[16,4,32,128]{3,2,1,0:T(8,128)(2,1)S(1)}, u32[]{:S(2)}) copy-start(bf16[16,4,32,128]{3,2,1,0:T(8,128)(2,1)S(1)} %collective-permute-done.7.refs_1_) | copy-start | bytes 1572868
  149.2 9.7 %copy-start.5 = (bf16[16,4,32,128]{3,2,1,0:T(8,128)(2,1)}, bf16[16,4,32,128]{3,2,1,0:T(8,128)(2,1)S(1)}, u32[]{:S(2)}) copy-start(bf16[16,4,32,128]{3,2,1,0:T(8,128)(2,1)S(1)} %collective-permute-done.8.refs_2_) | copy-start | bytes 1572868
  161.0 12.1 %copy-start.4 = (bf16[16,4,32,128]{3,2,1,0:T(8,128)(2,1)S(1)}, bf16[16,4,32,128]{3,2,1,0:T(8,128)(2,1)}, u32[]{:S(2)}) copy-start(bf16[16,4,32,128]{3,2,1,0:T(8,128)(2,1)} %copy-done.3) | copy-start | bytes 1572868
  161.0 12.1 %copy-start.6 = (bf16[16,4,32,128]{3,2,1,0:T(8,128)(2,1)S(1)}, bf16[16,4,32,128]{3,2,1,0:T(8,128)(2,1)}, u32[]{:S(2)}) copy-start(bf16[16,4,32,128]{3,2,1,0:T(8,128)(2,1)} %copy-done.5) | copy-start | bytes 1572868
  161.0 12.1 %copy-start.8 = (bf16[16,4,32,128]{3,2,1,0:T(8,128)(2,1)S(1)}, bf16[16,4,32,128]{3,2,1,0:T(8,128)(2,1)}, u32[]{:S(2)}) copy-start(bf16[16,4,32,128]{3,2,1,0:T(8,128)(2,1)} %copy-done.7) | copy-start | bytes 1572868
  161.0 12.2 %copy-start.10 = (bf16[16,4,32,128]{3,2,1,0:T(8,128)(2,1)S(1)}, bf16[16,4,32,128]{3,2,1,0:T(8,128)(2,1)}, u32[]{:S(2)}) copy-start(bf16[16,4,32,128]{3,2,1,0:T(8,128)(2,1)} %copy-done.9) | copy-start | bytes 1572868
  164.1 17.7 %collective-permute-start.11 = (bf16[16,4,32,128]{3,2,1,0:T(8,128)(2,1)}, bf16[16,4,32,128]{3,2,1,0:T(8,128)(2,1)S(1)}, u32[]{:S(2)}, u32[]{:S(2)}) collective-permute-start(bf16[16,4,32,128]{3,2,1,0:T(8,128)(2,1)} %get-tuple-element.37), channel_id=1, source_target_pairs={{0,18},{2,16},{16,0},{18,2},{32,48},{34,50},{48,34},{50,32},{1,19}... | collective-permute-start | bytes 1572872 | tf_op jit(solution)/shard_map/ppermute | solution.py:346
  166.8 37.9 %collective-permute-start.12 = (bf16[16,4,32,128]{3,2,1,0:T(8,128)(2,1)}, bf16[16,4,32,128]{3,2,1,0:T(8,128)(2,1)S(1)}, u32[]{:S(2)}, u32[]{:S(2)}) collective-permute-start(bf16[16,4,32,128]{3,2,1,0:T(8,128)(2,1)} %get-tuple-element.38), channel_id=1, source_target_pairs={{0,34},{2,32},{16,48},{18,50},{32,0},{34,2},{48,18},{50,16},{1,35}... | collective-permute-start | bytes 1572872 | tf_op jit(solution)/shard_map/ppermute | solution.py:346
  169.2 43.9 %collective-permute-start.13 = (bf16[16,4,32,128]{3,2,1,0:T(8,128)(2,1)}, bf16[16,4,32,128]{3,2,1,0:T(8,128)(2,1)}, u32[]{:S(2)}, u32[]{:S(2)}) collective-permute-start(bf16[16,4,32,128]{3,2,1,0:T(8,128)(2,1)} %get-tuple-element.39), channel_id=1, source_target_pairs={{0,50},{2,48},{16,32},{18,34},{32,16},{34,18},{48,2},{50,0},{1,51}... | collective-permute-start | bytes 1572872 | tf_op jit(solution)/shard_map/ppermute | solution.py:346
  169.2 43.9 %collective-permute-start.10 = (bf16[16,4,32,128]{3,2,1,0:T(8,128)(2,1)}, bf16[16,4,32,128]{3,2,1,0:T(8,128)(2,1)}, u32[]{:S(2)}, u32[]{:S(2)}) collective-permute-start(bf16[16,4,32,128]{3,2,1,0:T(8,128)(2,1)} %get-tuple-element.36.refs_4_), channel_id=1, source_target_pairs={{0,2},{2,0},{16,16},{18,18},{32,32},{34,34},{48,50},{50,48},{1,3},... | collective-permute-start | bytes 1572872 | tf_op jit(solution)/shard_map/ppermute | solution.py:346
  175.7 38.1 %all-to-all-start.3 = ((bf16[16,4,4,32,128]{4,3,2,1,0:T(8,128)(2,1)}), bf16[16,4,4,32,128]{4,3,2,1,0:T(8,128)(2,1)}, u32[]{:S(2)}, u32[]{:S(2)}) async-start(bf16[16,4,4,32,128]{4,3,2,1,0:T(8,128)(2,1)} %join.3), calls=%async_computation.3 | async-start | bytes 4194304 | tf_op jit(solution)/shard_map/all_to_all | solution.py:362
  181.8 31.4 %copy-start.22 = (bf16[16,4,32,128]{3,2,1,0:T(8,128)(2,1)}, bf16[16,4,32,128]{3,2,1,0:T(8,128)(2,1)S(1)}, u32[]{:S(2)}) copy-start(bf16[16,4,32,128]{3,2,1,0:T(8,128)(2,1)S(1)} %collective-permute-done.11.refs_1_.refs_4_) | copy-start | bytes 1572868
  (10 other events, 17.1 us)

commit v7 on v6

--- a/solution.py
+++ b/solution.py
@@ -15,6 +15,7 @@
 F32 = jnp.float32
 BF16 = jnp.bfloat16
 LIMIT = 24 * 2**20
+SMALL = 6 * 2**20
 ALL = 58 * 2**20
 LOG2E = 1.4426950408889634
 ANY = pl.BlockSpec(memory_space=pl.ANY)
@@ -69,13 +70,20 @@
     )
 
 
+def sending(made, out_refs, split, shift, sems):
+    to = out_refs[shift] if split else out_refs[0].at[:, shift]
+    copy = pltpu.make_async_copy(made.at[shift], to, sems.at[shift])
+    copy.start()
+    return copy
+
+
 def pack_kernel(sizes, chunk, split, place_ref, *refs):
     ys, _, z0s, xs, _, cores = sizes
-    *refs, held, sems = refs
+    *refs, held, made, sems, out_sems = refs
     far_refs, out_refs = refs[:4], refs[4 + (not split) :]
     rows = far_refs[0].shape[0]
     my_z, my_w = place_ref[0] * z0s + place_ref[1], place_ref[2]
-    copies = []
+    copies, sent = [], []
     for shift in range(ZS):
         z = (my_z + shift) % ZS
         quarter, slot = other_run(my_w, z) * cores, z // 2 * 2 + chunk
@@ -96,15 +104,14 @@
                 for core in range(cores):
                     for array in range(4):
                         for row in range(rows):
-                            tile = held[shift, array, row, core, y, x]
                             to = (y * xs + x) * cores + core
-                            if split:
-                                out_refs[shift][to, array, row] = tile
-                            else:
-                                out_refs[0][to, shift, array, row] = tile
+                            made[shift, to, array, row] = held[shift, array, row, core, y, x]
             return carry
 
         lax.fori_loop(0, ys, step, 0)
+        sent.append(sending(made, out_refs, split, shift, out_sems))
+    for copy in sent:
+        copy.wait()
 
 
 def pack(arrays, place, sizes, chunk, split, after=()):
@@ -119,10 +126,12 @@
         lambda *refs: pack_kernel(sizes, chunk, split, *refs),
         out_shape=shapes,
         in_specs=[SCALARS] + [FAR] * 4 + [ANY] * len(after),
-        out_specs=[WHOLE] * len(shapes),
+        out_specs=[FAR] * len(shapes),
         scratch_shapes=[
             pltpu.VMEM((ZS, 4, rows, cores, ys, xs, inner, feature), BF16),
+            pltpu.VMEM((ZS, first, *tail), BF16),
             pltpu.SemaphoreType.DMA((ZS, 4)),
+            pltpu.SemaphoreType.DMA((ZS,)),
         ],
         compiler_params=pltpu.CompilerParams(vmem_limit_bytes=ALL),
         name="pack",
@@ -132,7 +141,8 @@
 def attend_kernel(sizes, pieces, split, place_ref, *refs):
     ys, _, z0s, xs, _, cores = sizes
     in_refs, refs = refs[:pieces], refs[pieces + 1 :]
-    *out_refs, wide_in, wide_out = refs
+    *out_refs, wide_in, wide_out, made, out_sems = refs
+    sent = []
     sources = in_refs[0].shape[0]
     arrays, tile, feature = in_refs[0].shape[-3:]
     inner = tile // 4
@@ -178,14 +188,13 @@
                 for core in range(cores):
                     spot = pl.ds(pl.multiple_of(core * rows * inner + start, tile), tile)
                     block = wide_out[array, spot, :].astype(BF16)
-                    to = slice(core * tile, (core + 1) * tile)
-                    if split:
-                        out_refs[shift][at, array, to] = block
-                    else:
-                        out_refs[0][at, shift, array, to] = block
+                    made[shift, at, array, core * tile : (core + 1) * tile] = block
             return carry
 
         lax.fori_loop(0, ys * xs, narrow, 0, unroll=2)
+        sent.append(sending(made, out_refs, split, shift, out_sems))
+    for copy in sent:
+        copy.wait()
 
 
 def attend(pieces, place, sizes, split, after):
@@ -202,55 +211,85 @@
         lambda *refs: attend_kernel(sizes, len(pieces), split, *refs),
         out_shape=shapes,
         in_specs=[SCALARS] + [WHOLE] * len(pieces) + [ANY],
-        out_specs=[WHOLE] * len(shapes),
-        scratch_shapes=[pltpu.VMEM((arrays, rows * columns, feature), F32)] * 2,
+        out_specs=[FAR] * len(shapes),
+        scratch_shapes=[
+            pltpu.VMEM((arrays, rows * columns, feature), F32),
+            pltpu.VMEM((arrays, rows * columns, feature), F32),
+            pltpu.VMEM((ZS, ys * xs, *tail), BF16),
+            pltpu.SemaphoreType.DMA((ZS,)),
+        ],
         compiler_params=pltpu.CompilerParams(vmem_limit_bytes=LIMIT),
         cost_estimate=pl.CostEstimate(flops=0, bytes_accessed=0, transcendentals=0),
         name="attend",
     )(place, *pieces, after)
 
 
+def relay(sources, targets, held, sems):
+    first = held.shape[1]
+    cuts = [0, first // 2, first] if first > 1 else [0, first]
+    steps = []
+    for at, (source, target) in enumerate(zip(sources, targets)):
+        for part_at in range(len(cuts) - 1):
+            some = slice(cuts[part_at], cuts[part_at + 1])
+            spot, sem = held.at[at, some], sems.at[at, part_at]
+            into = pltpu.make_async_copy(source.at[some], spot, sem.at[0])
+            out = pltpu.make_async_copy(spot, target.at[some], sem.at[1])
+            into.start()
+            steps.append((into, out))
+    for into, out in steps:
+        into.wait()
+        out.start()
+    for _, out in steps:
+        out.wait()
+
+
+def relay_scratch(count, shape):
+    return [pltpu.VMEM((count, *shape), BF16), pltpu.SemaphoreType.DMA((count, 2, 2))]
+
+
 def join_kernel(*refs):
-    *in_refs, _, out_ref = refs
-    for side, ref in enumerate(in_refs):
-        out_ref[:, side] = ref[...]
+    *in_refs, _, out_ref, held, sems = refs
+    relay(in_refs, [out_ref.at[:, k] for k in range(len(in_refs))], held, sems)
 
 
 def join(pieces, after):
     first, *tail = pieces[0].shape
+    count = len(pieces)
     return pl.pallas_call(
         join_kernel,
-        out_shape=jax.ShapeDtypeStruct((first, len(pieces), *tail), BF16),
-        in_specs=[WHOLE] * len(pieces) + [ANY],
-        out_specs=WHOLE,
-        compiler_params=pltpu.CompilerParams(vmem_limit_bytes=LIMIT),
+        out_shape=jax.ShapeDtypeStruct((first, count, *tail), BF16),
+        in_specs=[ANY] * (count + 1),
+        out_specs=ANY,
+        scratch_shapes=relay_scratch(count, (first, *tail)),
+        compiler_params=pltpu.CompilerParams(vmem_limit_bytes=SMALL),
         name="join",
     )(*pieces, after)
 
 
-def part_kernel(in_ref, _, *refs):
-    *out_refs, sems = refs
-    copies = [
-        pltpu.make_async_copy(in_ref.at[:, shift], ref, sems.at[shift])
-        for shift, ref in enumerate(out_refs)
-    ]
-    for copy in copies:
-        copy.start()
-    for copy in copies:
-        copy.wait()
-
-
-def part(joined, after):
-    first, shifts, *tail = joined.shape
-    return pl.pallas_call(
-        part_kernel,
-        out_shape=[jax.ShapeDtypeStruct((first, *tail), BF16)] * shifts,
-        in_specs=[FAR, ANY],
-        out_specs=[WHOLE] * shifts,
-        scratch_shapes=[pltpu.SemaphoreType.DMA((shifts,))],
-        compiler_params=pltpu.CompilerParams(vmem_limit_bytes=ALL),
+def part_kernel(picks, in_ref, _, *refs):
+    *out_refs, held, sems = refs
+    relay([in_ref.at[:, pick] for pick in picks], out_refs, held, sems)
+
+
+def part(joined, after, picks):
+    first, _, *tail = joined.shape
+    count = len(picks)
+    return pl.pallas_call(
+        lambda *refs: part_kernel(picks, *refs),
+        out_shape=[jax.ShapeDtypeStruct((first, *tail), BF16)] * count,
+        in_specs=[ANY] * 2,
+        out_specs=[ANY] * count,
+        scratch_shapes=relay_scratch(count, (first, *tail)),
+        compiler_params=pltpu.CompilerParams(vmem_limit_bytes=SMALL),
         name="part",
     )(joined, after)
+
+
+def parts(joined, after, early):
+    late = [k for k in range(ZS) if k not in early]
+    made = part(joined, after, early)
+    found = dict(zip(early, made)) | dict(zip(late, part(joined, made[0], late)))
+    return [found[k] for k in range(ZS)]
 
 
 def hold_kernel(*refs):
@@ -263,6 +302,7 @@
         out_shape=jax.ShapeDtypeStruct((8, 128), F32),
         in_specs=[ANY] * len(waited),
         out_specs=WHOLE,
+        compiler_params=pltpu.CompilerParams(vmem_limit_bytes=SMALL),
         cost_estimate=pl.CostEstimate(flops=flops, bytes_accessed=4096, transcendentals=0),
         name="hold",
     )(*waited)
@@ -364,18 +404,18 @@
     packed = [flat(p) for p in pack(arrays, place, sizes, 0, True)]
     second = flat(pack(arrays, place, sizes, 1, False, packed[:1])[0])
     first = z_in(packed)
-    pieces = part(across(second, NEAR), hold(first[1:]))
+    pieces = parts(across(second, NEAR), hold(first[1:]), [2])
     second = z_in(pieces)
-    first = across(join(first, pieces[0]), NEAR)
+    first = across(join(first, pieces[2]), NEAR)
 
     done = attend([first], place, sizes, True, hold(second[2:3]))
     first = z_out(done)
     second = attend(second, place, sizes, False, done[0])[0]
-    pieces = part(across(second, ("y", "x")), hold(first))
+    pieces = parts(across(second, ("y", "x")), hold(first), [1, 2])
     second = z_out(pieces)
-    first = across(join(first, pieces[0]), ("y", "x"))
-
-    results = unpack(first, second, place, sizes, rows, hold(second))
+    first = across(join(first, pieces[1]), ("y", "x"))
+
+    results = unpack(first, second, place, sizes, rows, hold(second[1:3]))
     return tuple(r.reshape(rows, columns // (ws * cores), ws * cores, feature) for r in results)
 
 

time: 221 us -> 212 us (0.959)
  local copies, waits for them, and re-layouts: 6.77 us -> 2.22 us
  Pallas kernels: 40.6 us -> 38.1 us
    unnamed x48 -> x14, local copies, waits for them, and re-layouts: 6.77 us -> 2.22 us
    ppermute x8, waiting for transfers between devices: 55.6 us -> 51.8 us  [z_out(): lax.ppermute(pieces[k], ('z1', 'z0', 'w'), pairs(k))]
    ppermute x8, starting transfers between devices: 22.1 us -> 24.8 us  [z_out(): lax.ppermute(pieces[k], ('z1', 'z0', 'w'), pairs(k))]
    all_to_all x4, waiting for transfers between devices: 5.62 us -> 8.08 us  [across(): return lax.all_to_all(whole, names, 0, 0, tiled=True)]
    pallas_call x4, Pallas kernels: 2.37 us -> 0.01 us  [hold(): pl.pallas_call(hold_kernel, out_shape=jax.ShapeDtypeStruct((8, 128), F32)...]
    pallas_call x4 -> x6, Pallas kernels: 8.84 us -> 10.5 us  [the longest x4 7.26 us: part(): pl.pallas_call(lambda *refs: part_kernel(picks, *refs), out_shape=[jax.Sh...]
  transfers between devices with their start and end apart: 18 -> 18, of which waited for: 8 -> 10; matrix products, arithmetic and copies ran while one was open for 0% -> 0% of each run, Pallas kernels for 12% -> 12%
where the time goes in v7:
time: 212 us; the launch traced here: 210 us
  waiting for transfers between devices  102 us (48%)
  starting transfers between devices  67.3 us (32%)
  Pallas kernels  38.1 us (18%)
  local copies, waits for them, and re-layouts  2.22 us (1%)
    ppermute x8, waiting for transfers between devices, z_out(): lax.ppermute(pieces[k], ('z1', 'z0', 'w'), pairs(k))  51.8 us
    ppermute x6, waiting for transfers between devices, z_in(): lax.ppermute(pieces[k], ('z1', 'z0'), [(z, (z + k) % ZS) for z in range(Z...  41.7 us
    all_to_all x4, starting transfers between devices, across(): return lax.all_to_all(whole, names, 0, 0, tiled=True)  27.4 us
    ppermute x8, starting transfers between devices, z_out(): lax.ppermute(pieces[k], ('z1', 'z0', 'w'), pairs(k))  24.8 us
    pallas_call x2, Pallas kernels, attend(): pl.pallas_call(lambda *refs: attend_kernel(sizes, len(pieces), split, *re...  15.1 us
    ppermute x6, starting transfers between devices, z_in(): lax.ppermute(pieces[k], ('z1', 'z0'), [(z, (z + k) % ZS) for z in range(Z...  15.1 us
    all_to_all x4, waiting for transfers between devices, across(): return lax.all_to_all(whole, names, 0, 0, tiled=True)  8.08 us
    pallas_call x4, Pallas kernels, part(): pl.pallas_call(lambda *refs: part_kernel(picks, *refs), out_shape=[jax.Sh...  7.26 us
  transfers between devices with their start and end apart: 18, of which 10 were waited for; matrix products, arithmetic and copies ran while one was open for 0% of the time, Pallas kernels for 12%

profile of v7, /device:TPU:2, one launch (start us, length us, event | category | flops | bytes accessed | tf_op | source)
XLA Modules:
  0.0 210.5 jit_solution(1707993797234149116)
XLA Ops:
  1.2 3.6 %pack.2 = (bf16[32,4,4,4,128]{4,3,2,1,0:T(4,128)(2,1)}, bf16[32,4,4,4,128]{4,3,2,1,0:T(4,128)(2,1)}, bf16[32,4,4,4,128]{4,3,2,1,0:T(4,128)(2,1)}, bf16[32,4,4,4,128]{4,3,2,1,0:T(4,128)(2,1)}) custom-call(s32[3]{0:T(128)} %pad_add_fusion.refs_0_, bf16[4,4,4,4,4,4,128]{6,5,4,3,2,1,0:T(4,128)(2,1)} %bitcast.19, bf16[4,4,4,4,4,4,128]{6,5,4,3,2,1,0:T(4,128)(2,1)} %bitcast.21, ...), custom_call_target="tpu_custom_call" | custom-call | tf_op jit(solution)/shard_map/pack/pallas_call | solution.py:125
  4.8 2.0 collective-permute-start
  6.8 3.3 %collective-permute-start.1 = (bf16[32,4,16,128]{3,2,1,0:T(8,128)(2,1)}, bf16[32,4,16,128]{3,2,1,0:T(8,128)(2,1)S(1)}, u32[]{:S(2)}, u32[]{:S(2)}) collective-permute-start(bf16[32,4,16,128]{3,2,1,0:T(8,128)(2,1)} %bitcast.32), channel_id=1, source_target_pairs={{0,32},{16,48},{32,0},{48,16},{1,33},{17,49},{33,1},{49,17},{2,34}... | collective-permute-start | bytes 1572872 | tf_op jit(solution)/shard_map/ppermute | solution.py:370
  11.1 3.6 %pack.3 = bf16[32,4,4,4,4,128]{5,4,3,2,1,0:T(4,128)(2,1)} custom-call(s32[3]{0:T(128)} %pad_add_fusion.refs_0_, bf16[4,4,4,4,4,4,128]{6,5,4,3,2,1,0:T(4,128)(2,1)} %bitcast.20, bf16[4,4,4,4,4,4,128]{6,5,4,3,2,1,0:T(4,128)(2,1)} %bitcast.22, bf16[4,4,4,4,4,4,128]{6,5,4,3,2,1,0:T(4,128)(2,1)} %bitcast.24, bf16[4,4,4,4,4,4,128]{6,5,4,3,2,1,0:T(4,128)(2,1)} %bitcast.26, ...), custom_call_target="tpu_custom_call" | custom-call | tf_op jit(solution)/shard_map/pack/pallas_call | solution.py:125
  14.7 7.7 %all-to-all-start = ((bf16[32,4,4,16,128]{4,3,2,1,0:T(8,128)(2,1)}), bf16[32,4,4,16,128]{4,3,2,1,0:T(8,128)(2,1)}, u32[]{:S(2)}, u32[]{:S(2)}) async-start(bf16[32,4,4,16,128]{4,3,2,1,0:T(8,128)(2,1)} %bitcast.18), calls=%async_computation | async-start | bytes 4194304 | tf_op jit(solution)/shard_map/all_to_all | solution.py:402
  22.6 21.6 %collective-permute-done.1.refs_1_.refs_2_ = bf16[32,4,16,128]{3,2,1,0:T(8,128)(2,1)S(1)} collective-permute-done((bf16[32,4,16,128]{3,2,1,0:T(8,128)(2,1)}, bf16[32,4,16,128]{3,2,1,0:T(8,128)(2,1)S(1)}, u32[]{:S(2)}, u32[]{:S(2)}) %collective-permute-start.1) | collective-permute-done | bytes 524320 | tf_op jit(solution)/shard_map/ppermute | solution.py:370
  44.2 6.1 %all-to-all-done.refs_0_ = bf16[32,4,4,16,128]{4,3,2,1,0:T(8,128)(2,1)} async-done(((bf16[32,4,4,16,128]{4,3,2,1,0:T(8,128)(2,1)}), bf16[32,4,4,16,128]{4,3,2,1,0:T(8,128)(2,1)}, u32[]{:S(2)}, u32[]{:S(2)}) %all-to-all-start) | async-done | bytes 2097184 | tf_op jit(solution)/shard_map/all_to_all | solution.py:402
  51.4 4.9 %collective-permute-start.4 = (bf16[32,4,16,128]{3,2,1,0:T(8,128)(2,1)S(1)}, bf16[32,4,16,128]{3,2,1,0:T(8,128)(2,1)S(1)}, u32[]{:S(2)}, u32[]{:S(2)}) collective-permute-start(bf16[32,4,16,128]{3,2,1,0:T(8,128)(2,1)S(1)} %part.4.refs_1_.refs_4_), channel_id=1, source_target_pairs={{0,32},{16,48},{32,0},{48,16},{1,33},{17,49},{33,1},{49,17},{2,34}... | collective-permute-start | bytes 1572872 | tf_op jit(solution)/shard_map/ppermute | solution.py:370
  56.3 1.6 join.2
  57.9 7.7 %all-to-all-start.1 = ((bf16[32,4,4,16,128]{4,3,2,1,0:T(8,128)(2,1)}), bf16[32,4,4,16,128]{4,3,2,1,0:T(8,128)(2,1)}, u32[]{:S(2)}, u32[]{:S(2)}) async-start(bf16[32,4,4,16,128]{4,3,2,1,0:T(8,128)(2,1)} %join.2), calls=%async_computation.1 | async-start | bytes 4194304 | tf_op jit(solution)/shard_map/all_to_all | solution.py:402
  65.6 2.2 %part.5 = (bf16[32,4,16,128]{3,2,1,0:T(8,128)(2,1)S(1)}, bf16[32,4,16,128]{3,2,1,0:T(8,128)(2,1)}, bf16[32,4,16,128]{3,2,1,0:T(8,128)(2,1)}) custom-call(bf16[32,4,4,16,128]{4,3,2,1,0:T(8,128)(2,1)} %all-to-all-done.refs_0_, bf16[32,4,16,128]{3,2,1,0:T(8,128)(2,1)S(1)} %part.4.refs_1_.refs_4_), custom_call_target="tpu_custom_call" | custom-call | tf_op jit(solution)/shard_map/part/pallas_call | solution.py:277
  67.8 2.2 %collective-permute-start.3 = (bf16[32,4,16,128]{3,2,1,0:T(8,128)(2,1)}, bf16[32,4,16,128]{3,2,1,0:T(8,128)(2,1)}, u32[]{:S(2)}, u32[]{:S(2)}) collective-permute-start(bf16[32,4,16,128]{3,2,1,0:T(8,128)(2,1)} %get-tuple-element.28), channel_id=1, source_target_pairs={{0,16},{16,32},{32,48},{48,0},{1,17},{17,33},{33,49},{49,1},{2,18}... | collective-permute-start | bytes 1572872 | tf_op jit(solution)/shard_map/ppermute | solution.py:370
  70.0 1.7 collective-permute-start.5
  71.7 19.8 %collective-permute-done.4.refs_0_.refs_3_ = bf16[32,4,16,128]{3,2,1,0:T(8,128)(2,1)S(1)} collective-permute-done((bf16[32,4,16,128]{3,2,1,0:T(8,128)(2,1)S(1)}, bf16[32,4,16,128]{3,2,1,0:T(8,128)(2,1)S(1)}, u32[]{:S(2)}, u32[]{:S(2)}) %collective-permute-start.4) | collective-permute-done | bytes 524320 | tf_op jit(solution)/shard_map/ppermute | solution.py:370
  91.5 2.0 all-to-all-done.1.refs_1_
  93.5 7.7 %attend.2 = (bf16[16,4,32,128]{3,2,1,0:T(8,128)(2,1)}, bf16[16,4,32,128]{3,2,1,0:T(8,128)(2,1)}, bf16[16,4,32,128]{3,2,1,0:T(8,128)(2,1)}, bf16[16,4,32,128]{3,2,1,0:T(8,128)(2,1)}) custom-call(s32[3]{0:T(128)S(1)} %copy-done.5, bf16[32,4,4,16,128]{4,3,2,1,0:T(8,128)(2,1)} %all-to-all-done.1.refs_1_, f32[8,128]{1,0:T(8,128)S(1)} %hold.5.refs_2_), custom_call_target="tpu_custom_call" | custom-call | tf_op jit(solution)/shard_map/attend/pallas_call | solution.py:210
  101.3 6.2 %collective-permute-start.7 = (bf16[16,4,32,128]{3,2,1,0:T(8,128)(2,1)}, bf16[16,4,32,128]{3,2,1,0:T(8,128)(2,1)S(1)}, u32[]{:S(2)}, u32[]{:S(2)}) collective-permute-start(bf16[16,4,32,128]{3,2,1,0:T(8,128)(2,1)} %get-tuple-element.31), channel_id=1, source_target_pairs={{0,18},{2,16},{16,0},{18,2},{32,48},{34,50},{48,34},{50,32},{1,19}... | collective-permute-start | bytes 1572872 | tf_op jit(solution)/shard_map/ppermute | solution.py:386
  108.8 5.3 %collective-permute-start.6 = (bf16[16,4,32,128]{3,2,1,0:T(8,128)(2,1)}, bf16[16,4,32,128]{3,2,1,0:T(8,128)(2,1)S(1)}, u32[]{:S(2)}, u32[]{:S(2)}) collective-permute-start(bf16[16,4,32,128]{3,2,1,0:T(8,128)(2,1)} %get-tuple-element.30.refs_5_), channel_id=1, source_target_pairs={{0,2},{2,0},{16,16},{18,18},{32,32},{34,34},{48,50},{50,48},{1,3},... | collective-permute-start | bytes 1572872 | tf_op jit(solution)/shard_map/ppermute | solution.py:386
  114.1 7.4 %attend.3 = bf16[16,4,4,32,128]{4,3,2,1,0:T(8,128)(2,1)} custom-call(s32[3]{0:T(128)S(1)} %copy-done.5, bf16[32,4,16,128]{3,2,1,0:T(8,128)(2,1)S(1)} %get-tuple-element.27.refs_1_, bf16[32,4,16,128]{3,2,1,0:T(8,128)(2,1)} %collective-permute-done.3.refs_2_, bf16[32,4,16,128]{3,2,1,0:T(8,128)(2,1)S(1)} %collective-permute-done.4.refs_0_.refs_3_, ...), custom_call_target="tpu_custom_call" | custom-call | tf_op jit(solution)/shard_map/attend/pallas_call | solution.py:210
  121.5 6.5 %all-to-all-start.2 = ((bf16[16,4,4,32,128]{4,3,2,1,0:T(8,128)(2,1)}), bf16[16,4,4,32,128]{4,3,2,1,0:T(8,128)(2,1)}, u32[]{:S(2)}, u32[]{:S(2)}) async-start(bf16[16,4,4,32,128]{4,3,2,1,0:T(8,128)(2,1)} %attend.3), calls=%async_computation.2 | async-start | bytes 4194304 | tf_op jit(solution)/shard_map/all_to_all | solution.py:402
  128.0 14.7 %collective-permute-done.8.refs_2_ = bf16[16,4,32,128]{3,2,1,0:T(8,128)(2,1)S(1)} collective-permute-done((bf16[16,4,32,128]{3,2,1,0:T(8,128)(2,1)}, bf16[16,4,32,128]{3,2,1,0:T(8,128)(2,1)S(1)}, u32[]{:S(2)}, u32[]{:S(2)}) %collective-permute-start.8) | collective-permute-done | bytes 524320 | tf_op jit(solution)/shard_map/ppermute | solution.py:386
  142.7 10.1 %collective-permute-done.9.refs_3_ = bf16[16,4,32,128]{3,2,1,0:T(8,128)(2,1)S(1)} collective-permute-done((bf16[16,4,32,128]{3,2,1,0:T(8,128)(2,1)}, bf16[16,4,32,128]{3,2,1,0:T(8,128)(2,1)S(1)}, u32[]{:S(2)}, u32[]{:S(2)}) %collective-permute-start.9) | collective-permute-done | bytes 524320 | tf_op jit(solution)/shard_map/ppermute | solution.py:386
  153.6 2.0 part.6
  155.7 2.4 %collective-permute-start.11 = (bf16[16,4,32,128]{3,2,1,0:T(8,128)(2,1)}, bf16[16,4,32,128]{3,2,1,0:T(8,128)(2,1)S(1)}, u32[]{:S(2)}, u32[]{:S(2)}) collective-permute-start(bf16[16,4,32,128]{3,2,1,0:T(8,128)(2,1)} %get-tuple-element.35), channel_id=1, source_target_pairs={{0,34},{2,32},{16,48},{18,50},{32,0},{34,2},{48,18},{50,16},{1,35}... | collective-permute-start | bytes 1572872 | tf_op jit(solution)/shard_map/ppermute | solution.py:386
  158.1 3.1 %collective-permute-start.10 = (bf16[16,4,32,128]{3,2,1,0:T(8,128)(2,1)S(1)}, bf16[16,4,32,128]{3,2,1,0:T(8,128)(2,1)S(1)}, u32[]{:S(2)}, u32[]{:S(2)}) collective-permute-start(bf16[16,4,32,128]{3,2,1,0:T(8,128)(2,1)S(1)} %get-tuple-element.34.refs_4_.refs_1_), channel_id=1, source_target_pairs={{0,18},{2,16},{16,0},{18,2},{32,48},{34,50},{48,34},{50,32},{1,19}... | collective-permute-start | bytes 1572872 | tf_op jit(solution)/shard_map/ppermute | solution.py:386
  162.9 5.5 %all-to-all-start.3 = ((bf16[16,4,4,32,128]{4,3,2,1,0:T(8,128)(2,1)}), bf16[16,4,4,32,128]{4,3,2,1,0:T(8,128)(2,1)}, u32[]{:S(2)}, u32[]{:S(2)}) async-start(bf16[16,4,4,32,128]{4,3,2,1,0:T(8,128)(2,1)} %join.3), calls=%async_computation.3 | async-start | bytes 4194304 | tf_op jit(solution)/shard_map/all_to_all | solution.py:402
  168.4 2.0 part.7
  170.4 5.6 %collective-permute-start.12 = (bf16[16,4,32,128]{3,2,1,0:T(8,128)(2,1)}, bf16[16,4,32,128]{3,2,1,0:T(8,128)(2,1)}, u32[]{:S(2)}, u32[]{:S(2)}) collective-permute-start(bf16[16,4,32,128]{3,2,1,0:T(8,128)(2,1)} %get-tuple-element.36), channel_id=1, source_target_pairs={{0,2},{2,0},{16,16},{18,18},{32,32},{34,34},{48,50},{50,48},{1,3},... | collective-permute-start | bytes 1572872 | tf_op jit(solution)/shard_map/ppermute | solution.py:386
  176.8 6.3 %collective-permute-done.10.refs_0_.refs_4_ = bf16[16,4,32,128]{3,2,1,0:T(8,128)(2,1)S(1)} collective-permute-done((bf16[16,4,32,128]{3,2,1,0:T(8,128)(2,1)S(1)}, bf16[16,4,32,128]{3,2,1,0:T(8,128)(2,1)S(1)}, u32[]{:S(2)}, u32[]{:S(2)}) %collective-permute-start.10) | collective-permute-done | bytes 524320 | tf_op jit(solution)/shard_map/ppermute | solution.py:386
  184.5 11.0 %collective-permute-done.12.refs_3_ = bf16[16,4,32,128]{3,2,1,0:T(8,128)(2,1)} collective-permute-done((bf16[16,4,32,128]{3,2,1,0:T(8,128)(2,1)}, bf16[16,4,32,128]{3,2,1,0:T(8,128)(2,1)}, u32[]{:S(2)}, u32[]{:S(2)}) %collective-permute-start.12) | collective-permute-done | bytes 524320 | tf_op jit(solution)/shard_map/ppermute | solution.py:386
  195.5 9.7 %collective-permute-done.13.refs_6_ = bf16[16,4,32,128]{3,2,1,0:T(8,128)(2,1)} collective-permute-done((bf16[16,4,32,128]{3,2,1,0:T(8,128)(2,1)}, bf16[16,4,32,128]{3,2,1,0:T(8,128)(2,1)}, u32[]{:S(2)}, u32[]{:S(2)}) %collective-permute-start.13) | collective-permute-done | bytes 524320 | tf_op jit(solution)/shard_map/ppermute | solution.py:386
  205.2 5.3 %unpack.1 = (bf16[4,1024,128]{2,1,0:T(8,128)(2,1)}, bf16[4,1024,128]{2,1,0:T(8,128)(2,1)}, bf16[4,1024,128]{2,1,0:T(8,128)(2,1)}, bf16[4,1024,128]{2,1,0:T(8,128)(2,1)}) custom-call(s32[3]{0:T(128)} %pad_add_fusion.refs_0_, f32[8,128]{1,0:T(8,128)} %copy-done.6, bf16[16,4,4,32,128]{4,3,2,1,0:T(8,128)(2,1)} %all-to-all-done.3.refs_2_, ...), custom_call_target="tpu_custom_call" | custom-call | tf_op jit(solution)/shard_map/unpack/pallas_call | solution.py:354
  (34 shorter events, 8.9 us)
Async XLA Ops:
  4.8 17.8 %collective-permute-start = (bf16[32,4,16,128]{3,2,1,0:T(8,128)(2,1)}, bf16[32,4,16,128]{3,2,1,0:T(8,128)(2,1)S(1)}, u32[]{:S(2)}, u32[]{:S(2)}) collective-permute-start(bf16[32,4,16,128]{3,2,1,0:T(8,128)(2,1)} %bitcast.33), channel_id=1, source_target_pairs={{0,16},{16,32},{32,48},{48,0},{1,17},{17,33},{33,49},{49,1},{2,18}... | collective-permute-start | bytes 1572872 | tf_op jit(solution)/shard_map/ppermute | solution.py:370
  6.8 37.4 %collective-permute-start.1 = (bf16[32,4,16,128]{3,2,1,0:T(8,128)(2,1)}, bf16[32,4,16,128]{3,2,1,0:T(8,128)(2,1)S(1)}, u32[]{:S(2)}, u32[]{:S(2)}) collective-permute-start(bf16[32,4,16,128]{3,2,1,0:T(8,128)(2,1)} %bitcast.32), channel_id=1, source_target_pairs={{0,32},{16,48},{32,0},{48,16},{1,33},{17,49},{33,1},{49,17},{2,34}... | collective-permute-start | bytes 1572872 | tf_op jit(solution)/shard_map/ppermute | solution.py:370
  10.1 34.2 %collective-permute-start.2 = (bf16[32,4,16,128]{3,2,1,0:T(8,128)(2,1)}, bf16[32,4,16,128]{3,2,1,0:T(8,128)(2,1)S(1)}, u32[]{:S(2)}, u32[]{:S(2)}) collective-permute-start(bf16[32,4,16,128]{3,2,1,0:T(8,128)(2,1)} %bitcast.31), channel_id=1, source_target_pairs={{0,48},{16,0},{32,16},{48,32},{1,49},{17,1},{33,17},{49,33},{2,50}... | collective-permute-start | bytes 1572872 | tf_op jit(solution)/shard_map/ppermute | solution.py:370
  14.7 35.6 %all-to-all-start = ((bf16[32,4,4,16,128]{4,3,2,1,0:T(8,128)(2,1)}), bf16[32,4,4,16,128]{4,3,2,1,0:T(8,128)(2,1)}, u32[]{:S(2)}, u32[]{:S(2)}) async-start(bf16[32,4,4,16,128]{4,3,2,1,0:T(8,128)(2,1)} %bitcast.18), calls=%async_computation | async-start | bytes 4194304 | tf_op jit(solution)/shard_map/all_to_all | solution.py:402
  44.2 12.0 %copy-start = (bf16[32,4,4,4,128]{4,3,2,1,0:T(4,128)(2,1)S(1)}, bf16[32,4,4,4,128]{4,3,2,1,0:T(4,128)(2,1)}, u32[]{:S(2)}) copy-start(bf16[32,4,4,4,128]{4,3,2,1,0:T(4,128)(2,1)} %get-tuple-element.23) | copy-start | bytes 1572868
  51.4 40.1 %collective-permute-start.4 = (bf16[32,4,16,128]{3,2,1,0:T(8,128)(2,1)S(1)}, bf16[32,4,16,128]{3,2,1,0:T(8,128)(2,1)S(1)}, u32[]{:S(2)}, u32[]{:S(2)}) collective-permute-start(bf16[32,4,16,128]{3,2,1,0:T(8,128)(2,1)S(1)} %part.4.refs_1_.refs_4_), channel_id=1, source_target_pairs={{0,32},{16,48},{32,0},{48,16},{1,33},{17,49},{33,1},{49,17},{2,34}... | collective-permute-start | bytes 1572872 | tf_op jit(solution)/shard_map/ppermute | solution.py:370
  57.9 35.6 %all-to-all-start.1 = ((bf16[32,4,4,16,128]{4,3,2,1,0:T(8,128)(2,1)}), bf16[32,4,4,16,128]{4,3,2,1,0:T(8,128)(2,1)}, u32[]{:S(2)}, u32[]{:S(2)}) async-start(bf16[32,4,4,16,128]{4,3,2,1,0:T(8,128)(2,1)} %join.2), calls=%async_computation.1 | async-start | bytes 4194304 | tf_op jit(solution)/shard_map/all_to_all | solution.py:402
  67.8 41.0 %collective-permute-start.3 = (bf16[32,4,16,128]{3,2,1,0:T(8,128)(2,1)}, bf16[32,4,16,128]{3,2,1,0:T(8,128)(2,1)}, u32[]{:S(2)}, u32[]{:S(2)}) collective-permute-start(bf16[32,4,16,128]{3,2,1,0:T(8,128)(2,1)} %get-tuple-element.28), channel_id=1, source_target_pairs={{0,16},{16,32},{32,48},{48,0},{1,17},{17,33},{33,49},{49,1},{2,18}... | collective-permute-start | bytes 1572872 | tf_op jit(solution)/shard_map/ppermute | solution.py:370
  70.0 44.1 %collective-permute-start.5 = (bf16[32,4,16,128]{3,2,1,0:T(8,128)(2,1)}, bf16[32,4,16,128]{3,2,1,0:T(8,128)(2,1)}, u32[]{:S(2)}, u32[]{:S(2)}) collective-permute-start(bf16[32,4,16,128]{3,2,1,0:T(8,128)(2,1)} %get-tuple-element.29), channel_id=1, source_target_pairs={{0,48},{16,0},{32,16},{48,32},{1,49},{17,1},{33,17},{49,33},{2,50}... | collective-permute-start | bytes 1572872 | tf_op jit(solution)/shard_map/ppermute | solution.py:370
  91.5 2.0 copy-start.5
  101.3 26.7 %collective-permute-start.7 = (bf16[16,4,32,128]{3,2,1,0:T(8,128)(2,1)}, bf16[16,4,32,128]{3,2,1,0:T(8,128)(2,1)S(1)}, u32[]{:S(2)}, u32[]{:S(2)}) collective-permute-start(bf16[16,4,32,128]{3,2,1,0:T(8,128)(2,1)} %get-tuple-element.31), channel_id=1, source_target_pairs={{0,18},{2,16},{16,0},{18,2},{32,48},{34,50},{48,34},{50,32},{1,19}... | collective-permute-start | bytes 1572872 | tf_op jit(solution)/shard_map/ppermute | solution.py:386
  107.5 35.3 %collective-permute-start.8 = (bf16[16,4,32,128]{3,2,1,0:T(8,128)(2,1)}, bf16[16,4,32,128]{3,2,1,0:T(8,128)(2,1)S(1)}, u32[]{:S(2)}, u32[]{:S(2)}) collective-permute-start(bf16[16,4,32,128]{3,2,1,0:T(8,128)(2,1)} %get-tuple-element.32), channel_id=1, source_target_pairs={{0,34},{2,32},{16,48},{18,50},{32,0},{34,2},{48,18},{50,16},{1,35}... | collective-permute-start | bytes 1572872 | tf_op jit(solution)/shard_map/ppermute | solution.py:386
  108.8 44.0 %collective-permute-start.9 = (bf16[16,4,32,128]{3,2,1,0:T(8,128)(2,1)}, bf16[16,4,32,128]{3,2,1,0:T(8,128)(2,1)S(1)}, u32[]{:S(2)}, u32[]{:S(2)}) collective-permute-start(bf16[16,4,32,128]{3,2,1,0:T(8,128)(2,1)} %get-tuple-element.33), channel_id=1, source_target_pairs={{0,50},{2,48},{16,32},{18,34},{32,16},{34,18},{48,2},{50,0},{1,51}... | collective-permute-start | bytes 1572872 | tf_op jit(solution)/shard_map/ppermute | solution.py:386
  108.8 44.0 %collective-permute-start.6 = (bf16[16,4,32,128]{3,2,1,0:T(8,128)(2,1)}, bf16[16,4,32,128]{3,2,1,0:T(8,128)(2,1)S(1)}, u32[]{:S(2)}, u32[]{:S(2)}) collective-permute-start(bf16[16,4,32,128]{3,2,1,0:T(8,128)(2,1)} %get-tuple-element.30.refs_5_), channel_id=1, source_target_pairs={{0,2},{2,0},{16,16},{18,18},{32,32},{34,34},{48,50},{50,48},{1,3},... | collective-permute-start | bytes 1572872 | tf_op jit(solution)/shard_map/ppermute | solution.py:386
  121.5 32.1 %all-to-all-start.2 = ((bf16[16,4,4,32,128]{4,3,2,1,0:T(8,128)(2,1)}), bf16[16,4,4,32,128]{4,3,2,1,0:T(8,128)(2,1)}, u32[]{:S(2)}, u32[]{:S(2)}) async-start(bf16[16,4,4,32,128]{4,3,2,1,0:T(8,128)(2,1)} %attend.3), calls=%async_computation.2 | async-start | bytes 4194304 | tf_op jit(solution)/shard_map/all_to_all | solution.py:402
  152.8 0.8 copy-start.2
  153.6 7.6 %copy-start.3 = (bf16[16,4,32,128]{3,2,1,0:T(8,128)(2,1)S(1)}, bf16[16,4,32,128]{3,2,1,0:T(8,128)(2,1)}, u32[]{:S(2)}) copy-start(bf16[16,4,32,128]{3,2,1,0:T(8,128)(2,1)} %copy-done.2) | copy-start | bytes 1572868
  155.7 21.1 %collective-permute-start.11 = (bf16[16,4,32,128]{3,2,1,0:T(8,128)(2,1)}, bf16[16,4,32,128]{3,2,1,0:T(8,128)(2,1)S(1)}, u32[]{:S(2)}, u32[]{:S(2)}) collective-permute-start(bf16[16,4,32,128]{3,2,1,0:T(8,128)(2,1)} %get-tuple-element.35), channel_id=1, source_target_pairs={{0,34},{2,32},{16,48},{18,50},{32,0},{34,2},{48,18},{50,16},{1,35}... | collective-permute-start | bytes 1572872 | tf_op jit(solution)/shard_map/ppermute | solution.py:386
  158.1 25.0 %collective-permute-start.10 = (bf16[16,4,32,128]{3,2,1,0:T(8,128)(2,1)S(1)}, bf16[16,4,32,128]{3,2,1,0:T(8,128)(2,1)S(1)}, u32[]{:S(2)}, u32[]{:S(2)}) collective-permute-start(bf16[16,4,32,128]{3,2,1,0:T(8,128)(2,1)S(1)} %get-tuple-element.34.refs_4_.refs_1_), channel_id=1, source_target_pairs={{0,18},{2,16},{16,0},{18,2},{32,48},{34,50},{48,34},{50,32},{1,19}... | collective-permute-start | bytes 1572872 | tf_op jit(solution)/shard_map/ppermute | solution.py:386
  162.9 42.4 %all-to-all-start.3 = ((bf16[16,4,4,32,128]{4,3,2,1,0:T(8,128)(2,1)}), bf16[16,4,4,32,128]{4,3,2,1,0:T(8,128)(2,1)}, u32[]{:S(2)}, u32[]{:S(2)}) async-start(bf16[16,4,4,32,128]{4,3,2,1,0:T(8,128)(2,1)} %join.3), calls=%async_computation.3 | async-start | bytes 4194304 | tf_op jit(solution)/shard_map/all_to_all | solution.py:402
  170.4 25.1 %collective-permute-start.12 = (bf16[16,4,32,128]{3,2,1,0:T(8,128)(2,1)}, bf16[16,4,32,128]{3,2,1,0:T(8,128)(2,1)}, u32[]{:S(2)}, u32[]{:S(2)}) collective-permute-start(bf16[16,4,32,128]{3,2,1,0:T(8,128)(2,1)} %get-tuple-element.36), channel_id=1, source_target_pairs={{0,2},{2,0},{16,16},{18,18},{32,32},{34,34},{48,50},{50,48},{1,3},... | collective-permute-start | bytes 1572872 | tf_op jit(solution)/shard_map/ppermute | solution.py:386
  176.0 29.2 %collective-permute-start.13 = (bf16[16,4,32,128]{3,2,1,0:T(8,128)(2,1)}, bf16[16,4,32,128]{3,2,1,0:T(8,128)(2,1)}, u32[]{:S(2)}, u32[]{:S(2)}) collective-permute-start(bf16[16,4,32,128]{3,2,1,0:T(8,128)(2,1)} %get-tuple-element.37), channel_id=1, source_target_pairs={{0,50},{2,48},{16,32},{18,34},{32,16},{34,18},{48,2},{50,0},{1,51}... | collective-permute-start | bytes 1572872 | tf_op jit(solution)/shard_map/ppermute | solution.py:386
  176.8 6.3 %copy-start.1 = (bf16[16,4,32,128]{3,2,1,0:T(8,128)(2,1)}, bf16[16,4,32,128]{3,2,1,0:T(8,128)(2,1)S(1)}, u32[]{:S(2)}) copy-start(bf16[16,4,32,128]{3,2,1,0:T(8,128)(2,1)S(1)} %collective-permute-done.11.refs_1_.refs_5_) | copy-start | bytes 1572868
  183.1 0.8 copy-start.4
  183.9 0.6 copy-start.6

commit v8 on v7

--- a/solution.py
+++ b/solution.py
@@ -213,8 +213,8 @@
         in_specs=[SCALARS] + [WHOLE] * len(pieces) + [ANY],
         out_specs=[FAR] * len(shapes),
         scratch_shapes=[
-            pltpu.VMEM((arrays, rows * columns, feature), F32),
-            pltpu.VMEM((arrays, rows * columns, feature), F32),
+            pltpu.VMEM((arrays, rows * columns + 8, feature), F32),
+            pltpu.VMEM((arrays, rows * columns + 8, feature), F32),
             pltpu.VMEM((ZS, ys * xs, *tail), BF16),
             pltpu.SemaphoreType.DMA((ZS,)),
         ],
@@ -359,7 +359,7 @@
         + [pl.BlockSpec((xs, ZS, arrays, tile, feature), lambda i: (i, 0, 0, 0, 0))]
         + [pl.BlockSpec((xs, arrays, tile, feature), lambda i: (i, 0, 0, 0))] * ZS,
         out_specs=[pl.BlockSpec((rows, width // ys, feature), lambda i: (0, i, 0))] * arrays,
-        scratch_shapes=[pltpu.VMEM((2 * arrays * tile * ws, feature), F32)],
+        scratch_shapes=[pltpu.VMEM((2 * arrays * tile * ws + 8, feature), F32)],
         compiler_params=pltpu.CompilerParams(vmem_limit_bytes=ALL),
         name="unpack",
     )(place, after, first, *second)
@@ -411,11 +411,11 @@
     done = attend([first], place, sizes, True, hold(second[2:3]))
     first = z_out(done)
     second = attend(second, place, sizes, False, done[0])[0]
-    pieces = parts(across(second, ("y", "x")), hold(first), [1, 2])
+    pieces = parts(across(second, ("y", "x")), hold(first), [0, 3])
     second = z_out(pieces)
-    first = across(join(first, pieces[1]), ("y", "x"))
-
-    results = unpack(first, second, place, sizes, rows, hold(second[1:3]))
+    first = across(join(first, pieces[0]), ("y", "x"))
+
+    results = unpack(first, second, place, sizes, rows, hold([second[k] for k in [0, 3]]))
     return tuple(r.reshape(rows, columns // (ws * cores), ws * cores, feature) for r in results)
 
 

time: 212 us -> 211 us (level)
  no operation moved by 1% of the time
where the time goes in v8:
time: 211 us; the launch traced here: 209 us
  waiting for transfers between devices  101 us (48%)
  starting transfers between devices  66.5 us (32%)
  Pallas kernels  38 us (18%)
  local copies, waits for them, and re-layouts  2.38 us (1%)
    ppermute x8, waiting for transfers between devices, z_out(): lax.ppermute(pieces[k], ('z1', 'z0', 'w'), pairs(k))  51.1 us
    ppermute x6, waiting for transfers between devices, z_in(): lax.ppermute(pieces[k], ('z1', 'z0'), [(z, (z + k) % ZS) for z in range(Z...  41.7 us
    all_to_all x4, starting transfers between devices, across(): return lax.all_to_all(whole, names, 0, 0, tiled=True)  28.5 us
    ppermute x8, starting transfers between devices, z_out(): lax.ppermute(pieces[k], ('z1', 'z0', 'w'), pairs(k))  23 us
    pallas_call x2, Pallas kernels, attend(): pl.pallas_call(lambda *refs: attend_kernel(sizes, len(pieces), split, *re...  15.1 us
    ppermute x6, starting transfers between devices, z_in(): lax.ppermute(pieces[k], ('z1', 'z0'), [(z, (z + k) % ZS) for z in range(Z...  15.1 us
    all_to_all x4, waiting for transfers between devices, across(): return lax.all_to_all(whole, names, 0, 0, tiled=True)  8.08 us
    pallas_call x4, Pallas kernels, part(): pl.pallas_call(lambda *refs: part_kernel(picks, *refs), out_shape=[jax.Sh...  7.26 us
  transfers between devices with their start and end apart: 18, of which 10 were waited for; matrix products, arithmetic and copies ran while one was open for 0% of the time, Pallas kernels for 12%

profile of v8, /device:TPU:2, one launch (start us, length us, event | category | flops | bytes accessed | tf_op | source)
XLA Modules:
  0.0 209.2 jit_solution(13682704866674815513)
XLA Ops:
  1.2 3.6 %pack.2 = (bf16[32,4,4,4,128]{4,3,2,1,0:T(4,128)(2,1)}, bf16[32,4,4,4,128]{4,3,2,1,0:T(4,128)(2,1)}, bf16[32,4,4,4,128]{4,3,2,1,0:T(4,128)(2,1)}, bf16[32,4,4,4,128]{4,3,2,1,0:T(4,128)(2,1)}) custom-call(s32[3]{0:T(128)} %pad_add_fusion.refs_0_, bf16[4,4,4,4,4,4,128]{6,5,4,3,2,1,0:T(4,128)(2,1)} %bitcast.19, bf16[4,4,4,4,4,4,128]{6,5,4,3,2,1,0:T(4,128)(2,1)} %bitcast.21, ...), custom_call_target="tpu_custom_call" | custom-call | tf_op jit(solution)/shard_map/pack/pallas_call | solution.py:125
  4.8 2.0 collective-permute-start
  6.8 3.3 %collective-permute-start.1 = (bf16[32,4,16,128]{3,2,1,0:T(8,128)(2,1)}, bf16[32,4,16,128]{3,2,1,0:T(8,128)(2,1)S(1)}, u32[]{:S(2)}, u32[]{:S(2)}) collective-permute-start(bf16[32,4,16,128]{3,2,1,0:T(8,128)(2,1)} %bitcast.32), channel_id=1, source_target_pairs={{0,32},{16,48},{32,0},{48,16},{1,33},{17,49},{33,1},{49,17},{2,34}... | collective-permute-start | bytes 1572872 | tf_op jit(solution)/shard_map/ppermute | solution.py:370
  11.1 3.6 %pack.3 = bf16[32,4,4,4,4,128]{5,4,3,2,1,0:T(4,128)(2,1)} custom-call(s32[3]{0:T(128)} %pad_add_fusion.refs_0_, bf16[4,4,4,4,4,4,128]{6,5,4,3,2,1,0:T(4,128)(2,1)} %bitcast.20, bf16[4,4,4,4,4,4,128]{6,5,4,3,2,1,0:T(4,128)(2,1)} %bitcast.22, bf16[4,4,4,4,4,4,128]{6,5,4,3,2,1,0:T(4,128)(2,1)} %bitcast.24, bf16[4,4,4,4,4,4,128]{6,5,4,3,2,1,0:T(4,128)(2,1)} %bitcast.26, ...), custom_call_target="tpu_custom_call" | custom-call | tf_op jit(solution)/shard_map/pack/pallas_call | solution.py:125
  14.7 7.7 %all-to-all-start = ((bf16[32,4,4,16,128]{4,3,2,1,0:T(8,128)(2,1)}), bf16[32,4,4,16,128]{4,3,2,1,0:T(8,128)(2,1)}, u32[]{:S(2)}, u32[]{:S(2)}) async-start(bf16[32,4,4,16,128]{4,3,2,1,0:T(8,128)(2,1)} %bitcast.18), calls=%async_computation | async-start | bytes 4194304 | tf_op jit(solution)/shard_map/all_to_all | solution.py:402
  22.6 21.6 %collective-permute-done.1.refs_1_.refs_2_ = bf16[32,4,16,128]{3,2,1,0:T(8,128)(2,1)S(1)} collective-permute-done((bf16[32,4,16,128]{3,2,1,0:T(8,128)(2,1)}, bf16[32,4,16,128]{3,2,1,0:T(8,128)(2,1)S(1)}, u32[]{:S(2)}, u32[]{:S(2)}) %collective-permute-start.1) | collective-permute-done | bytes 524320 | tf_op jit(solution)/shard_map/ppermute | solution.py:370
  44.2 6.1 %all-to-all-done.refs_0_ = bf16[32,4,4,16,128]{4,3,2,1,0:T(8,128)(2,1)} async-done(((bf16[32,4,4,16,128]{4,3,2,1,0:T(8,128)(2,1)}), bf16[32,4,4,16,128]{4,3,2,1,0:T(8,128)(2,1)}, u32[]{:S(2)}, u32[]{:S(2)}) %all-to-all-start) | async-done | bytes 2097184 | tf_op jit(solution)/shard_map/all_to_all | solution.py:402
  51.4 4.9 %collective-permute-start.4 = (bf16[32,4,16,128]{3,2,1,0:T(8,128)(2,1)S(1)}, bf16[32,4,16,128]{3,2,1,0:T(8,128)(2,1)S(1)}, u32[]{:S(2)}, u32[]{:S(2)}) collective-permute-start(bf16[32,4,16,128]{3,2,1,0:T(8,128)(2,1)S(1)} %part.4.refs_1_.refs_4_), channel_id=1, source_target_pairs={{0,32},{16,48},{32,0},{48,16},{1,33},{17,49},{33,1},{49,17},{2,34}... | collective-permute-start | bytes 1572872 | tf_op jit(solution)/shard_map/ppermute | solution.py:370
  56.3 1.6 join.2
  57.9 7.7 %all-to-all-start.1 = ((bf16[32,4,4,16,128]{4,3,2,1,0:T(8,128)(2,1)}), bf16[32,4,4,16,128]{4,3,2,1,0:T(8,128)(2,1)}, u32[]{:S(2)}, u32[]{:S(2)}) async-start(bf16[32,4,4,16,128]{4,3,2,1,0:T(8,128)(2,1)} %join.2), calls=%async_computation.1 | async-start | bytes 4194304 | tf_op jit(solution)/shard_map/all_to_all | solution.py:402
  65.6 2.2 %part.5 = (bf16[32,4,16,128]{3,2,1,0:T(8,128)(2,1)S(1)}, bf16[32,4,16,128]{3,2,1,0:T(8,128)(2,1)}, bf16[32,4,16,128]{3,2,1,0:T(8,128)(2,1)}) custom-call(bf16[32,4,4,16,128]{4,3,2,1,0:T(8,128)(2,1)} %all-to-all-done.refs_0_, bf16[32,4,16,128]{3,2,1,0:T(8,128)(2,1)S(1)} %part.4.refs_1_.refs_4_), custom_call_target="tpu_custom_call" | custom-call | tf_op jit(solution)/shard_map/part/pallas_call | solution.py:277
  67.8 2.2 %collective-permute-start.3 = (bf16[32,4,16,128]{3,2,1,0:T(8,128)(2,1)}, bf16[32,4,16,128]{3,2,1,0:T(8,128)(2,1)}, u32[]{:S(2)}, u32[]{:S(2)}) collective-permute-start(bf16[32,4,16,128]{3,2,1,0:T(8,128)(2,1)} %get-tuple-element.28), channel_id=1, source_target_pairs={{0,16},{16,32},{32,48},{48,0},{1,17},{17,33},{33,49},{49,1},{2,18}... | collective-permute-start | bytes 1572872 | tf_op jit(solution)/shard_map/ppermute | solution.py:370
  70.0 1.7 collective-permute-start.5
  71.7 19.8 %collective-permute-done.4.refs_0_.refs_3_ = bf16[32,4,16,128]{3,2,1,0:T(8,128)(2,1)S(1)} collective-permute-done((bf16[32,4,16,128]{3,2,1,0:T(8,128)(2,1)S(1)}, bf16[32,4,16,128]{3,2,1,0:T(8,128)(2,1)S(1)}, u32[]{:S(2)}, u32[]{:S(2)}) %collective-permute-start.4) | collective-permute-done | bytes 524320 | tf_op jit(solution)/shard_map/ppermute | solution.py:370
  91.5 2.0 all-to-all-done.1.refs_1_
  93.5 7.7 %attend.2 = (bf16[16,4,32,128]{3,2,1,0:T(8,128)(2,1)}, bf16[16,4,32,128]{3,2,1,0:T(8,128)(2,1)}, bf16[16,4,32,128]{3,2,1,0:T(8,128)(2,1)}, bf16[16,4,32,128]{3,2,1,0:T(8,128)(2,1)}) custom-call(s32[3]{0:T(128)S(1)} %copy-done.5, bf16[32,4,4,16,128]{4,3,2,1,0:T(8,128)(2,1)} %all-to-all-done.1.refs_1_, f32[8,128]{1,0:T(8,128)S(1)} %hold.5.refs_2_), custom_call_target="tpu_custom_call" | custom-call | tf_op jit(solution)/shard_map/attend/pallas_call | solution.py:210
  101.3 6.2 %collective-permute-start.7 = (bf16[16,4,32,128]{3,2,1,0:T(8,128)(2,1)}, bf16[16,4,32,128]{3,2,1,0:T(8,128)(2,1)S(1)}, u32[]{:S(2)}, u32[]{:S(2)}) collective-permute-start(bf16[16,4,32,128]{3,2,1,0:T(8,128)(2,1)} %get-tuple-element.31), channel_id=1, source_target_pairs={{0,18},{2,16},{16,0},{18,2},{32,48},{34,50},{48,34},{50,32},{1,19}... | collective-permute-start | bytes 1572872 | tf_op jit(solution)/shard_map/ppermute | solution.py:386
  108.8 5.3 %collective-permute-start.6 = (bf16[16,4,32,128]{3,2,1,0:T(8,128)(2,1)}, bf16[16,4,32,128]{3,2,1,0:T(8,128)(2,1)S(1)}, u32[]{:S(2)}, u32[]{:S(2)}) collective-permute-start(bf16[16,4,32,128]{3,2,1,0:T(8,128)(2,1)} %get-tuple-element.30.refs_5_), channel_id=1, source_target_pairs={{0,2},{2,0},{16,16},{18,18},{32,32},{34,34},{48,50},{50,48},{1,3},... | collective-permute-start | bytes 1572872 | tf_op jit(solution)/shard_map/ppermute | solution.py:386
  114.1 7.4 %attend.3 = bf16[16,4,4,32,128]{4,3,2,1,0:T(8,128)(2,1)} custom-call(s32[3]{0:T(128)S(1)} %copy-done.5, bf16[32,4,16,128]{3,2,1,0:T(8,128)(2,1)S(1)} %get-tuple-element.27.refs_1_, bf16[32,4,16,128]{3,2,1,0:T(8,128)(2,1)} %collective-permute-done.3.refs_2_, bf16[32,4,16,128]{3,2,1,0:T(8,128)(2,1)S(1)} %collective-permute-done.4.refs_0_.refs_3_, ...), custom_call_target="tpu_custom_call" | custom-call | tf_op jit(solution)/shard_map/attend/pallas_call | solution.py:210
  121.4 6.5 %all-to-all-start.2 = ((bf16[16,4,4,32,128]{4,3,2,1,0:T(8,128)(2,1)}), bf16[16,4,4,32,128]{4,3,2,1,0:T(8,128)(2,1)}, u32[]{:S(2)}, u32[]{:S(2)}) async-start(bf16[16,4,4,32,128]{4,3,2,1,0:T(8,128)(2,1)} %attend.3), calls=%async_computation.2 | async-start | bytes 4194304 | tf_op jit(solution)/shard_map/all_to_all | solution.py:402
  128.0 14.7 %collective-permute-done.8.refs_2_ = bf16[16,4,32,128]{3,2,1,0:T(8,128)(2,1)S(1)} collective-permute-done((bf16[16,4,32,128]{3,2,1,0:T(8,128)(2,1)}, bf16[16,4,32,128]{3,2,1,0:T(8,128)(2,1)S(1)}, u32[]{:S(2)}, u32[]{:S(2)}) %collective-permute-start.8) | collective-permute-done | bytes 524320 | tf_op jit(solution)/shard_map/ppermute | solution.py:386
  142.7 10.1 %collective-permute-done.9.refs_3_ = bf16[16,4,32,128]{3,2,1,0:T(8,128)(2,1)S(1)} collective-permute-done((bf16[16,4,32,128]{3,2,1,0:T(8,128)(2,1)}, bf16[16,4,32,128]{3,2,1,0:T(8,128)(2,1)S(1)}, u32[]{:S(2)}, u32[]{:S(2)}) %collective-permute-start.9) | collective-permute-done | bytes 524320 | tf_op jit(solution)/shard_map/ppermute | solution.py:386
  153.6 2.0 part.6
  155.6 3.2 %collective-permute-start.11 = (bf16[16,4,32,128]{3,2,1,0:T(8,128)(2,1)}, bf16[16,4,32,128]{3,2,1,0:T(8,128)(2,1)S(1)}, u32[]{:S(2)}, u32[]{:S(2)}) collective-permute-start(bf16[16,4,32,128]{3,2,1,0:T(8,128)(2,1)} %get-tuple-element.35), channel_id=1, source_target_pairs={{0,50},{2,48},{16,32},{18,34},{32,16},{34,18},{48,2},{50,0},{1,51}... | collective-permute-start | bytes 1572872 | tf_op jit(solution)/shard_map/ppermute | solution.py:386
  158.8 4.5 %collective-permute-start.10 = (bf16[16,4,32,128]{3,2,1,0:T(8,128)(2,1)S(1)}, bf16[16,4,32,128]{3,2,1,0:T(8,128)(2,1)S(1)}, u32[]{:S(2)}, u32[]{:S(2)}) collective-permute-start(bf16[16,4,32,128]{3,2,1,0:T(8,128)(2,1)S(1)} %get-tuple-element.34.refs_4_.refs_1_), channel_id=1, source_target_pairs={{0,2},{2,0},{16,16},{18,18},{32,32},{34,34},{48,50},{50,48},{1,3},... | collective-permute-start | bytes 1572872 | tf_op jit(solution)/shard_map/ppermute | solution.py:386
  165.0 6.6 %all-to-all-start.3 = ((bf16[16,4,4,32,128]{4,3,2,1,0:T(8,128)(2,1)}), bf16[16,4,4,32,128]{4,3,2,1,0:T(8,128)(2,1)}, u32[]{:S(2)}, u32[]{:S(2)}) async-start(bf16[16,4,4,32,128]{4,3,2,1,0:T(8,128)(2,1)} %join.3), calls=%async_computation.3 | async-start | bytes 4194304 | tf_op jit(solution)/shard_map/all_to_all | solution.py:402
  171.6 2.0 part.7
  173.6 2.5 %collective-permute-start.12 = (bf16[16,4,32,128]{3,2,1,0:T(8,128)(2,1)}, bf16[16,4,32,128]{3,2,1,0:T(8,128)(2,1)}, u32[]{:S(2)}, u32[]{:S(2)}) collective-permute-start(bf16[16,4,32,128]{3,2,1,0:T(8,128)(2,1)} %get-tuple-element.36), channel_id=1, source_target_pairs={{0,18},{2,16},{16,0},{18,2},{32,48},{34,50},{48,34},{50,32},{1,19}... | collective-permute-start | bytes 1572872 | tf_op jit(solution)/shard_map/ppermute | solution.py:386
  176.0 7.2 %collective-permute-done.11.refs_1_.refs_6_ = bf16[16,4,32,128]{3,2,1,0:T(8,128)(2,1)S(1)} collective-permute-done((bf16[16,4,32,128]{3,2,1,0:T(8,128)(2,1)}, bf16[16,4,32,128]{3,2,1,0:T(8,128)(2,1)S(1)}, u32[]{:S(2)}, u32[]{:S(2)}) %collective-permute-start.11) | collective-permute-done | bytes 524320 | tf_op jit(solution)/shard_map/ppermute | solution.py:386
  184.8 9.2 %collective-permute-done.12.refs_4_ = bf16[16,4,32,128]{3,2,1,0:T(8,128)(2,1)} collective-permute-done((bf16[16,4,32,128]{3,2,1,0:T(8,128)(2,1)}, bf16[16,4,32,128]{3,2,1,0:T(8,128)(2,1)}, u32[]{:S(2)}, u32[]{:S(2)}) %collective-permute-start.12) | collective-permute-done | bytes 524320 | tf_op jit(solution)/shard_map/ppermute | solution.py:386
  194.0 9.9 %collective-permute-done.13.refs_5_ = bf16[16,4,32,128]{3,2,1,0:T(8,128)(2,1)} collective-permute-done((bf16[16,4,32,128]{3,2,1,0:T(8,128)(2,1)}, bf16[16,4,32,128]{3,2,1,0:T(8,128)(2,1)}, u32[]{:S(2)}, u32[]{:S(2)}) %collective-permute-start.13) | collective-permute-done | bytes 524320 | tf_op jit(solution)/shard_map/ppermute | solution.py:386
  203.9 5.3 %unpack.1 = (bf16[4,1024,128]{2,1,0:T(8,128)(2,1)}, bf16[4,1024,128]{2,1,0:T(8,128)(2,1)}, bf16[4,1024,128]{2,1,0:T(8,128)(2,1)}, bf16[4,1024,128]{2,1,0:T(8,128)(2,1)}) custom-call(s32[3]{0:T(128)} %pad_add_fusion.refs_0_, f32[8,128]{1,0:T(8,128)} %copy-done.6, bf16[16,4,4,32,128]{4,3,2,1,0:T(8,128)(2,1)} %all-to-all-done.3.refs_2_, ...), custom_call_target="tpu_custom_call" | custom-call | tf_op jit(solution)/shard_map/unpack/pallas_call | solution.py:354
  (34 shorter events, 8.3 us)
Async XLA Ops:
  4.8 17.8 %collective-permute-start = (bf16[32,4,16,128]{3,2,1,0:T(8,128)(2,1)}, bf16[32,4,16,128]{3,2,1,0:T(8,128)(2,1)S(1)}, u32[]{:S(2)}, u32[]{:S(2)}) collective-permute-start(bf16[32,4,16,128]{3,2,1,0:T(8,128)(2,1)} %bitcast.33), channel_id=1, source_target_pairs={{0,16},{16,32},{32,48},{48,0},{1,17},{17,33},{33,49},{49,1},{2,18}... | collective-permute-start | bytes 1572872 | tf_op jit(solution)/shard_map/ppermute | solution.py:370
  6.8 37.4 %collective-permute-start.1 = (bf16[32,4,16,128]{3,2,1,0:T(8,128)(2,1)}, bf16[32,4,16,128]{3,2,1,0:T(8,128)(2,1)S(1)}, u32[]{:S(2)}, u32[]{:S(2)}) collective-permute-start(bf16[32,4,16,128]{3,2,1,0:T(8,128)(2,1)} %bitcast.32), channel_id=1, source_target_pairs={{0,32},{16,48},{32,0},{48,16},{1,33},{17,49},{33,1},{49,17},{2,34}... | collective-permute-start | bytes 1572872 | tf_op jit(solution)/shard_map/ppermute | solution.py:370
  10.1 34.2 %collective-permute-start.2 = (bf16[32,4,16,128]{3,2,1,0:T(8,128)(2,1)}, bf16[32,4,16,128]{3,2,1,0:T(8,128)(2,1)S(1)}, u32[]{:S(2)}, u32[]{:S(2)}) collective-permute-start(bf16[32,4,16,128]{3,2,1,0:T(8,128)(2,1)} %bitcast.31), channel_id=1, source_target_pairs={{0,48},{16,0},{32,16},{48,32},{1,49},{17,1},{33,17},{49,33},{2,50}... | collective-permute-start | bytes 1572872 | tf_op jit(solution)/shard_map/ppermute | solution.py:370
  14.7 35.6 %all-to-all-start = ((bf16[32,4,4,16,128]{4,3,2,1,0:T(8,128)(2,1)}), bf16[32,4,4,16,128]{4,3,2,1,0:T(8,128)(2,1)}, u32[]{:S(2)}, u32[]{:S(2)}) async-start(bf16[32,4,4,16,128]{4,3,2,1,0:T(8,128)(2,1)} %bitcast.18), calls=%async_computation | async-start | bytes 4194304 | tf_op jit(solution)/shard_map/all_to_all | solution.py:402
  44.2 12.0 %copy-start = (bf16[32,4,4,4,128]{4,3,2,1,0:T(4,128)(2,1)S(1)}, bf16[32,4,4,4,128]{4,3,2,1,0:T(4,128)(2,1)}, u32[]{:S(2)}) copy-start(bf16[32,4,4,4,128]{4,3,2,1,0:T(4,128)(2,1)} %get-tuple-element.23) | copy-start | bytes 1572868
  51.4 40.1 %collective-permute-start.4 = (bf16[32,4,16,128]{3,2,1,0:T(8,128)(2,1)S(1)}, bf16[32,4,16,128]{3,2,1,0:T(8,128)(2,1)S(1)}, u32[]{:S(2)}, u32[]{:S(2)}) collective-permute-start(bf16[32,4,16,128]{3,2,1,0:T(8,128)(2,1)S(1)} %part.4.refs_1_.refs_4_), channel_id=1, source_target_pairs={{0,32},{16,48},{32,0},{48,16},{1,33},{17,49},{33,1},{49,17},{2,34}... | collective-permute-start | bytes 1572872 | tf_op jit(solution)/shard_map/ppermute | solution.py:370
  57.9 35.6 %all-to-all-start.1 = ((bf16[32,4,4,16,128]{4,3,2,1,0:T(8,128)(2,1)}), bf16[32,4,4,16,128]{4,3,2,1,0:T(8,128)(2,1)}, u32[]{:S(2)}, u32[]{:S(2)}) async-start(bf16[32,4,4,16,128]{4,3,2,1,0:T(8,128)(2,1)} %join.2), calls=%async_computation.1 | async-start | bytes 4194304 | tf_op jit(solution)/shard_map/all_to_all | solution.py:402
  67.8 41.0 %collective-permute-start.3 = (bf16[32,4,16,128]{3,2,1,0:T(8,128)(2,1)}, bf16[32,4,16,128]{3,2,1,0:T(8,128)(2,1)}, u32[]{:S(2)}, u32[]{:S(2)}) collective-permute-start(bf16[32,4,16,128]{3,2,1,0:T(8,128)(2,1)} %get-tuple-element.28), channel_id=1, source_target_pairs={{0,16},{16,32},{32,48},{48,0},{1,17},{17,33},{33,49},{49,1},{2,18}... | collective-permute-start | bytes 1572872 | tf_op jit(solution)/shard_map/ppermute | solution.py:370
  70.0 44.0 %collective-permute-start.5 = (bf16[32,4,16,128]{3,2,1,0:T(8,128)(2,1)}, bf16[32,4,16,128]{3,2,1,0:T(8,128)(2,1)}, u32[]{:S(2)}, u32[]{:S(2)}) collective-permute-start(bf16[32,4,16,128]{3,2,1,0:T(8,128)(2,1)} %get-tuple-element.29), channel_id=1, source_target_pairs={{0,48},{16,0},{32,16},{48,32},{1,49},{17,1},{33,17},{49,33},{2,50}... | collective-permute-start | bytes 1572872 | tf_op jit(solution)/shard_map/ppermute | solution.py:370
  91.5 2.0 copy-start.5
  101.3 26.7 %collective-permute-start.7 = (bf16[16,4,32,128]{3,2,1,0:T(8,128)(2,1)}, bf16[16,4,32,128]{3,2,1,0:T(8,128)(2,1)S(1)}, u32[]{:S(2)}, u32[]{:S(2)}) collective-permute-start(bf16[16,4,32,128]{3,2,1,0:T(8,128)(2,1)} %get-tuple-element.31), channel_id=1, source_target_pairs={{0,18},{2,16},{16,0},{18,2},{32,48},{34,50},{48,34},{50,32},{1,19}... | collective-permute-start | bytes 1572872 | tf_op jit(solution)/shard_map/ppermute | solution.py:386
  107.4 35.3 %collective-permute-start.8 = (bf16[16,4,32,128]{3,2,1,0:T(8,128)(2,1)}, bf16[16,4,32,128]{3,2,1,0:T(8,128)(2,1)S(1)}, u32[]{:S(2)}, u32[]{:S(2)}) collective-permute-start(bf16[16,4,32,128]{3,2,1,0:T(8,128)(2,1)} %get-tuple-element.32), channel_id=1, source_target_pairs={{0,34},{2,32},{16,48},{18,50},{32,0},{34,2},{48,18},{50,16},{1,35}... | collective-permute-start | bytes 1572872 | tf_op jit(solution)/shard_map/ppermute | solution.py:386
  108.8 44.0 %collective-permute-start.9 = (bf16[16,4,32,128]{3,2,1,0:T(8,128)(2,1)}, bf16[16,4,32,128]{3,2,1,0:T(8,128)(2,1)S(1)}, u32[]{:S(2)}, u32[]{:S(2)}) collective-permute-start(bf16[16,4,32,128]{3,2,1,0:T(8,128)(2,1)} %get-tuple-element.33), channel_id=1, source_target_pairs={{0,50},{2,48},{16,32},{18,34},{32,16},{34,18},{48,2},{50,0},{1,51}... | collective-permute-start | bytes 1572872 | tf_op jit(solution)/shard_map/ppermute | solution.py:386
  108.8 44.0 %collective-permute-start.6 = (bf16[16,4,32,128]{3,2,1,0:T(8,128)(2,1)}, bf16[16,4,32,128]{3,2,1,0:T(8,128)(2,1)S(1)}, u32[]{:S(2)}, u32[]{:S(2)}) collective-permute-start(bf16[16,4,32,128]{3,2,1,0:T(8,128)(2,1)} %get-tuple-element.30.refs_5_), channel_id=1, source_target_pairs={{0,2},{2,0},{16,16},{18,18},{32,32},{34,34},{48,50},{50,48},{1,3},... | collective-permute-start | bytes 1572872 | tf_op jit(solution)/shard_map/ppermute | solution.py:386
  121.4 32.1 %all-to-all-start.2 = ((bf16[16,4,4,32,128]{4,3,2,1,0:T(8,128)(2,1)}), bf16[16,4,4,32,128]{4,3,2,1,0:T(8,128)(2,1)}, u32[]{:S(2)}, u32[]{:S(2)}) async-start(bf16[16,4,4,32,128]{4,3,2,1,0:T(8,128)(2,1)} %attend.3), calls=%async_computation.2 | async-start | bytes 4194304 | tf_op jit(solution)/shard_map/all_to_all | solution.py:402
  152.8 0.8 copy-start.2
  153.6 9.7 %copy-start.3 = (bf16[16,4,32,128]{3,2,1,0:T(8,128)(2,1)S(1)}, bf16[16,4,32,128]{3,2,1,0:T(8,128)(2,1)}, u32[]{:S(2)}) copy-start(bf16[16,4,32,128]{3,2,1,0:T(8,128)(2,1)} %copy-done.2) | copy-start | bytes 1572868
  155.6 27.6 %collective-permute-start.11 = (bf16[16,4,32,128]{3,2,1,0:T(8,128)(2,1)}, bf16[16,4,32,128]{3,2,1,0:T(8,128)(2,1)S(1)}, u32[]{:S(2)}, u32[]{:S(2)}) collective-permute-start(bf16[16,4,32,128]{3,2,1,0:T(8,128)(2,1)} %get-tuple-element.35), channel_id=1, source_target_pairs={{0,50},{2,48},{16,32},{18,34},{32,16},{34,18},{48,2},{50,0},{1,51}... | collective-permute-start | bytes 1572872 | tf_op jit(solution)/shard_map/ppermute | solution.py:386
  158.8 24.4 %collective-permute-start.10 = (bf16[16,4,32,128]{3,2,1,0:T(8,128)(2,1)S(1)}, bf16[16,4,32,128]{3,2,1,0:T(8,128)(2,1)S(1)}, u32[]{:S(2)}, u32[]{:S(2)}) collective-permute-start(bf16[16,4,32,128]{3,2,1,0:T(8,128)(2,1)S(1)} %get-tuple-element.34.refs_4_.refs_1_), channel_id=1, source_target_pairs={{0,2},{2,0},{16,16},{18,18},{32,32},{34,34},{48,50},{50,48},{1,3},... | collective-permute-start | bytes 1572872 | tf_op jit(solution)/shard_map/ppermute | solution.py:386
  165.0 39.0 %all-to-all-start.3 = ((bf16[16,4,4,32,128]{4,3,2,1,0:T(8,128)(2,1)}), bf16[16,4,4,32,128]{4,3,2,1,0:T(8,128)(2,1)}, u32[]{:S(2)}, u32[]{:S(2)}) async-start(bf16[16,4,4,32,128]{4,3,2,1,0:T(8,128)(2,1)} %join.3), calls=%async_computation.3 | async-start | bytes 4194304 | tf_op jit(solution)/shard_map/all_to_all | solution.py:402
  173.6 20.4 %collective-permute-start.12 = (bf16[16,4,32,128]{3,2,1,0:T(8,128)(2,1)}, bf16[16,4,32,128]{3,2,1,0:T(8,128)(2,1)}, u32[]{:S(2)}, u32[]{:S(2)}) collective-permute-start(bf16[16,4,32,128]{3,2,1,0:T(8,128)(2,1)} %get-tuple-element.36), channel_id=1, source_target_pairs={{0,18},{2,16},{16,0},{18,2},{32,48},{34,50},{48,34},{50,32},{1,19}... | collective-permute-start | bytes 1572872 | tf_op jit(solution)/shard_map/ppermute | solution.py:386
  176.0 27.9 %collective-permute-start.13 = (bf16[16,4,32,128]{3,2,1,0:T(8,128)(2,1)}, bf16[16,4,32,128]{3,2,1,0:T(8,128)(2,1)}, u32[]{:S(2)}, u32[]{:S(2)}) collective-permute-start(bf16[16,4,32,128]{3,2,1,0:T(8,128)(2,1)} %get-tuple-element.37), channel_id=1, source_target_pairs={{0,34},{2,32},{16,48},{18,50},{32,0},{34,2},{48,18},{50,16},{1,35}... | collective-permute-start | bytes 1572872 | tf_op jit(solution)/shard_map/ppermute | solution.py:386
  183.2 0.8 copy-start.1
  183.2 1.0 copy-start.4
  184.2 0.6 copy-start.6

commit v9 on v8

--- a/solution.py
+++ b/solution.py
@@ -411,7 +411,7 @@
     done = attend([first], place, sizes, True, hold(second[2:3]))
     first = z_out(done)
     second = attend(second, place, sizes, False, done[0])[0]
-    pieces = parts(across(second, ("y", "x")), hold(first), [0, 3])
+    pieces = parts(across(second, ("y", "x")), hold([first[0], first[1], first[3]]), [0, 3])
     second = z_out(pieces)
     first = across(join(first, pieces[0]), ("y", "x"))
 

time: 211 us -> 208 us (0.986)
  waiting for transfers between devices: 101 us -> 69.8 us
  starting transfers between devices: 66.5 us -> 92.9 us
    ppermute x8, waiting for transfers between devices: 51.1 us -> 12.9 us  [z_out(): lax.ppermute(pieces[k], ('z1', 'z0', 'w'), pairs(k))]
    ppermute x8, starting transfers between devices: 23 us -> 44 us  [z_out(): lax.ppermute(pieces[k], ('z1', 'z0', 'w'), pairs(k))]
    all_to_all x4, waiting for transfers between devices: 8.08 us -> 15.2 us  [across(): return lax.all_to_all(whole, names, 0, 0, tiled=True)]
    all_to_all x4, starting transfers between devices: 28.5 us -> 33.8 us  [across(): return lax.all_to_all(whole, names, 0, 0, tiled=True)]
  transfers between devices with their start and end apart: 18 -> 18, of which waited for: 10 -> 9; matrix products, arithmetic and copies ran while one was open for 0% -> 0% of each run, Pallas kernels for 12% -> 14%
where the time goes in v9:
time: 208 us; the launch traced here: 205 us
  starting transfers between devices  92.9 us (45%)
  waiting for transfers between devices  69.8 us (34%)
  Pallas kernels  38.9 us (19%)
    ppermute x8, starting transfers between devices, z_out(): lax.ppermute(pieces[k], ('z1', 'z0', 'w'), pairs(k))  44 us
    ppermute x6, waiting for transfers between devices, z_in(): lax.ppermute(pieces[k], ('z1', 'z0'), [(z, (z + k) % ZS) for z in range(Z...  41.7 us
    all_to_all x4, starting transfers between devices, across(): return lax.all_to_all(whole, names, 0, 0, tiled=True)  33.8 us
    all_to_all x4, waiting for transfers between devices, across(): return lax.all_to_all(whole, names, 0, 0, tiled=True)  15.2 us
    pallas_call x2, Pallas kernels, attend(): pl.pallas_call(lambda *refs: attend_kernel(sizes, len(pieces), split, *re...  15.2 us
    ppermute x6, starting transfers between devices, z_in(): lax.ppermute(pieces[k], ('z1', 'z0'), [(z, (z + k) % ZS) for z in range(Z...  15.1 us
    ppermute x8, waiting for transfers between devices, z_out(): lax.ppermute(pieces[k], ('z1', 'z0', 'w'), pairs(k))  12.9 us
    pallas_call x4, Pallas kernels, part(): pl.pallas_call(lambda *refs: part_kernel(picks, *refs), out_shape=[jax.Sh...  7.2 us
  transfers between devices with their start and end apart: 18, of which 9 were waited for; matrix products, arithmetic and copies ran while one was open for 0% of the time, Pallas kernels for 14%

profile of v9, /device:TPU:2, one launch (start us, length us, event | category | flops | bytes accessed | tf_op | source)
XLA Modules:
  0.0 204.6 jit_solution(7007307222449185835)
XLA Ops:
  1.2 3.6 %pack.2 = (bf16[32,4,4,4,128]{4,3,2,1,0:T(4,128)(2,1)}, bf16[32,4,4,4,128]{4,3,2,1,0:T(4,128)(2,1)}, bf16[32,4,4,4,128]{4,3,2,1,0:T(4,128)(2,1)}, bf16[32,4,4,4,128]{4,3,2,1,0:T(4,128)(2,1)}) custom-call(s32[3]{0:T(128)} %pad_add_fusion.refs_0_, bf16[4,4,4,4,4,4,128]{6,5,4,3,2,1,0:T(4,128)(2,1)} %bitcast.19, bf16[4,4,4,4,4,4,128]{6,5,4,3,2,1,0:T(4,128)(2,1)} %bitcast.21, ...), custom_call_target="tpu_custom_call" | custom-call | tf_op jit(solution)/shard_map/pack/pallas_call | solution.py:125
  4.8 2.0 collective-permute-start
  6.8 3.3 %collective-permute-start.1 = (bf16[32,4,16,128]{3,2,1,0:T(8,128)(2,1)}, bf16[32,4,16,128]{3,2,1,0:T(8,128)(2,1)S(1)}, u32[]{:S(2)}, u32[]{:S(2)}) collective-permute-start(bf16[32,4,16,128]{3,2,1,0:T(8,128)(2,1)} %bitcast.32), channel_id=1, source_target_pairs={{0,32},{16,48},{32,0},{48,16},{1,33},{17,49},{33,1},{49,17},{2,34}... | collective-permute-start | bytes 1572872 | tf_op jit(solution)/shard_map/ppermute | solution.py:370
  11.1 3.6 %pack.3 = bf16[32,4,4,4,4,128]{5,4,3,2,1,0:T(4,128)(2,1)} custom-call(s32[3]{0:T(128)} %pad_add_fusion.refs_0_, bf16[4,4,4,4,4,4,128]{6,5,4,3,2,1,0:T(4,128)(2,1)} %bitcast.20, bf16[4,4,4,4,4,4,128]{6,5,4,3,2,1,0:T(4,128)(2,1)} %bitcast.22, bf16[4,4,4,4,4,4,128]{6,5,4,3,2,1,0:T(4,128)(2,1)} %bitcast.24, bf16[4,4,4,4,4,4,128]{6,5,4,3,2,1,0:T(4,128)(2,1)} %bitcast.26, ...), custom_call_target="tpu_custom_call" | custom-call | tf_op jit(solution)/shard_map/pack/pallas_call | solution.py:125
  14.7 7.7 %all-to-all-start = ((bf16[32,4,4,16,128]{4,3,2,1,0:T(8,128)(2,1)}), bf16[32,4,4,16,128]{4,3,2,1,0:T(8,128)(2,1)}, u32[]{:S(2)}, u32[]{:S(2)}) async-start(bf16[32,4,4,16,128]{4,3,2,1,0:T(8,128)(2,1)} %bitcast.18), calls=%async_computation | async-start | bytes 4194304 | tf_op jit(solution)/shard_map/all_to_all | solution.py:402
  22.6 21.6 %collective-permute-done.1.refs_1_.refs_2_ = bf16[32,4,16,128]{3,2,1,0:T(8,128)(2,1)S(1)} collective-permute-done((bf16[32,4,16,128]{3,2,1,0:T(8,128)(2,1)}, bf16[32,4,16,128]{3,2,1,0:T(8,128)(2,1)S(1)}, u32[]{:S(2)}, u32[]{:S(2)}) %collective-permute-start.1) | collective-permute-done | bytes 524320 | tf_op jit(solution)/shard_map/ppermute | solution.py:370
  44.3 6.0 %all-to-all-done.refs_0_ = bf16[32,4,4,16,128]{4,3,2,1,0:T(8,128)(2,1)} async-done(((bf16[32,4,4,16,128]{4,3,2,1,0:T(8,128)(2,1)}), bf16[32,4,4,16,128]{4,3,2,1,0:T(8,128)(2,1)}, u32[]{:S(2)}, u32[]{:S(2)}) %all-to-all-start) | async-done | bytes 2097184 | tf_op jit(solution)/shard_map/all_to_all | solution.py:402
  51.4 4.9 %collective-permute-start.4 = (bf16[32,4,16,128]{3,2,1,0:T(8,128)(2,1)S(1)}, bf16[32,4,16,128]{3,2,1,0:T(8,128)(2,1)S(1)}, u32[]{:S(2)}, u32[]{:S(2)}) collective-permute-start(bf16[32,4,16,128]{3,2,1,0:T(8,128)(2,1)S(1)} %part.4.refs_1_.refs_4_), channel_id=1, source_target_pairs={{0,32},{16,48},{32,0},{48,16},{1,33},{17,49},{33,1},{49,17},{2,34}... | collective-permute-start | bytes 1572872 | tf_op jit(solution)/shard_map/ppermute | solution.py:370
  56.3 1.7 join.2
  58.0 7.7 %all-to-all-start.1 = ((bf16[32,4,4,16,128]{4,3,2,1,0:T(8,128)(2,1)}), bf16[32,4,4,16,128]{4,3,2,1,0:T(8,128)(2,1)}, u32[]{:S(2)}, u32[]{:S(2)}) async-start(bf16[32,4,4,16,128]{4,3,2,1,0:T(8,128)(2,1)} %join.2), calls=%async_computation.1 | async-start | bytes 4194304 | tf_op jit(solution)/shard_map/all_to_all | solution.py:402
  65.7 2.2 %part.5 = (bf16[32,4,16,128]{3,2,1,0:T(8,128)(2,1)S(1)}, bf16[32,4,16,128]{3,2,1,0:T(8,128)(2,1)}, bf16[32,4,16,128]{3,2,1,0:T(8,128)(2,1)}) custom-call(bf16[32,4,4,16,128]{4,3,2,1,0:T(8,128)(2,1)} %all-to-all-done.refs_0_, bf16[32,4,16,128]{3,2,1,0:T(8,128)(2,1)S(1)} %part.4.refs_1_.refs_4_), custom_call_target="tpu_custom_call" | custom-call | tf_op jit(solution)/shard_map/part/pallas_call | solution.py:277
  67.8 2.2 %collective-permute-start.3 = (bf16[32,4,16,128]{3,2,1,0:T(8,128)(2,1)}, bf16[32,4,16,128]{3,2,1,0:T(8,128)(2,1)}, u32[]{:S(2)}, u32[]{:S(2)}) collective-permute-start(bf16[32,4,16,128]{3,2,1,0:T(8,128)(2,1)} %get-tuple-element.28), channel_id=1, source_target_pairs={{0,16},{16,32},{32,48},{48,0},{1,17},{17,33},{33,49},{49,1},{2,18}... | collective-permute-start | bytes 1572872 | tf_op jit(solution)/shard_map/ppermute | solution.py:370
  70.1 1.7 collective-permute-start.5
  71.8 19.8 %collective-permute-done.4.refs_0_.refs_3_ = bf16[32,4,16,128]{3,2,1,0:T(8,128)(2,1)S(1)} collective-permute-done((bf16[32,4,16,128]{3,2,1,0:T(8,128)(2,1)S(1)}, bf16[32,4,16,128]{3,2,1,0:T(8,128)(2,1)S(1)}, u32[]{:S(2)}, u32[]{:S(2)}) %collective-permute-start.4) | collective-permute-done | bytes 524320 | tf_op jit(solution)/shard_map/ppermute | solution.py:370
  91.5 2.1 %all-to-all-done.1.refs_1_ = bf16[32,4,4,16,128]{4,3,2,1,0:T(8,128)(2,1)} async-done(((bf16[32,4,4,16,128]{4,3,2,1,0:T(8,128)(2,1)}), bf16[32,4,4,16,128]{4,3,2,1,0:T(8,128)(2,1)}, u32[]{:S(2)}, u32[]{:S(2)}) %all-to-all-start.1) | async-done | bytes 2097184 | tf_op jit(solution)/shard_map/all_to_all | solution.py:402
  93.6 7.8 %attend.2 = (bf16[16,4,32,128]{3,2,1,0:T(8,128)(2,1)S(1)}, bf16[16,4,32,128]{3,2,1,0:T(8,128)(2,1)}, bf16[16,4,32,128]{3,2,1,0:T(8,128)(2,1)}, bf16[16,4,32,128]{3,2,1,0:T(8,128)(2,1)}) custom-call(s32[3]{0:T(128)S(1)} %copy-done.3, bf16[32,4,4,16,128]{4,3,2,1,0:T(8,128)(2,1)} %all-to-all-done.1.refs_1_, f32[8,128]{1,0:T(8,128)S(1)} %hold.5.refs_2_), custom_call_target="tpu_custom_call" | custom-call | tf_op jit(solution)/shard_map/attend/pallas_call | solution.py:210
  101.4 6.2 %collective-permute-start.7 = (bf16[16,4,32,128]{3,2,1,0:T(8,128)(2,1)}, bf16[16,4,32,128]{3,2,1,0:T(8,128)(2,1)S(1)}, u32[]{:S(2)}, u32[]{:S(2)}) collective-permute-start(bf16[16,4,32,128]{3,2,1,0:T(8,128)(2,1)} %get-tuple-element.31), channel_id=1, source_target_pairs={{0,18},{2,16},{16,0},{18,2},{32,48},{34,50},{48,34},{50,32},{1,19}... | collective-permute-start | bytes 1572872 | tf_op jit(solution)/shard_map/ppermute | solution.py:386
  107.5 4.4 %collective-permute-start.6 = (bf16[16,4,32,128]{3,2,1,0:T(8,128)(2,1)S(1)}, bf16[16,4,32,128]{3,2,1,0:T(8,128)(2,1)S(1)}, u32[]{:S(2)}, u32[]{:S(2)}) collective-permute-start(bf16[16,4,32,128]{3,2,1,0:T(8,128)(2,1)S(1)} %get-tuple-element.30.refs_5_), channel_id=1, source_target_pairs={{0,2},{2,0},{16,16},{18,18},{32,32},{34,34},{48,50},{50,48},{1,3},... | collective-permute-start | bytes 1572872 | tf_op jit(solution)/shard_map/ppermute | solution.py:386
  112.0 7.4 %attend.3 = bf16[16,4,4,32,128]{4,3,2,1,0:T(8,128)(2,1)} custom-call(s32[3]{0:T(128)S(1)} %copy-done.3, bf16[32,4,16,128]{3,2,1,0:T(8,128)(2,1)S(1)} %get-tuple-element.27.refs_1_, bf16[32,4,16,128]{3,2,1,0:T(8,128)(2,1)} %collective-permute-done.3.refs_2_, bf16[32,4,16,128]{3,2,1,0:T(8,128)(2,1)S(1)} %collective-permute-done.4.refs_0_.refs_3_, ...), custom_call_target="tpu_custom_call" | custom-call | tf_op jit(solution)/shard_map/attend/pallas_call | solution.py:210
  119.4 6.5 %all-to-all-start.2 = ((bf16[16,4,4,32,128]{4,3,2,1,0:T(8,128)(2,1)}), bf16[16,4,4,32,128]{4,3,2,1,0:T(8,128)(2,1)}, u32[]{:S(2)}, u32[]{:S(2)}) async-start(bf16[16,4,4,32,128]{4,3,2,1,0:T(8,128)(2,1)} %attend.3), calls=%async_computation.2 | async-start | bytes 4194304 | tf_op jit(solution)/shard_map/all_to_all | solution.py:402
  126.0 19.8 %collective-permute-start.11 = (bf16[16,4,32,128]{3,2,1,0:T(8,128)(2,1)}, bf16[16,4,32,128]{3,2,1,0:T(8,128)(2,1)}, u32[]{:S(2)}, u32[]{:S(2)}) collective-permute-start(bf16[16,4,32,128]{3,2,1,0:T(8,128)(2,1)} %get-tuple-element.35), channel_id=1, source_target_pairs={{0,34},{2,32},{16,48},{18,50},{32,0},{34,2},{48,18},{50,16},{1,35}... | collective-permute-start | bytes 1572872 | tf_op jit(solution)/shard_map/ppermute | solution.py:386
  145.8 5.6 %all-to-all-done.2.refs_0_ = bf16[16,4,4,32,128]{4,3,2,1,0:T(8,128)(2,1)} async-done(((bf16[16,4,4,32,128]{4,3,2,1,0:T(8,128)(2,1)}), bf16[16,4,4,32,128]{4,3,2,1,0:T(8,128)(2,1)}, u32[]{:S(2)}, u32[]{:S(2)}) %all-to-all-start.2) | async-done | bytes 2097184 | tf_op jit(solution)/shard_map/all_to_all | solution.py:402
  151.5 2.0 part.6
  154.7 7.3 %collective-permute-start.9 = (bf16[16,4,32,128]{3,2,1,0:T(8,128)(2,1)S(1)}, bf16[16,4,32,128]{3,2,1,0:T(8,128)(2,1)S(1)}, u32[]{:S(2)}, u32[]{:S(2)}) collective-permute-start(bf16[16,4,32,128]{3,2,1,0:T(8,128)(2,1)S(1)} %get-tuple-element.33.refs_4_.refs_1_), channel_id=1, source_target_pairs={{0,2},{2,0},{16,16},{18,18},{32,32},{34,34},{48,50},{50,48},{1,3},... | collective-permute-start | bytes 1572872 | tf_op jit(solution)/shard_map/ppermute | solution.py:386
  162.1 2.4 %join.3 = bf16[16,4,4,32,128]{4,3,2,1,0:T(8,128)(2,1)} custom-call(bf16[16,4,32,128]{3,2,1,0:T(8,128)(2,1)S(1)} %collective-permute-done.6.refs_0_, bf16[16,4,32,128]{3,2,1,0:T(8,128)(2,1)S(1)} %collective-permute-done.7.refs_1_, bf16[16,4,32,128]{3,2,1,0:T(8,128)(2,1)} %collective-permute-done.11.refs_2_, ...), custom_call_target="tpu_custom_call" | custom-call | tf_op jit(solution)/shard_map/join/pallas_call | solution.py:258
  164.5 11.9 %all-to-all-start.3 = ((bf16[16,4,4,32,128]{4,3,2,1,0:T(8,128)(2,1)}), bf16[16,4,4,32,128]{4,3,2,1,0:T(8,128)(2,1)}, u32[]{:S(2)}, u32[]{:S(2)}) async-start(bf16[16,4,4,32,128]{4,3,2,1,0:T(8,128)(2,1)} %join.3), calls=%async_computation.3 | async-start | bytes 4194304 | tf_op jit(solution)/shard_map/all_to_all | solution.py:402
  176.4 2.0 part.7
  178.4 4.3 %collective-permute-start.12 = (bf16[16,4,32,128]{3,2,1,0:T(8,128)(2,1)}, bf16[16,4,32,128]{3,2,1,0:T(8,128)(2,1)}, u32[]{:S(2)}, u32[]{:S(2)}) collective-permute-start(bf16[16,4,32,128]{3,2,1,0:T(8,128)(2,1)} %get-tuple-element.36), channel_id=1, source_target_pairs={{0,18},{2,16},{16,0},{18,2},{32,48},{34,50},{48,34},{50,32},{1,19}... | collective-permute-start | bytes 1572872 | tf_op jit(solution)/shard_map/ppermute | solution.py:386
  184.9 9.1 %collective-permute-done.12.refs_4_ = bf16[16,4,32,128]{3,2,1,0:T(8,128)(2,1)} collective-permute-done((bf16[16,4,32,128]{3,2,1,0:T(8,128)(2,1)}, bf16[16,4,32,128]{3,2,1,0:T(8,128)(2,1)}, u32[]{:S(2)}, u32[]{:S(2)}) %collective-permute-start.12) | collective-permute-done | bytes 524320 | tf_op jit(solution)/shard_map/ppermute | solution.py:386
  194.0 3.8 %collective-permute-done.13.refs_5_ = bf16[16,4,32,128]{3,2,1,0:T(8,128)(2,1)} collective-permute-done((bf16[16,4,32,128]{3,2,1,0:T(8,128)(2,1)}, bf16[16,4,32,128]{3,2,1,0:T(8,128)(2,1)}, u32[]{:S(2)}, u32[]{:S(2)}) %collective-permute-start.13) | collective-permute-done | bytes 524320 | tf_op jit(solution)/shard_map/ppermute | solution.py:386
  197.8 1.5 all-to-all-done.3.refs_2_
  199.3 5.3 %unpack.1 = (bf16[4,1024,128]{2,1,0:T(8,128)(2,1)}, bf16[4,1024,128]{2,1,0:T(8,128)(2,1)}, bf16[4,1024,128]{2,1,0:T(8,128)(2,1)}, bf16[4,1024,128]{2,1,0:T(8,128)(2,1)}) custom-call(s32[3]{0:T(128)} %pad_add_fusion.refs_0_, f32[8,128]{1,0:T(8,128)} %copy-done.4, bf16[16,4,4,32,128]{4,3,2,1,0:T(8,128)(2,1)} %all-to-all-done.3.refs_2_, ...), custom_call_target="tpu_custom_call" | custom-call | tf_op jit(solution)/shard_map/unpack/pallas_call | solution.py:354
  (30 shorter events, 6.5 us)
Async XLA Ops:
  4.8 17.8 %collective-permute-start = (bf16[32,4,16,128]{3,2,1,0:T(8,128)(2,1)}, bf16[32,4,16,128]{3,2,1,0:T(8,128)(2,1)S(1)}, u32[]{:S(2)}, u32[]{:S(2)}) collective-permute-start(bf16[32,4,16,128]{3,2,1,0:T(8,128)(2,1)} %bitcast.33), channel_id=1, source_target_pairs={{0,16},{16,32},{32,48},{48,0},{1,17},{17,33},{33,49},{49,1},{2,18}... | collective-permute-start | bytes 1572872 | tf_op jit(solution)/shard_map/ppermute | solution.py:370
  6.8 37.4 %collective-permute-start.1 = (bf16[32,4,16,128]{3,2,1,0:T(8,128)(2,1)}, bf16[32,4,16,128]{3,2,1,0:T(8,128)(2,1)S(1)}, u32[]{:S(2)}, u32[]{:S(2)}) collective-permute-start(bf16[32,4,16,128]{3,2,1,0:T(8,128)(2,1)} %bitcast.32), channel_id=1, source_target_pairs={{0,32},{16,48},{32,0},{48,16},{1,33},{17,49},{33,1},{49,17},{2,34}... | collective-permute-start | bytes 1572872 | tf_op jit(solution)/shard_map/ppermute | solution.py:370
  10.1 34.2 %collective-permute-start.2 = (bf16[32,4,16,128]{3,2,1,0:T(8,128)(2,1)}, bf16[32,4,16,128]{3,2,1,0:T(8,128)(2,1)S(1)}, u32[]{:S(2)}, u32[]{:S(2)}) collective-permute-start(bf16[32,4,16,128]{3,2,1,0:T(8,128)(2,1)} %bitcast.31), channel_id=1, source_target_pairs={{0,48},{16,0},{32,16},{48,32},{1,49},{17,1},{33,17},{49,33},{2,50}... | collective-permute-start | bytes 1572872 | tf_op jit(solution)/shard_map/ppermute | solution.py:370
  14.7 35.6 %all-to-all-start = ((bf16[32,4,4,16,128]{4,3,2,1,0:T(8,128)(2,1)}), bf16[32,4,4,16,128]{4,3,2,1,0:T(8,128)(2,1)}, u32[]{:S(2)}, u32[]{:S(2)}) async-start(bf16[32,4,4,16,128]{4,3,2,1,0:T(8,128)(2,1)} %bitcast.18), calls=%async_computation | async-start | bytes 4194304 | tf_op jit(solution)/shard_map/all_to_all | solution.py:402
  44.3 12.0 %copy-start = (bf16[32,4,4,4,128]{4,3,2,1,0:T(4,128)(2,1)S(1)}, bf16[32,4,4,4,128]{4,3,2,1,0:T(4,128)(2,1)}, u32[]{:S(2)}) copy-start(bf16[32,4,4,4,128]{4,3,2,1,0:T(4,128)(2,1)} %get-tuple-element.23) | copy-start | bytes 1572868
  51.4 40.1 %collective-permute-start.4 = (bf16[32,4,16,128]{3,2,1,0:T(8,128)(2,1)S(1)}, bf16[32,4,16,128]{3,2,1,0:T(8,128)(2,1)S(1)}, u32[]{:S(2)}, u32[]{:S(2)}) collective-permute-start(bf16[32,4,16,128]{3,2,1,0:T(8,128)(2,1)S(1)} %part.4.refs_1_.refs_4_), channel_id=1, source_target_pairs={{0,32},{16,48},{32,0},{48,16},{1,33},{17,49},{33,1},{49,17},{2,34}... | collective-permute-start | bytes 1572872 | tf_op jit(solution)/shard_map/ppermute | solution.py:370
  58.0 35.6 %all-to-all-start.1 = ((bf16[32,4,4,16,128]{4,3,2,1,0:T(8,128)(2,1)}), bf16[32,4,4,16,128]{4,3,2,1,0:T(8,128)(2,1)}, u32[]{:S(2)}, u32[]{:S(2)}) async-start(bf16[32,4,4,16,128]{4,3,2,1,0:T(8,128)(2,1)} %join.2), calls=%async_computation.1 | async-start | bytes 4194304 | tf_op jit(solution)/shard_map/all_to_all | solution.py:402
  67.8 44.1 %collective-permute-start.3 = (bf16[32,4,16,128]{3,2,1,0:T(8,128)(2,1)}, bf16[32,4,16,128]{3,2,1,0:T(8,128)(2,1)}, u32[]{:S(2)}, u32[]{:S(2)}) collective-permute-start(bf16[32,4,16,128]{3,2,1,0:T(8,128)(2,1)} %get-tuple-element.28), channel_id=1, source_target_pairs={{0,16},{16,32},{32,48},{48,0},{1,17},{17,33},{33,49},{49,1},{2,18}... | collective-permute-start | bytes 1572872 | tf_op jit(solution)/shard_map/ppermute | solution.py:370
  70.1 41.9 %collective-permute-start.5 = (bf16[32,4,16,128]{3,2,1,0:T(8,128)(2,1)}, bf16[32,4,16,128]{3,2,1,0:T(8,128)(2,1)}, u32[]{:S(2)}, u32[]{:S(2)}) collective-permute-start(bf16[32,4,16,128]{3,2,1,0:T(8,128)(2,1)} %get-tuple-element.29), channel_id=1, source_target_pairs={{0,48},{16,0},{32,16},{48,32},{1,49},{17,1},{33,17},{49,33},{2,50}... | collective-permute-start | bytes 1572872 | tf_op jit(solution)/shard_map/ppermute | solution.py:370
  91.5 2.1 %copy-start.3 = (s32[3]{0:T(128)S(1)}, s32[3]{0:T(128)}, u32[]{:S(2)}) copy-start(s32[3]{0:T(128)} %pad_add_fusion.refs_0_) | copy-start | bytes 40
  101.4 44.5 %collective-permute-start.7 = (bf16[16,4,32,128]{3,2,1,0:T(8,128)(2,1)}, bf16[16,4,32,128]{3,2,1,0:T(8,128)(2,1)S(1)}, u32[]{:S(2)}, u32[]{:S(2)}) collective-permute-start(bf16[16,4,32,128]{3,2,1,0:T(8,128)(2,1)} %get-tuple-element.31), channel_id=1, source_target_pairs={{0,18},{2,16},{16,0},{18,2},{32,48},{34,50},{48,34},{50,32},{1,19}... | collective-permute-start | bytes 1572872 | tf_op jit(solution)/shard_map/ppermute | solution.py:386
  107.5 38.3 %collective-permute-start.8 = (bf16[16,4,32,128]{3,2,1,0:T(8,128)(2,1)}, bf16[16,4,32,128]{3,2,1,0:T(8,128)(2,1)S(1)}, u32[]{:S(2)}, u32[]{:S(2)}) collective-permute-start(bf16[16,4,32,128]{3,2,1,0:T(8,128)(2,1)} %get-tuple-element.32), channel_id=1, source_target_pairs={{0,50},{2,48},{16,32},{18,34},{32,16},{34,18},{48,2},{50,0},{1,51}... | collective-permute-start | bytes 1572872 | tf_op jit(solution)/shard_map/ppermute | solution.py:386
  107.5 38.3 %collective-permute-start.6 = (bf16[16,4,32,128]{3,2,1,0:T(8,128)(2,1)S(1)}, bf16[16,4,32,128]{3,2,1,0:T(8,128)(2,1)S(1)}, u32[]{:S(2)}, u32[]{:S(2)}) collective-permute-start(bf16[16,4,32,128]{3,2,1,0:T(8,128)(2,1)S(1)} %get-tuple-element.30.refs_5_), channel_id=1, source_target_pairs={{0,2},{2,0},{16,16},{18,18},{32,32},{34,34},{48,50},{50,48},{1,3},... | collective-permute-start | bytes 1572872 | tf_op jit(solution)/shard_map/ppermute | solution.py:386
  119.4 32.0 %all-to-all-start.2 = ((bf16[16,4,4,32,128]{4,3,2,1,0:T(8,128)(2,1)}), bf16[16,4,4,32,128]{4,3,2,1,0:T(8,128)(2,1)}, u32[]{:S(2)}, u32[]{:S(2)}) async-start(bf16[16,4,4,32,128]{4,3,2,1,0:T(8,128)(2,1)} %attend.3), calls=%async_computation.2 | async-start | bytes 4194304 | tf_op jit(solution)/shard_map/all_to_all | solution.py:402
  126.0 36.1 %collective-permute-start.11 = (bf16[16,4,32,128]{3,2,1,0:T(8,128)(2,1)}, bf16[16,4,32,128]{3,2,1,0:T(8,128)(2,1)}, u32[]{:S(2)}, u32[]{:S(2)}) collective-permute-start(bf16[16,4,32,128]{3,2,1,0:T(8,128)(2,1)} %get-tuple-element.35), channel_id=1, source_target_pairs={{0,34},{2,32},{16,48},{18,50},{32,0},{34,2},{48,18},{50,16},{1,35}... | collective-permute-start | bytes 1572872 | tf_op jit(solution)/shard_map/ppermute | solution.py:386
  153.4 29.9 %collective-permute-start.10 = (bf16[16,4,32,128]{3,2,1,0:T(8,128)(2,1)}, bf16[16,4,32,128]{3,2,1,0:T(8,128)(2,1)S(1)}, u32[]{:S(2)}, u32[]{:S(2)}) collective-permute-start(bf16[16,4,32,128]{3,2,1,0:T(8,128)(2,1)} %get-tuple-element.34), channel_id=1, source_target_pairs={{0,50},{2,48},{16,32},{18,34},{32,16},{34,18},{48,2},{50,0},{1,51}... | collective-permute-start | bytes 1572872 | tf_op jit(solution)/shard_map/ppermute | solution.py:386
  154.7 28.6 %collective-permute-start.9 = (bf16[16,4,32,128]{3,2,1,0:T(8,128)(2,1)S(1)}, bf16[16,4,32,128]{3,2,1,0:T(8,128)(2,1)S(1)}, u32[]{:S(2)}, u32[]{:S(2)}) collective-permute-start(bf16[16,4,32,128]{3,2,1,0:T(8,128)(2,1)S(1)} %get-tuple-element.33.refs_4_.refs_1_), channel_id=1, source_target_pairs={{0,2},{2,0},{16,16},{18,18},{32,32},{34,34},{48,50},{50,48},{1,3},... | collective-permute-start | bytes 1572872 | tf_op jit(solution)/shard_map/ppermute | solution.py:386
  164.5 34.8 %all-to-all-start.3 = ((bf16[16,4,4,32,128]{4,3,2,1,0:T(8,128)(2,1)}), bf16[16,4,4,32,128]{4,3,2,1,0:T(8,128)(2,1)}, u32[]{:S(2)}, u32[]{:S(2)}) async-start(bf16[16,4,4,32,128]{4,3,2,1,0:T(8,128)(2,1)} %join.3), calls=%async_computation.3 | async-start | bytes 4194304 | tf_op jit(solution)/shard_map/all_to_all | solution.py:402
  178.4 15.6 %collective-permute-start.12 = (bf16[16,4,32,128]{3,2,1,0:T(8,128)(2,1)}, bf16[16,4,32,128]{3,2,1,0:T(8,128)(2,1)}, u32[]{:S(2)}, u32[]{:S(2)}) collective-permute-start(bf16[16,4,32,128]{3,2,1,0:T(8,128)(2,1)} %get-tuple-element.36), channel_id=1, source_target_pairs={{0,18},{2,16},{16,0},{18,2},{32,48},{34,50},{48,34},{50,32},{1,19}... | collective-permute-start | bytes 1572872 | tf_op jit(solution)/shard_map/ppermute | solution.py:386
  182.7 15.1 %collective-permute-start.13 = (bf16[16,4,32,128]{3,2,1,0:T(8,128)(2,1)}, bf16[16,4,32,128]{3,2,1,0:T(8,128)(2,1)}, u32[]{:S(2)}, u32[]{:S(2)}) collective-permute-start(bf16[16,4,32,128]{3,2,1,0:T(8,128)(2,1)} %get-tuple-element.37), channel_id=1, source_target_pairs={{0,34},{2,32},{16,48},{18,50},{32,0},{34,2},{48,18},{50,16},{1,35}... | collective-permute-start | bytes 1572872 | tf_op jit(solution)/shard_map/ppermute | solution.py:386
  183.3 0.8 copy-start.1
  183.3 1.0 copy-start.2
  184.3 0.6 copy-start.4
